TPU v7x, 32 devices: a whole 2x2x4 slice. The times are simulated.
32 devices in a mesh: groups: 2 (over y), ctx: 4 (over z), dp: 4 (over x, core).
Axes of the slice: x: 2, y: 2, z: 4, core: 2. Of those that a mesh axis runs over, the one named last changes fastest.
Arguments:
- inputs: bfloat16 [8, 1536, 1024], P(('groups', 'dp'), 'ctx'), parts along dimension 0, may hold values from -6 to 6
- queries: bfloat16 [8, 1536, 1024], P(('groups', 'dp'), 'ctx'), parts along dimension 0, may hold values from -96 to 96
- cotangent: bfloat16 [8, 1536, 1024], P(('groups', 'dp'), 'ctx'), parts along dimension 0, may hold values from -6 to 6
- length_proj: bfloat16 [1536, 2, 256], P('ctx'), may hold values from -0.15625 to 0.15625
- key_value_weight: bfloat16 [1024, 2, 1024], P(None, None, 'ctx'), may hold values from -0.1875 to 0.1875
Outputs:
- query_grad: bfloat16 [8, 1536, 1024], P(('groups', 'dp'), 'ctx'), parts along dimension 0
- input_grad: bfloat16 [8, 1536, 1024], P(('groups', 'dp'), 'ctx'), parts along dimension 0
- length_grad: float32 [3072, 2, 256], P(('groups', 'ctx', 'dp')), parts along dimension 0
- weight_grad: float32 [2048, 2, 1024], P(('groups', 'dp'), None, 'ctx'), parts along dimension 0
There are 2 independent parts, one for each index of `groups`. A program takes and returns all parts, laid end to end along the dimension named above; an argument that names none is the same for every part. Nothing has to cross between parts.
All inputs are finite; a program needn't handle non-finite values.
Results may differ from a plain program's by a relative error of at most 0.018.
The roundings to bfloat16 on the way count: a program that leaves them out, or rounds other values in their place, can miss the bound.
Values may be sent and summed in bfloat16 or wider, within the bound.
No kernel may reach another device: no remote copies, remote signals or barrier semaphores. Data moves between devices by JAX's collectives and lax.ppermute only.
A program may use at most 64 MiB of HBM per device.

v0:
```python
import jax
import jax.numpy as jnp
from jax import lax
from jax.sharding import PartitionSpec as P

HEADS = 16
DH = 64
KP = 256


def local(inputs, queries, cotangent, length_proj, key_value_weight):
    scale = DH ** (-0.5)
    tokens = inputs[0]
    query_row_block = queries[0]
    grad_rows = cotangent[0]
    rows = tokens.shape[0]
    full_width = key_value_weight.shape[0]
    compress = jnp.einsum("lsk,ld->skd", length_proj, tokens, preferred_element_type=jnp.float32)
    length_compressed = lax.psum(compress, "ctx").astype(jnp.bfloat16)
    own_proj = jnp.einsum(
        "skd,dsc->skc", length_compressed, key_value_weight, preferred_element_type=jnp.float32
    ).astype(jnp.bfloat16)
    length_projected = lax.all_gather(own_proj, "ctx", axis=2, tiled=True)
    keys = length_projected[0].reshape(KP, HEADS, DH)
    values = length_projected[1].reshape(KP, HEADS, DH)
    query_heads = query_row_block.reshape(rows, HEADS, DH)
    grad_heads = grad_rows.reshape(rows, HEADS, DH)
    scores = (
        jnp.einsum("lhd,khd->hlk", query_heads, keys, preferred_element_type=jnp.float32) * scale
    )
    probs = jax.nn.softmax(scores, axis=-1)
    probs_low = probs.astype(jnp.bfloat16)
    dprobs = jnp.einsum("lhd,khd->hlk", grad_heads, values, preferred_element_type=jnp.float32)
    delta = jnp.sum(probs * dprobs, axis=-1, keepdims=True)
    dscores = (probs * (dprobs - delta) * scale).astype(jnp.bfloat16)
    query_grad = jnp.einsum(
        "hlk,khd->lhd", dscores, keys, preferred_element_type=jnp.float32
    ).astype(jnp.bfloat16)
    query_grad = query_grad.reshape(1, rows, full_width)
    key_part = jnp.einsum("hlk,lhd->khd", dscores, query_heads, preferred_element_type=jnp.float32)
    value_part = jnp.einsum(
        "hlk,lhd->khd", probs_low, grad_heads, preferred_element_type=jnp.float32
    )
    partial_grad = jnp.stack([key_part.reshape(KP, full_width), value_part.reshape(KP, full_width)])
    own_grad = lax.psum_scatter(partial_grad, "ctx", scatter_dimension=2, tiled=True).astype(
        jnp.bfloat16
    )
    grad_term = jnp.einsum(
        "skc,dsc->skd", own_grad, key_value_weight, preferred_element_type=jnp.float32
    )
    compression_gradient = lax.psum(grad_term, "ctx").astype(jnp.bfloat16)
    input_grad = jnp.einsum(
        "lsk,skd->ld", length_proj, compression_gradient, preferred_element_type=jnp.float32
    ).astype(jnp.bfloat16)
    input_grad = input_grad.reshape(1, rows, full_width)
    length_grad = lax.psum_scatter(
        jnp.einsum("ld,skd->lsk", tokens, compression_gradient, preferred_element_type=jnp.float32),
        "dp",
        scatter_dimension=0,
        tiled=True,
    )
    weight_grad = lax.psum_scatter(
        jnp.einsum("skd,skc->dsc", length_compressed, own_grad, preferred_element_type=jnp.float32),
        "dp",
        scatter_dimension=0,
        tiled=True,
    )
    return (query_grad, input_grad, length_grad, weight_grad)


def solution(mesh):
    in_specs = (
        P(("groups", "dp"), "ctx", None),
        P(("groups", "dp"), "ctx", None),
        P(("groups", "dp"), "ctx", None),
        P("ctx", None, None),
        P(None, None, "ctx"),
    )
    out_specs = (
        P(("groups", "dp"), "ctx", None),
        P(("groups", "dp"), "ctx", None),
        P(("groups", "ctx", "dp"), None, None),
        P(("groups", "dp"), None, "ctx"),
    )
    return jax.shard_map(local, mesh=mesh, in_specs=in_specs, out_specs=out_specs, check_vma=False)
```

profile of v0, /device:TPU:9, one launch (start us, length us, event | category | flops | bytes accessed | tf_op | source)
XLA Modules:
  0.0 348.5 jit_solution(7658990200136108198)
XLA Ops:
  7.2 2.1 fusion.22
  9.3 72.4 %all-reduce.6 = bf16[2,256,1024]{2,1,0:T(8,128)(2,1)} all-reduce(f32[2,256,1024]{2,1,0:T(8,128)S(1)} %fusion.22), channel_id=1, replica_groups=mesh['groups'=2,'ctx'=4,'dp'=4] {'ctx'}, use_global_device_ids=true, to_apply=%region_0.0 | all-reduce | flops 524288 | bytes 3145728 | tf_op jit(solution)/shard_map/psum | solution.py:19
  81.6 2.4 convolution_convert_fusion
  84.1 2.3 copy.49
  86.4 1.5 copy.51
  87.9 27.3 %all-gather.2.cloned.1.call-done = bf16[2,256,1024]{2,1,0:T(8,128)(2,1)} async-done(((bf16[2,256,256]{2,1,0:T(8,128)(2,1)}), bf16[2,256,1024]{2,1,0:T(8,128)(2,1)}) %all-gather.2.cloned.1.call-update) | async-done | bytes 1048592 | tf_op jit(solution)/shard_map/all_gather | solution.py:23
  115.2 1.3 fusion.39
  117.6 3.7 %fusion.41 = f32[16,256,384]{2,1,0:T(8,128)} fusion(bf16[256,16,64]{0,2,1:T(8,128)(2,1)S(1)} %bitcast.84, bf16[384,16,64]{0,2,1:T(8,128)(2,1)S(1)} %bitcast.82), kind=kOutput, calls=%fused_computation.49 | convolution fusion | flops 201326592 | bytes 7602176 | tf_op jit(solution)/shard_map/lhd,khd->hlk/dot_general | solution.py:33
  121.3 5.6 %fusion.40 = (f32[16,384]{1,0:T(8,128)S(1)}, f32[16,384,256]{1,2,0:T(8,128)}) fusion(bf16[256,16,64]{0,2,1:T(8,128)(2,1)} %bitcast.90, bf16[384,16,64]{0,2,1:T(8,128)(2,1)S(1)} %bitcast.88), kind=kOutput, calls=%fused_computation.48 | convolution fusion | flops 206045440 | bytes 7626752 | tf_op jit(solution)/shard_map/sub | solution.py:31
  127.0 3.9 %fusion.10 = f32[16,256,64]{1,2,0:T(8,128)S(1)} fusion(bf16[384,16,64]{0,2,1:T(8,128)(2,1)S(1)} %bitcast.83, f32[16,384,256]{1,2,0:T(8,128)} %get-tuple-element.19, f32[16,384]{1,0:T(8,128)S(1)} %get-tuple-element.18), kind=kOutput, calls=%fused_computation.12 | convolution fusion | flops 204472320 | bytes 8151040 | tf_op jit(solution)/shard_map/hlk,lhd->khd/dot_general | solution.py:41
  130.9 11.4 %fusion.14 = f32[16,256,64]{1,2,0:T(8,128)} fusion(bf16[384,16,64]{0,2,1:T(8,128)(2,1)} %bitcast.87, f32[16,256,384]{2,1,0:T(8,128)} %fusion.41, f32[16,384,256]{1,2,0:T(8,128)} %get-tuple-element.19, f32[16,384]{1,0:T(8,128)S(1)} %get-tuple-element.18), kind=kOutput, calls=%fused_computation.17 | convolution fusion | flops 212343040 | bytes 14442496 | tf_op jit(solution)/shard_map/hlk,lhd->khd/dot_general | solution.py:40
  142.2 2.7 pad_maximum_fusion
  145.0 43.4 %reduce-scatter.3.cloned.1.call-done = f32[2,256,256]{1,2,0:T(8,128)} async-done(((f32[2,256,1024]{1,2,0:T(8,128)}), f32[2,256,256]{1,2,0:T(8,128)}) %reduce-scatter.3.cloned.1.call-update) | async-done | bytes 524304 | tf_op jit(solution)/shard_map/reduce_scatter | solution.py:45
  188.4 1.5 fusion.18
  189.9 73.8 %all-reduce.7 = bf16[2,256,1024]{2,1,0:T(8,128)(2,1)} all-reduce(f32[2,256,1024]{2,1,0:T(8,128)S(1)} %fusion.18), channel_id=1, replica_groups=mesh['groups'=2,'ctx'=4,'dp'=4] {'ctx'}, use_global_device_ids=true, to_apply=%region_5.0 | all-reduce | flops 524288 | bytes 3145728 | tf_op jit(solution)/shard_map/psum | solution.py:51
  263.8 2.2 convolution_bitcast_fusion.1
  266.0 1.2 copy.59
  267.5 3.2 convolution_bitcast_fusion
  272.0 10.3 %fusion.16 = bf16[16,64,384]{2,1,0:T(8,128)(2,1)S(1)} fusion(bf16[256,16,64]{0,2,1:T(8,128)(2,1)S(1)} %bitcast.91, f32[16,256,384]{2,1,0:T(8,128)} %fusion.41, f32[16,384,256]{1,2,0:T(8,128)} %get-tuple-element.19, f32[16,384]{1,0:T(8,128)S(1)} %get-tuple-element.18), kind=kOutput, calls=%fused_computation.22 | convolution fusion | flops 212736256 | bytes 13918208 | tf_op jit(solution)/shard_map/hlk,khd->lhd/dot_general | solution.py:36
  283.4 1.7 fusion.17
  286.3 18.6 %all-reduce.5.cloned.1.call-done = f32[384,2,256]{2,1,0:T(2,128)} async-done(((f32[384,2,256]{2,1,0:T(2,128)}), f32[384,2,256]{2,1,0:T(2,128)}) %all-reduce.5.cloned.1.call-update) | async-done | bytes 786448
  305.0 1.6 constant_dynamic-slice_fusion
  306.6 33.3 %reduce-scatter.5.cloned.1.call-done = f32[256,2,256]{0,2,1:T(8,128)} async-done(((f32[1024,2,256]{0,2,1:T(8,128)}), f32[256,2,256]{0,2,1:T(8,128)}) %reduce-scatter.5.cloned.1.call-update) | async-done | bytes 524304 | tf_op jit(solution)/shard_map/reduce_scatter | solution.py:62
  339.9 2.0 copy.62
  (23 shorter events, 4.6 us)
Async XLA Ops:
  7.2 74.5 %copy-start = (bf16[1024,2,256]{2,1,0:T(2,128)(2,1)S(1)}, bf16[1024,2,256]{2,1,0:T(2,128)(2,1)}, u32[]{:S(2)}) copy-start(bf16[1024,2,256]{2,1,0:T(2,128)(2,1)} %param.9) | copy-start | bytes 3145732
  7.2 108.0 %all-gather.2.cloned.1.call-start = ((), (), s32[]{:S(2)}) async-start(), calls=%async_computation.2 | async-start | bytes 1310720 | tf_op jit(solution)/shard_map/all_gather | solution.py:23
  84.0 104.3 %reduce-scatter.3.cloned.1.call-start = ((), (), s32[]{:S(2)}) async-start(), calls=%async_computation.3 | async-start | bytes 2621440 | tf_op jit(solution)/shard_map/reduce_scatter | solution.py:45
  117.6 3.7 %copy-start.2 = (bf16[1,384,1024]{1,2,0:T(8,128)(2,1)S(1)}, bf16[1,384,1024]{1,2,0:T(8,128)(2,1)}, u32[]{:S(2)}) copy-start(bf16[1,384,1024]{1,2,0:T(8,128)(2,1)} %copy.49) | copy-start | bytes 2359300
  145.0 160.0 %all-reduce.5.cloned.1.call-start = ((), (), s32[]{:S(2)}) async-start(), calls=%async_computation.5 | async-start | bytes 1572864
  189.9 80.8 %copy-start.4 = (u32[32]{0:T(128)S(1)}, u32[32]{0:T(128)}, u32[]{:S(2)}) copy-start(u32[32]{0:T(128)} %constant.12) | copy-start | bytes 388
  263.8 8.2 %copy-start.3 = (bf16[1,256,1024]{1,2,0:T(8,128)(2,1)S(1)}, bf16[1,256,1024]{1,2,0:T(8,128)(2,1)}, u32[]{:S(2)}) copy-start(bf16[1,256,1024]{1,2,0:T(8,128)(2,1)} %copy.48) | copy-start | bytes 1572868
  267.2 72.6 %reduce-scatter.5.cloned.1.call-start = ((), (), s32[]{:S(2)}) async-start(), calls=%async_computation.4 | async-start | bytes 2621440 | tf_op jit(solution)/shard_map/reduce_scatter | solution.py:62
  272.0 11.5 %copy-start.1 = (bf16[2,256,1024]{2,1,0:T(8,128)(2,1)S(1)}, bf16[2,256,1024]{2,1,0:T(8,128)(2,1)}, u32[]{:S(2)}) copy-start(bf16[2,256,1024]{2,1,0:T(8,128)(2,1)} %all-reduce.7) | copy-start | bytes 3145732
Sparse Core Ops, SparseCore 0:
  84.2 30.9 all-gather.1
  145.1 43.2 reduce-scatter.2
  267.4 37.5 all-reduce.4
  307.5 32.3 reduce-scatter.4
where the time goes:
time: 351 us; the launch traced here: 348 us
  blocking collectives  146 us (42%)
  waiting for transfers between devices  123 us (35%)
  matrix products  48 us (14%)
  between operations  14.5 us (4%)
  local copies, waits for them, and re-layouts  14.1 us (4%)
    psum x1, blocking collectives, local(): compression_gradient = lax.psum(grad_term, 'ctx').astype(jnp.bfloat16)  73.8 us
    psum x1, blocking collectives, local(): length_compressed = lax.psum(compress, 'ctx').astype(jnp.bfloat16)  72.4 us
    reduce_scatter x1, waiting for transfers between devices, local(): lax.psum_scatter(partial_grad, 'ctx', scatter_dimension=2, tiled=True)  43.4 us
    reduce_scatter x1, waiting for transfers between devices, local(): lax.psum_scatter(jnp.einsum('skd,skc->dsc', length_compressed, own_grad,...  33.3 us
    all_gather x1, waiting for transfers between devices, local(): length_projected = lax.all_gather(own_proj, 'ctx', axis=2, tiled=True)  27.3 us
    unnamed x5, waiting for transfers between devices  18.7 us
    dot_general x1, matrix products, local(): jnp.einsum('hlk,lhd->khd', dscores, query_heads, preferred_element_type=j...  11.4 us
    unnamed x17, local copies, waits for them, and re-layouts  10.4 us
  transfers between devices with their start and end apart: 4, of which 4 were waited for; matrix products, arithmetic and copies ran while one was open for 7% of the time, Pallas kernels for 0%

commit v1 on v0

--- a/solution.py
+++ b/solution.py
@@ -1,14 +1,245 @@
+import functools
+
 import jax
 import jax.numpy as jnp
 from jax import lax
+from jax.experimental import pallas as pl
+from jax.experimental.pallas import tpu as pltpu
 from jax.sharding import PartitionSpec as P
 
 HEADS = 16
 DH = 64
 KP = 256
-
-
-def local(inputs, queries, cotangent, length_proj, key_value_weight):
+BF = jnp.bfloat16
+F32 = jnp.float32
+VMEM_LIMIT = 40 * 1024 * 1024
+
+
+def dot(a, b, ca, cb):
+    return lax.dot_general(a, b, (((ca,), (cb,)), ((), ())), preferred_element_type=F32)
+
+
+def call(body, outs, args, scratch=(), flops=0, name=None):
+    nbytes = sum(a.size * a.dtype.itemsize for a in args) + sum(o.size * o.dtype.itemsize for o in outs)
+    vmem = pl.BlockSpec(memory_space=pltpu.VMEM)
+    return pl.pallas_call(
+        body,
+        out_shape=outs,
+        in_specs=[pl.BlockSpec(memory_space=pltpu.SMEM)] + [vmem] * (len(args) - 1),
+        out_specs=[vmem] * len(outs),
+        scratch_shapes=list(scratch),
+        compiler_params=pltpu.CompilerParams(vmem_limit_bytes=VMEM_LIMIT),
+        cost_estimate=pl.CostEstimate(flops=flops, bytes_accessed=nbytes, transcendentals=0),
+        name=name,
+    )(*args)
+
+
+def shape(dims, dtype):
+    return jax.ShapeDtypeStruct(dims, dtype)
+
+
+def compress_body(n, plane, rows, idx, e_own, e_core, *rest):
+    blocks, out, e_all = rest[:n], rest[n], rest[n + 1]
+    part = rows // plane
+    for c, e in enumerate((e_own, e_core)):
+        for a in range(plane // 2):
+            piece = idx[2 + a] ^ c
+            for k in range(n):
+                row = pl.multiple_of(k * rows + piece * part, 16)
+                e_all[pl.ds(row, part), :] = e[a, k]
+    total = dot(e_all[0:rows, :], blocks[0][...], 0, 0)
+    for k in range(1, n):
+        total += dot(e_all[k * rows : (k + 1) * rows, :], blocks[k][...], 0, 0)
+    out[...] = total.astype(BF)
+
+
+def project_body(n, own, idx, *rest):
+    parts, w, keys, values = rest[:n], rest[n], rest[n + 1], rest[n + 2]
+    for s, out in enumerate((keys, values)):
+        total = None
+        for k in range(n):
+            row = pl.multiple_of(lax.rem(idx[0] - k + n, n) * own, own)
+            term = dot(parts[k][s * KP : (s + 1) * KP, :], w[pl.ds(row, own), s * own : (s + 1) * own], 1, 0)
+            total = term if total is None else total + term
+        out[...] = total.astype(BF)
+
+
+def attention_body(heads, first, last, idx, keys, values, qg, *rest):
+    if first:
+        query_grad, acc = rest
+    else:
+        before, query_grad, acc = rest
+    q, g, kk, vv = qg[0], qg[1], keys[...], values[...]
+    scale = DH**-0.5
+    lane = lax.broadcasted_iota(jnp.int32, kk.shape, 1)
+    grad_q = key_part = value_part = None
+    for h in range(heads):
+        mask = (lane >= h * DH) & (lane < (h + 1) * DH)
+        k_h = jnp.where(mask, kk, jnp.zeros_like(kk))
+        v_h = jnp.where(mask, vv, jnp.zeros_like(vv))
+        scores = dot(k_h, q, 1, 1)
+        e = jnp.exp((scores - jnp.max(scores, axis=0, keepdims=True)) * scale)
+        p = e * (1.0 / jnp.sum(e, axis=0, keepdims=True))
+        dp = dot(v_h, g, 1, 1)
+        delta = jnp.sum(p * dp, axis=0, keepdims=True)
+        ds = (p * (dp - delta) * scale).astype(BF)
+        term_q = dot(ds, k_h, 0, 0)
+        term_k = jnp.where(mask, dot(ds, q, 1, 0), 0.0)
+        term_v = jnp.where(mask, dot(p.astype(BF), g, 1, 0), 0.0)
+        grad_q = term_q if h == 0 else grad_q + term_q
+        key_part = term_k if h == 0 else key_part + term_k
+        value_part = term_v if h == 0 else value_part + term_v
+    query_grad[...] = grad_q.astype(BF)
+    if not first:
+        key_part = key_part + before[0]
+        value_part = value_part + before[1]
+    acc[0] = key_part.astype(acc.dtype)
+    acc[1] = value_part.astype(acc.dtype)
+
+
+def weight_body(n, own, idx, *rest):
+    parts, grad, out = rest[:n], rest[n], rest[n + 1]
+    for k in range(n):
+        row = pl.multiple_of(lax.rem(idx[0] - k + n, n) * own, own)
+        for s in range(2):
+            out[pl.ds(row, own), s * own : (s + 1) * own] = dot(parts[k][s * KP : (s + 1) * KP, :], grad[s], 0, 0)
+
+
+def tail_body(n, nd, own, idx, *rest):
+    grads, w, e, x, input_grad, length_terms, cg = rest[:n], *rest[n:]
+    width = n * own
+    for s in range(2):
+        total = None
+        for k in range(n):
+            row = pl.multiple_of(lax.rem(idx[0] - k + n, n) * width, width)
+            term = dot(grads[k][s], w[pl.ds(row, width), s * own : (s + 1) * own], 1, 1)
+            total = term if total is None else total + term
+        cg[s * KP : (s + 1) * KP, :] = total.astype(BF)
+    both = cg[...]
+    part = x.shape[0] // nd
+    for a in range(nd):
+        row = pl.multiple_of((idx[1] ^ a) * part, 16)
+        length_terms[a] = dot(x[pl.ds(row, part), :], both, 1, 1)
+    input_grad[...] = dot(e[...], both, 1, 0).astype(BF)
+
+
+def place_body(n, own, idx, *rest):
+    out = rest[n]
+    for k in range(n):
+        col = pl.multiple_of(lax.rem(idx[0] + k, n) * own, own)
+        out[:, pl.ds(col, own)] = rest[k][...]
+
+
+def by_heads(ng, n, nd, inputs, queries, cotangent, length_proj, key_value_weight):
+    tokens, query_rows, grad_rows = inputs[0], queries[0], cotangent[0]
+    rows, width = tokens.shape
+    own = width // n
+    plane = ng * nd
+    g, i, d = lax.axis_index("groups"), lax.axis_index("ctx"), lax.axis_index("dp")
+    m = g * nd + d
+    flips = [(gy, dx) for gy in range(2) for dx in range(2)]
+    idx = jnp.stack([i, d] + [(g ^ gy) * nd + (d ^ (2 * dx)) for gy, dx in flips]).astype(jnp.int32)
+
+    def rot(k):
+        return [(j, (j + k) % n) for j in range(n)]
+
+    def swap(a):
+        return [(j, j ^ a) for j in range(nd)]
+
+    def chunk(x, k):
+        return lax.dynamic_slice_in_dim(x, lax.rem(i + k, n) * own, own, 1)
+
+    def gather(x):
+        return [x] + [lax.ppermute(x, "ctx", rot(k)) for k in range(1, n)]
+
+    part = rows // plane
+    piece = lax.dynamic_slice_in_dim(length_proj, m * part, part, 0).reshape(part, 2 * KP)
+    line = jnp.stack(gather(piece))
+    across = [line]
+    for gy, dx in flips[1:]:
+        perm = [
+            (a * nd + b, (a ^ gy) * nd + (b ^ (2 * dx))) for a in range(ng) for b in range(nd)
+        ]
+        across.append(lax.ppermute(line, ("groups", "dp"), perm))
+    e_own = jnp.stack(across)
+    e_core = lax.ppermute(e_own, "dp", swap(1))
+
+    blocks = [chunk(tokens, 0)]
+    blocks += [lax.ppermute(chunk(tokens, k), "ctx", rot(k)) for k in range(1, n)]
+    compressed = call(
+        functools.partial(compress_body, n, plane, rows),
+        [shape((2 * KP, own), BF)],
+        [idx, e_own, e_core, *blocks],
+        [pltpu.VMEM((n * rows, 2 * KP), BF)],
+        flops=4 * KP * own * n * rows,
+        name="compress",
+    )[0]
+    parts = gather(compressed)
+
+    w = key_value_weight.reshape(width, 2 * own)
+    w_piece = lax.dynamic_slice_in_dim(w, m * (width // plane), width // plane, 0)
+    w_all = lax.all_gather(w_piece, ("ctx", "groups", "dp"), axis=0, tiled=True)
+
+    qg = [jnp.stack([chunk(query_rows, k), chunk(grad_rows, k)]) for k in range(n)]
+    qg = [qg[0]] + [lax.ppermute(qg[k], "ctx", rot(k)) for k in range(1, n)]
+
+    keys, values = call(
+        functools.partial(project_body, n, own),
+        [shape((KP, own), BF)] * 2,
+        [idx, *parts, w],
+        flops=4 * KP * width * own,
+        name="project",
+    )
+    heads = own // DH
+    query_grads, acc = [], None
+    for k in range(n):
+        args = [idx, keys, values, qg[k]] + ([] if k == 0 else [acc])
+        grad, acc = call(
+            functools.partial(attention_body, heads, k == 0, k == n - 1),
+            [shape((rows, own), BF), shape((2, KP, own), BF if k == n - 1 else F32)],
+            args,
+            flops=10 * heads * rows * KP * own,
+            name="attention",
+        )
+        query_grads.append(grad)
+    grads = gather(acc)
+
+    weight = call(
+        functools.partial(weight_body, n, own),
+        [shape((width, 2 * own), F32)],
+        [idx, *parts, acc],
+        flops=4 * KP * own * width,
+        name="weight",
+    )[0]
+    weight_grad = lax.psum_scatter(weight, "dp", scatter_dimension=0, tiled=True)
+    weight_grad = weight_grad.reshape(-1, 2, own)
+
+    returned = [query_grads[0]]
+    returned += [lax.ppermute(query_grads[k], "ctx", rot(n - k)) for k in range(1, n)]
+
+    input_grad, terms = call(
+        functools.partial(tail_body, n, nd, own),
+        [shape((rows, width), BF), shape((nd, rows // nd, 2 * KP), F32)],
+        [idx, *grads, w_all, length_proj.reshape(rows, 2 * KP), tokens],
+        [pltpu.VMEM((2 * KP, width), BF)],
+        flops=4 * KP * width * width + 8 * KP * rows * width,
+        name="tail",
+    )
+    length_grad = terms[0]
+    for a in range(1, nd):
+        length_grad = length_grad + lax.ppermute(terms[a], "dp", swap(a))
+    length_grad = length_grad.reshape(-1, 2, KP)
+
+    query_grad = call(
+        functools.partial(place_body, n, own),
+        [shape((rows, width), BF)],
+        [idx, *returned],
+        name="place",
+    )[0]
+    return query_grad[None], input_grad[None], length_grad, weight_grad
+
+
+def by_positions(inputs, queries, cotangent, length_proj, key_value_weight):
     scale = DH ** (-0.5)
     tokens = inputs[0]
     query_row_block = queries[0]
@@ -69,6 +300,15 @@
 
 
 def solution(mesh):
+    ng, n, nd = (mesh.shape[a] for a in ("groups", "ctx", "dp"))
+
+    def local(*args):
+        rows, width = args[0].shape[1:]
+        fits = ng == 2 and nd == 4 and width % (n * 128) == 0 and HEADS % n == 0 and rows % 128 == 0
+        if fits:
+            return by_heads(ng, n, nd, *args)
+        return by_positions(*args)
+
     in_specs = (
         P(("groups", "dp"), "ctx", None),
         P(("groups", "dp"), "ctx", None),

time: 351 us -> 203 us (0.58)
  blocking collectives: 146 us -> 0 us
  matrix products: 48 us -> 0 us
  starting transfers between devices: 0.34 us -> 28.9 us
  Pallas kernels: 0 us -> 24.3 us
  waiting for transfers between devices: 123 us -> 119 us
    psum x2 -> x0, blocking collectives: 146 us -> none  [the longest x1 73.8 us: local(): compression_gradient = lax.psum(grad_term, 'ctx').astype(jnp.bfloat16)]
    ppermute x0 -> x25, waiting for transfers between devices: none -> 119 us  [the longest x9 83.1 us: gather(): return [x] + [lax.ppermute(x, 'ctx', rot(k)) for k in range(1, n)]]
    reduce_scatter x2 -> x1, waiting for transfers between devices: 76.7 us -> 0.01 us  [by_heads(): lax.psum_scatter(weight, 'dp', scatter_dimension=0, tiled=True)]
    dot_general x10 -> x0, matrix products: 42.3 us -> none  [the longest x1 11.4 us: local(): jnp.einsum('hlk,lhd->khd', dscores, query_heads, preferred_element_type=j...]
    ppermute x0 -> x25, starting transfers between devices: none -> 28.8 us  [the longest x9 12 us: gather(): return [x] + [lax.ppermute(x, 'ctx', rot(k)) for k in range(1, n)]]
    all_gather x1, waiting for transfers between devices: 27.3 us -> 0.01 us  [by_heads(): w_all = lax.all_gather(w_piece, ('ctx', 'groups', 'dp'), axis=0, tiled=True)]
    pallas_call x0 -> x9, Pallas kernels: none -> 24.3 us  [call(): pl.pallas_call(body, out_shape=outs, in_specs=[pl.BlockSpec(memory_space=...]
    unnamed x5 -> x2, waiting for transfers between devices: 18.7 us -> 0.03 us
  transfers between devices with their start and end apart: 4 -> 27, of which waited for: 4 -> 16; matrix products, arithmetic and copies ran while one was open for 7% -> 3% of each run, Pallas kernels for 0% -> 12%
where the time goes in v1:
time: 203 us; the launch traced here: 202 us
  waiting for transfers between devices  119 us (59%)
  starting transfers between devices  28.9 us (14%)
  Pallas kernels  24.3 us (12%)
  between operations  15.7 us (8%)
  local copies, waits for them, and re-layouts  14.1 us (7%)
    ppermute x9, waiting for transfers between devices, gather(): return [x] + [lax.ppermute(x, 'ctx', rot(k)) for k in range(1, n)]  83.1 us
    pallas_call x9, Pallas kernels, call(): pl.pallas_call(body, out_shape=outs, in_specs=[pl.BlockSpec(memory_space=...  24.3 us
    ppermute x3, waiting for transfers between devices, by_heads(): lax.ppermute(chunk(tokens, k), 'ctx', rot(k))  21.3 us
    ppermute x9, starting transfers between devices, gather(): return [x] + [lax.ppermute(x, 'ctx', rot(k)) for k in range(1, n)]  12 us
    ppermute x3, waiting for transfers between devices, by_heads(): across.append(lax.ppermute(line, ('groups', 'dp'), perm))  8.13 us
    unnamed x17, local copies, waits for them, and re-layouts  7.07 us
    ppermute x3, waiting for transfers between devices, by_heads(): length_grad = length_grad + lax.ppermute(terms[a], 'dp', swap(a))  5.44 us
    ppermute x3, starting transfers between devices, by_heads(): lax.ppermute(query_grads[k], 'ctx', rot(n - k))  5.37 us
  transfers between devices with their start and end apart: 27, of which 16 were waited for; matrix products, arithmetic and copies ran while one was open for 3% of the time, Pallas kernels for 12%

profile of v1, /device:TPU:9, one launch (start us, length us, event | category | flops | bytes accessed | tf_op | source)
XLA Modules:
  0.0 202.4 jit_solution(18218445230892651384)
XLA Ops:
  16.4 2.3 %collective-permute-done.2 = bf16[48,512]{1,0:T(8,128)(2,1)S(1)} collective-permute-done((bf16[48,512]{1,0:T(8,128)(2,1)S(1)}, bf16[48,512]{1,0:T(8,128)(2,1)S(1)}, u32[]{:S(2)}, u32[]{:S(2)}) %collective-permute-start.2) | collective-permute-done | bytes 49184 | tf_op jit(solution)/shard_map/ppermute | solution.py:153
  21.4 3.1 %collective-permute-done.3 = bf16[4,48,512]{2,1,0:T(8,128)(2,1)S(1)} collective-permute-done((bf16[4,48,512]{2,1,0:T(8,128)(2,1)S(1)}, bf16[4,48,512]{2,1,0:T(8,128)(2,1)S(1)}, u32[]{:S(2)}, u32[]{:S(2)}) %collective-permute-start.3) | collective-permute-done | bytes 196640 | tf_op jit(solution)/shard_map/ppermute | solution.py:163
  25.3 4.3 %collective-permute-done.5 = bf16[4,48,512]{2,1,0:T(8,128)(2,1)S(1)} collective-permute-done((bf16[4,48,512]{2,1,0:T(8,128)(2,1)S(1)}, bf16[4,48,512]{2,1,0:T(8,128)(2,1)S(1)}, u32[]{:S(2)}, u32[]{:S(2)}) %collective-permute-start.5) | collective-permute-done | bytes 196640 | tf_op jit(solution)/shard_map/ppermute | solution.py:163
  29.7 2.5 %collective-permute-start.6 = (bf16[4,4,48,512]{3,2,1,0:T(8,128)(2,1)S(1)}, bf16[4,4,48,512]{3,2,1,0:T(8,128)(2,1)}, u32[]{:S(2)}, u32[]{:S(2)}) collective-permute-start(bf16[4,4,48,512]{3,2,1,0:T(8,128)(2,1)S(1)} %pad_maximum_fusion.e_own), channel_id=1, source_target_pairs={{0,1},{1,0},{2,3},{3,2},{4,5},{5,4},{6,7},{7,6},{8,9},{9,8},{10,11... | collective-permute-start | bytes 2359304 | tf_op jit(solution)/shard_map/ppermute | solution.py:165
  33.0 2.4 %collective-permute-start.8 = (bf16[384,256]{1,0:T(8,128)(2,1)}, bf16[384,256]{1,0:T(8,128)(2,1)S(1)}, u32[]{:S(2)}, u32[]{:S(2)}) collective-permute-start(bf16[384,256]{1,0:T(8,128)(2,1)} %get-tuple-element.40), channel_id=1, source_target_pairs={{0,8},{4,12},{8,0},{12,4},{1,9},{5,13},{9,1},{13,5},{2,10},{6,14},... | collective-permute-start | bytes 589832 | tf_op jit(solution)/shard_map/ppermute | solution.py:168
  39.7 15.8 %collective-permute-done.8.rest_2_ = bf16[384,256]{1,0:T(8,128)(2,1)S(1)} collective-permute-done((bf16[384,256]{1,0:T(8,128)(2,1)}, bf16[384,256]{1,0:T(8,128)(2,1)S(1)}, u32[]{:S(2)}, u32[]{:S(2)}) %collective-permute-start.8) | collective-permute-done | bytes 196640 | tf_op jit(solution)/shard_map/ppermute | solution.py:168
  55.5 3.9 %collective-permute-done.9.rest_3_ = bf16[384,256]{1,0:T(8,128)(2,1)S(1)} collective-permute-done((bf16[384,256]{1,0:T(8,128)(2,1)}, bf16[384,256]{1,0:T(8,128)(2,1)S(1)}, u32[]{:S(2)}, u32[]{:S(2)}) %collective-permute-start.9) | collective-permute-done | bytes 196640 | tf_op jit(solution)/shard_map/ppermute | solution.py:168
  61.5 3.5 %collective-permute-start.11 = (bf16[512,256]{1,0:T(8,128)(2,1)S(1)}, bf16[512,256]{1,0:T(8,128)(2,1)S(1)}, u32[]{:S(2)}, u32[]{:S(2)}) collective-permute-start(bf16[512,256]{1,0:T(8,128)(2,1)S(1)} %compress.1.rest_0_), channel_id=1, source_target_pairs={{0,8},{4,12},{8,0},{12,4},{1,9},{5,13},{9,1},{13,5},{2,10},{6,14},... | collective-permute-start | bytes 786440 | tf_op jit(solution)/shard_map/ppermute | solution.py:153
  65.6 7.0 %collective-permute-done.10.rest_1_ = bf16[512,256]{1,0:T(8,128)(2,1)S(1)} collective-permute-done((bf16[512,256]{1,0:T(8,128)(2,1)S(1)}, bf16[512,256]{1,0:T(8,128)(2,1)S(1)}, u32[]{:S(2)}, u32[]{:S(2)}) %collective-permute-start.10) | collective-permute-done | bytes 262176 | tf_op jit(solution)/shard_map/ppermute | solution.py:153
  72.6 47.9 %collective-permute-done.11.rest_2_ = bf16[512,256]{1,0:T(8,128)(2,1)S(1)} collective-permute-done((bf16[512,256]{1,0:T(8,128)(2,1)S(1)}, bf16[512,256]{1,0:T(8,128)(2,1)S(1)}, u32[]{:S(2)}, u32[]{:S(2)}) %collective-permute-start.11) | collective-permute-done | bytes 262176 | tf_op jit(solution)/shard_map/ppermute | solution.py:153
  121.5 2.9 %attention.4 = (bf16[384,256]{1,0:T(8,128)(2,1)S(1)}, f32[2,256,256]{2,1,0:T(8,128)S(1)}) custom-call(s32[6]{0:T(128)S(1)} %stack.74.idx, bf16[256,256]{1,0:T(8,128)(2,1)S(1)} %get-tuple-element.16.keys, bf16[256,256]{1,0:T(8,128)(2,1)S(1)} %get-tuple-element.17.values, bf16[2,384,256]{2,1,0:T(8,128)(2,1)S(1)} %pad_maximum_fusion.1.qg), custom_call_target="tpu_custom_call" | custom-call | flops 1006632960 | bytes 1376280 | tf_op jit(solution)/shard_map/attention/pallas_call | solution.py:25
  124.4 3.4 %attention.5 = (bf16[384,256]{1,0:T(8,128)(2,1)}, f32[2,256,256]{2,1,0:T(8,128)S(1)}) custom-call(s32[6]{0:T(128)S(1)} %stack.74.idx, bf16[256,256]{1,0:T(8,128)(2,1)S(1)} %get-tuple-element.16.keys, bf16[256,256]{1,0:T(8,128)(2,1)S(1)} %get-tuple-element.17.values, bf16[2,384,256]{2,1,0:T(8,128)(2,1)S(1)} %collective-permute-done.13.qg, ...), custom_call_target="tpu_custom_call" | custom-call | flops 1006632960 | bytes 1900568 | tf_op jit(solution)/shard_map/attention/pallas_call | solution.py:25
  128.9 3.4 %attention.6 = (bf16[384,256]{1,0:T(8,128)(2,1)}, f32[2,256,256]{2,1,0:T(8,128)S(1)}) custom-call(s32[6]{0:T(128)S(1)} %stack.74.idx, bf16[256,256]{1,0:T(8,128)(2,1)S(1)} %get-tuple-element.16.keys, bf16[256,256]{1,0:T(8,128)(2,1)S(1)} %get-tuple-element.17.values, bf16[2,384,256]{2,1,0:T(8,128)(2,1)S(1)} %collective-permute-done.15.qg, ...), custom_call_target="tpu_custom_call" | custom-call | flops 1006632960 | bytes 1900568 | tf_op jit(solution)/shard_map/attention/pallas_call | solution.py:25
  132.4 3.4 %attention.7 = (bf16[384,256]{1,0:T(8,128)(2,1)}, bf16[2,256,256]{2,1,0:T(8,128)(2,1)S(1)}) custom-call(s32[6]{0:T(128)S(1)} %stack.74.idx, bf16[256,256]{1,0:T(8,128)(2,1)S(1)} %get-tuple-element.16.keys, bf16[256,256]{1,0:T(8,128)(2,1)S(1)} %get-tuple-element.17.values, bf16[2,384,256]{2,1,0:T(8,128)(2,1)S(1)} %collective-permute-done.17.qg, ...), custom_call_target="tpu_custom_call" | custom-call | flops 1006632960 | bytes 1638424 | tf_op jit(solution)/shard_map/attention/pallas_call | solution.py:25
  135.8 2.4 %weight.1 = f32[1024,512]{1,0:T(8,128)} custom-call(s32[6]{0:T(128)S(1)} %stack.74.idx, bf16[512,256]{1,0:T(8,128)(2,1)S(1)} %compress.1.rest_0_, bf16[512,256]{1,0:T(8,128)(2,1)S(1)} %collective-permute-done.10.rest_1_, bf16[512,256]{1,0:T(8,128)(2,1)S(1)} %collective-permute-done.11.rest_2_, bf16[512,256]{1,0:T(8,128)(2,1)S(1)} %collective-permute-done.12.rest_3_, ...), custom_call_target="tpu_custom_call" | custom-call | flops 268435456 | bytes 3407896 | tf_op jit(solution)/shard_map/weight/pallas_call | solution.py:25
  138.3 3.2 %collective-permute-start.20 = (bf16[2,256,256]{2,1,0:T(8,128)(2,1)S(1)}, bf16[2,256,256]{2,1,0:T(8,128)(2,1)S(1)}, u32[]{:S(2)}, u32[]{:S(2)}) collective-permute-start(bf16[2,256,256]{2,1,0:T(8,128)(2,1)S(1)} %get-tuple-element.25.rest_0_.rest_4_), channel_id=1, source_target_pairs={{0,8},{4,12},{8,0},{12,4},{1,9},{5,13},{9,1},{13,5},{2,10},{6,14},... | collective-permute-start | bytes 786440 | tf_op jit(solution)/shard_map/ppermute | solution.py:153
  143.0 2.0 collective-permute-start.16
  145.2 3.2 %collective-permute-start.14 = (bf16[384,256]{1,0:T(8,128)(2,1)}, bf16[384,256]{1,0:T(8,128)(2,1)S(1)}, u32[]{:S(2)}, u32[]{:S(2)}) collective-permute-start(bf16[384,256]{1,0:T(8,128)(2,1)} %get-tuple-element.20), channel_id=1, source_target_pairs={{0,12},{4,0},{8,4},{12,8},{1,13},{5,1},{9,5},{13,9},{2,14},{6,2},{... | collective-permute-start | bytes 589832 | tf_op jit(solution)/shard_map/ppermute | solution.py:218
  148.4 11.8 %collective-permute-done.20.rest_2_ = bf16[2,256,256]{2,1,0:T(8,128)(2,1)S(1)} collective-permute-done((bf16[2,256,256]{2,1,0:T(8,128)(2,1)S(1)}, bf16[2,256,256]{2,1,0:T(8,128)(2,1)S(1)}, u32[]{:S(2)}, u32[]{:S(2)}) %collective-permute-start.20) | collective-permute-done | bytes 262176 | tf_op jit(solution)/shard_map/ppermute | solution.py:153
  160.9 12.6 %collective-permute-done.21.rest_3_ = bf16[2,256,256]{2,1,0:T(8,128)(2,1)S(1)} collective-permute-done((bf16[2,256,256]{2,1,0:T(8,128)(2,1)S(1)}, bf16[2,256,256]{2,1,0:T(8,128)(2,1)S(1)}, u32[]{:S(2)}, u32[]{:S(2)}) %collective-permute-start.21) | collective-permute-done | bytes 262176 | tf_op jit(solution)/shard_map/ppermute | solution.py:153
  174.2 2.2 %copy-done.1 = bf16[4096,512]{1,0:T(8,128)(2,1)S(1)} copy-done((bf16[4096,512]{1,0:T(8,128)(2,1)S(1)}, bf16[4096,512]{1,0:T(8,128)(2,1)}, u32[]{:S(2)}) %copy-start.1) | copy-done | bytes 4194328
  178.3 4.3 %tail.1 = (bf16[384,1024]{1,0:T(8,128)(2,1)}, f32[4,96,512]{2,1,0:T(8,128)S(1)}) custom-call(s32[6]{0:T(128)S(1)} %stack.74.idx, bf16[2,256,256]{2,1,0:T(8,128)(2,1)S(1)} %get-tuple-element.25.rest_0_.rest_4_, bf16[2,256,256]{2,1,0:T(8,128)(2,1)S(1)} %collective-permute-done.19.rest_1_, bf16[2,256,256]{2,1,0:T(8,128)(2,1)S(1)} %copy-done.3, ...), custom_call_target="tpu_custom_call" | custom-call | flops 1879048192 | bytes 7995416 | tf_op jit(solution)/shard_map/tail/pallas_call | solution.py:25
  186.5 2.2 %reshape.47 = f32[256,2,256]{2,1,0:T(2,128)} reshape(f32[256,512]{1,0:T(8,128)} %reduce-scatter.2.cloned.1.call-done) | data formatting | bytes 1048576 | tf_op jit(solution)/shard_map/reshape | solution.py:215
  189.7 4.4 %collective-permute-done.24 = f32[96,512]{1,0:T(8,128)S(1)} collective-permute-done((f32[96,512]{1,0:T(8,128)S(1)}, f32[96,512]{1,0:T(8,128)S(1)}, u32[]{:S(2)}, u32[]{:S(2)}) %collective-permute-start.24) | collective-permute-done | bytes 196640 | tf_op jit(solution)/shard_map/ppermute | solution.py:230
  (74 shorter events, 32.8 us)
Async XLA Ops:
  8.0 166.2 %all-gather.2.cloned.1.call-start = ((), (), s32[]{:S(2)}) async-start(), calls=%async_computation.1 | async-start | bytes 4325376 | tf_op jit(solution)/shard_map/all_gather | solution.py:181
  10.3 176.2 %reduce-scatter.2.cloned.1.call-start = ((), (), s32[]{:S(2)}) async-start(), calls=%async_computation.2 | async-start | bytes 2621440 | tf_op jit(solution)/shard_map/reduce_scatter | solution.py:214
  18.7 5.8 %collective-permute-start.3 = (bf16[4,48,512]{2,1,0:T(8,128)(2,1)S(1)}, bf16[4,48,512]{2,1,0:T(8,128)(2,1)S(1)}, u32[]{:S(2)}, u32[]{:S(2)}) collective-permute-start(bf16[4,48,512]{2,1,0:T(8,128)(2,1)S(1)} %get-tuple-element.44), channel_id=1, source_target_pairs={{0,2},{1,3},{2,0},{3,1},{16,18},{17,19},{18,16},{19,17},{4,6},{5,7... | collective-permute-start | bytes 589832 | tf_op jit(solution)/shard_map/ppermute | solution.py:163
  19.5 5.8 %collective-permute-start.4 = (bf16[4,48,512]{2,1,0:T(8,128)(2,1)S(1)}, bf16[4,48,512]{2,1,0:T(8,128)(2,1)S(1)}, u32[]{:S(2)}, u32[]{:S(2)}) collective-permute-start(bf16[4,48,512]{2,1,0:T(8,128)(2,1)S(1)} %get-tuple-element.44), channel_id=1, source_target_pairs={{0,16},{1,17},{2,18},{3,19},{16,0},{17,1},{18,2},{19,3},{4,20},{5,... | collective-permute-start | bytes 589832 | tf_op jit(solution)/shard_map/ppermute | solution.py:163
  20.7 8.8 %collective-permute-start.5 = (bf16[4,48,512]{2,1,0:T(8,128)(2,1)S(1)}, bf16[4,48,512]{2,1,0:T(8,128)(2,1)S(1)}, u32[]{:S(2)}, u32[]{:S(2)}) collective-permute-start(bf16[4,48,512]{2,1,0:T(8,128)(2,1)S(1)} %get-tuple-element.44), channel_id=1, source_target_pairs={{0,18},{1,19},{2,16},{3,17},{16,2},{17,3},{18,0},{19,1},{4,22},{5,... | collective-permute-start | bytes 589832 | tf_op jit(solution)/shard_map/ppermute | solution.py:163
  29.7 29.7 %collective-permute-start.6 = (bf16[4,4,48,512]{3,2,1,0:T(8,128)(2,1)S(1)}, bf16[4,4,48,512]{3,2,1,0:T(8,128)(2,1)}, u32[]{:S(2)}, u32[]{:S(2)}) collective-permute-start(bf16[4,4,48,512]{3,2,1,0:T(8,128)(2,1)S(1)} %pad_maximum_fusion.e_own), channel_id=1, source_target_pairs={{0,1},{1,0},{2,3},{3,2},{4,5},{5,4},{6,7},{7,6},{8,9},{9,8},{10,11... | collective-permute-start | bytes 2359304 | tf_op jit(solution)/shard_map/ppermute | solution.py:165
  33.0 6.7 %collective-permute-start.7 = (bf16[384,256]{1,0:T(8,128)(2,1)}, bf16[384,256]{1,0:T(8,128)(2,1)S(1)}, u32[]{:S(2)}, u32[]{:S(2)}) collective-permute-start(bf16[384,256]{1,0:T(8,128)(2,1)} %get-tuple-element.41), channel_id=1, source_target_pairs={{0,4},{4,8},{8,12},{12,0},{1,5},{5,9},{9,13},{13,1},{2,6},{6,10},{... | collective-permute-start | bytes 589832 | tf_op jit(solution)/shard_map/ppermute | solution.py:168
  33.0 22.5 %collective-permute-start.8 = (bf16[384,256]{1,0:T(8,128)(2,1)}, bf16[384,256]{1,0:T(8,128)(2,1)S(1)}, u32[]{:S(2)}, u32[]{:S(2)}) collective-permute-start(bf16[384,256]{1,0:T(8,128)(2,1)} %get-tuple-element.40), channel_id=1, source_target_pairs={{0,8},{4,12},{8,0},{12,4},{1,9},{5,13},{9,1},{13,5},{2,10},{6,14},... | collective-permute-start | bytes 589832 | tf_op jit(solution)/shard_map/ppermute | solution.py:168
  35.4 23.9 %collective-permute-start.9 = (bf16[384,256]{1,0:T(8,128)(2,1)}, bf16[384,256]{1,0:T(8,128)(2,1)S(1)}, u32[]{:S(2)}, u32[]{:S(2)}) collective-permute-start(bf16[384,256]{1,0:T(8,128)(2,1)} %get-tuple-element.39), channel_id=1, source_target_pairs={{0,12},{4,0},{8,4},{12,8},{1,13},{5,1},{9,5},{13,9},{2,14},{6,2},{... | collective-permute-start | bytes 589832 | tf_op jit(solution)/shard_map/ppermute | solution.py:168
  61.3 11.2 %collective-permute-start.10 = (bf16[512,256]{1,0:T(8,128)(2,1)S(1)}, bf16[512,256]{1,0:T(8,128)(2,1)S(1)}, u32[]{:S(2)}, u32[]{:S(2)}) collective-permute-start(bf16[512,256]{1,0:T(8,128)(2,1)S(1)} %compress.1.rest_0_), channel_id=1, source_target_pairs={{0,4},{4,8},{8,12},{12,0},{1,5},{5,9},{9,13},{13,1},{2,6},{6,10},{... | collective-permute-start | bytes 786440 | tf_op jit(solution)/shard_map/ppermute | solution.py:153
  61.5 62.9 %collective-permute-start.13 = (bf16[2,384,256]{2,1,0:T(8,128)(2,1)S(1)}, bf16[2,384,256]{2,1,0:T(8,128)(2,1)S(1)}, u32[]{:S(2)}, u32[]{:S(2)}) collective-permute-start(bf16[2,384,256]{2,1,0:T(8,128)(2,1)S(1)} %pad_maximum_fusion.2), channel_id=1, source_target_pairs={{0,4},{4,8},{8,12},{12,0},{1,5},{5,9},{9,13},{13,1},{2,6},{6,10},{... | collective-permute-start | bytes 1179656 | tf_op jit(solution)/shard_map/ppermute | solution.py:184
  61.5 59.0 %collective-permute-start.11 = (bf16[512,256]{1,0:T(8,128)(2,1)S(1)}, bf16[512,256]{1,0:T(8,128)(2,1)S(1)}, u32[]{:S(2)}, u32[]{:S(2)}) collective-permute-start(bf16[512,256]{1,0:T(8,128)(2,1)S(1)} %compress.1.rest_0_), channel_id=1, source_target_pairs={{0,8},{4,12},{8,0},{12,4},{1,9},{5,13},{9,1},{13,5},{2,10},{6,14},... | collective-permute-start | bytes 786440 | tf_op jit(solution)/shard_map/ppermute | solution.py:153
  65.0 55.5 %collective-permute-start.12 = (bf16[512,256]{1,0:T(8,128)(2,1)S(1)}, bf16[512,256]{1,0:T(8,128)(2,1)S(1)}, u32[]{:S(2)}, u32[]{:S(2)}) collective-permute-start(bf16[512,256]{1,0:T(8,128)(2,1)S(1)} %compress.1.rest_0_), channel_id=1, source_target_pairs={{0,12},{4,0},{8,4},{12,8},{1,13},{5,1},{9,5},{13,9},{2,14},{6,2},{... | collective-permute-start | bytes 786440 | tf_op jit(solution)/shard_map/ppermute | solution.py:153
  65.1 63.9 %collective-permute-start.15 = (bf16[2,384,256]{2,1,0:T(8,128)(2,1)S(1)}, bf16[2,384,256]{2,1,0:T(8,128)(2,1)S(1)}, u32[]{:S(2)}, u32[]{:S(2)}) collective-permute-start(bf16[2,384,256]{2,1,0:T(8,128)(2,1)S(1)} %pad_maximum_fusion.3), channel_id=1, source_target_pairs={{0,8},{4,12},{8,0},{12,4},{1,9},{5,13},{9,1},{13,5},{2,10},{6,14},... | collective-permute-start | bytes 1179656 | tf_op jit(solution)/shard_map/ppermute | solution.py:184
  72.6 59.8 %collective-permute-start.17 = (bf16[2,384,256]{2,1,0:T(8,128)(2,1)S(1)}, bf16[2,384,256]{2,1,0:T(8,128)(2,1)S(1)}, u32[]{:S(2)}, u32[]{:S(2)}) collective-permute-start(bf16[2,384,256]{2,1,0:T(8,128)(2,1)S(1)} %pad_maximum_fusion.4), channel_id=1, source_target_pairs={{0,12},{4,0},{8,4},{12,8},{1,13},{5,1},{9,5},{13,9},{2,14},{6,2},{... | collective-permute-start | bytes 1179656 | tf_op jit(solution)/shard_map/ppermute | solution.py:184
  138.2 7.0 %collective-permute-start.19 = (bf16[2,256,256]{2,1,0:T(8,128)(2,1)S(1)}, bf16[2,256,256]{2,1,0:T(8,128)(2,1)S(1)}, u32[]{:S(2)}, u32[]{:S(2)}) collective-permute-start(bf16[2,256,256]{2,1,0:T(8,128)(2,1)S(1)} %get-tuple-element.25.rest_0_.rest_4_), channel_id=1, source_target_pairs={{0,4},{4,8},{8,12},{12,0},{1,5},{5,9},{9,13},{13,1},{2,6},{6,10},{... | collective-permute-start | bytes 786440 | tf_op jit(solution)/shard_map/ppermute | solution.py:153
  138.3 22.0 %collective-permute-start.20 = (bf16[2,256,256]{2,1,0:T(8,128)(2,1)S(1)}, bf16[2,256,256]{2,1,0:T(8,128)(2,1)S(1)}, u32[]{:S(2)}, u32[]{:S(2)}) collective-permute-start(bf16[2,256,256]{2,1,0:T(8,128)(2,1)S(1)} %get-tuple-element.25.rest_0_.rest_4_), channel_id=1, source_target_pairs={{0,8},{4,12},{8,0},{12,4},{1,9},{5,13},{9,1},{13,5},{2,10},{6,14},... | collective-permute-start | bytes 786440 | tf_op jit(solution)/shard_map/ppermute | solution.py:153
  141.4 32.1 %collective-permute-start.21 = (bf16[2,256,256]{2,1,0:T(8,128)(2,1)S(1)}, bf16[2,256,256]{2,1,0:T(8,128)(2,1)S(1)}, u32[]{:S(2)}, u32[]{:S(2)}) collective-permute-start(bf16[2,256,256]{2,1,0:T(8,128)(2,1)S(1)} %get-tuple-element.25.rest_0_.rest_4_), channel_id=1, source_target_pairs={{0,12},{4,0},{8,4},{12,8},{1,13},{5,1},{9,5},{13,9},{2,14},{6,2},{... | collective-permute-start | bytes 786440 | tf_op jit(solution)/shard_map/ppermute | solution.py:153
  142.9 40.7 %collective-permute-start.18 = (bf16[384,256]{1,0:T(8,128)(2,1)}, bf16[384,256]{1,0:T(8,128)(2,1)S(1)}, u32[]{:S(2)}, u32[]{:S(2)}) collective-permute-start(bf16[384,256]{1,0:T(8,128)(2,1)} %get-tuple-element.24), channel_id=1, source_target_pairs={{0,4},{4,8},{8,12},{12,0},{1,5},{5,9},{9,13},{13,1},{2,6},{6,10},{... | collective-permute-start | bytes 589832 | tf_op jit(solution)/shard_map/ppermute | solution.py:218
  143.0 42.0 %collective-permute-start.16 = (bf16[384,256]{1,0:T(8,128)(2,1)}, bf16[384,256]{1,0:T(8,128)(2,1)S(1)}, u32[]{:S(2)}, u32[]{:S(2)}) collective-permute-start(bf16[384,256]{1,0:T(8,128)(2,1)} %get-tuple-element.22), channel_id=1, source_target_pairs={{0,8},{4,12},{8,0},{12,4},{1,9},{5,13},{9,1},{13,5},{2,10},{6,14},... | collective-permute-start | bytes 589832 | tf_op jit(solution)/shard_map/ppermute | solution.py:218
  145.2 39.8 %collective-permute-start.14 = (bf16[384,256]{1,0:T(8,128)(2,1)}, bf16[384,256]{1,0:T(8,128)(2,1)S(1)}, u32[]{:S(2)}, u32[]{:S(2)}) collective-permute-start(bf16[384,256]{1,0:T(8,128)(2,1)} %get-tuple-element.20), channel_id=1, source_target_pairs={{0,12},{4,0},{8,4},{12,8},{1,13},{5,1},{9,5},{13,9},{2,14},{6,2},{... | collective-permute-start | bytes 589832 | tf_op jit(solution)/shard_map/ppermute | solution.py:218
  182.6 6.1 %collective-permute-start.22 = (f32[96,512]{1,0:T(8,128)S(1)}, f32[96,512]{1,0:T(8,128)S(1)}, u32[]{:S(2)}, u32[]{:S(2)}) collective-permute-start(f32[96,512]{1,0:T(8,128)S(1)} %get-tuple-element.28), channel_id=1, source_target_pairs={{0,1},{1,0},{2,3},{3,2},{4,5},{5,4},{6,7},{7,6},{8,9},{9,8},{10,11... | collective-permute-start | bytes 589832 | tf_op jit(solution)/shard_map/ppermute | solution.py:230
  183.3 6.5 %collective-permute-start.23 = (f32[96,512]{1,0:T(8,128)S(1)}, f32[96,512]{1,0:T(8,128)S(1)}, u32[]{:S(2)}, u32[]{:S(2)}) collective-permute-start(f32[96,512]{1,0:T(8,128)S(1)} %get-tuple-element.30), channel_id=1, source_target_pairs={{0,2},{1,3},{2,0},{3,1},{4,6},{5,7},{6,4},{7,5},{8,10},{9,11},{10,... | collective-permute-start | bytes 589832 | tf_op jit(solution)/shard_map/ppermute | solution.py:230
  183.6 10.5 %collective-permute-start.24 = (f32[96,512]{1,0:T(8,128)S(1)}, f32[96,512]{1,0:T(8,128)S(1)}, u32[]{:S(2)}, u32[]{:S(2)}) collective-permute-start(f32[96,512]{1,0:T(8,128)S(1)} %get-tuple-element.29), channel_id=1, source_target_pairs={{0,3},{1,2},{2,1},{3,0},{4,7},{5,6},{6,5},{7,4},{8,11},{9,10},{10,... | collective-permute-start | bytes 589832 | tf_op jit(solution)/shard_map/ppermute | solution.py:230
  (10 other events, 52.9 us)
Sparse Core Ops, SparseCore 0:
  11.7 90.5 all-gather.1
Sparse Core Ops, SparseCore 1:
  138.3 32.4 reduce-scatter.1

commit v2 on v1

--- a/solution.py
+++ b/solution.py
@@ -12,30 +12,79 @@
 KP = 256
 BF = jnp.bfloat16
 F32 = jnp.float32
-VMEM_LIMIT = 40 * 1024 * 1024
+VMEM_LIMIT = 24 * 1024 * 1024
 
 
 def dot(a, b, ca, cb):
     return lax.dot_general(a, b, (((ca,), (cb,)), ((), ())), preferred_element_type=F32)
 
 
-def call(body, outs, args, scratch=(), flops=0, name=None):
-    nbytes = sum(a.size * a.dtype.itemsize for a in args) + sum(o.size * o.dtype.itemsize for o in outs)
+def call(body, outs, args, after=(), scratch=(), name=None):
     vmem = pl.BlockSpec(memory_space=pltpu.VMEM)
+
+    def run(*refs):
+        body(*refs[: len(args)], *refs[len(args) + len(after) :])
+
     return pl.pallas_call(
-        body,
+        run,
         out_shape=outs,
-        in_specs=[pl.BlockSpec(memory_space=pltpu.SMEM)] + [vmem] * (len(args) - 1),
+        in_specs=[pl.BlockSpec(memory_space=pltpu.SMEM)]
+        + [vmem] * (len(args) - 1)
+        + [pl.BlockSpec(memory_space=pl.ANY)] * len(after),
         out_specs=[vmem] * len(outs),
         scratch_shapes=list(scratch),
         compiler_params=pltpu.CompilerParams(vmem_limit_bytes=VMEM_LIMIT),
-        cost_estimate=pl.CostEstimate(flops=flops, bytes_accessed=nbytes, transcendentals=0),
+        cost_estimate=pl.CostEstimate(flops=1, bytes_accessed=1, transcendentals=0),
         name=name,
-    )(*args)
+    )(*args, *after)
+
+
+def gate(arrays, after, name):
+    return pl.pallas_call(
+        lambda *refs: None,
+        out_shape=[shape(a.shape, a.dtype) for a in arrays],
+        in_specs=[pl.BlockSpec(memory_space=pl.ANY)] * (len(arrays) + len(after)),
+        out_specs=[pl.BlockSpec(memory_space=pl.ANY)] * len(arrays),
+        input_output_aliases={k: k for k in range(len(arrays))},
+        cost_estimate=pl.CostEstimate(flops=1, bytes_accessed=1, transcendentals=0),
+        name=name,
+    )(*arrays, *after)
 
 
 def shape(dims, dtype):
     return jax.ShapeDtypeStruct(dims, dtype)
+
+
+def pack_body(n, own, idx, *rest):
+    x, outs = rest[0], rest[1:]
+    for k in range(n):
+        col = pl.multiple_of((idx[0] ^ k) * own, own)
+        outs[k][...] = x[:, pl.ds(col, own)]
+
+
+def pack_pair_body(own, k, idx, q, g, out):
+    col = pl.multiple_of((idx[0] ^ k) * own, own)
+    out[0] = q[:, pl.ds(col, own)]
+    out[1] = g[:, pl.ds(col, own)]
+
+
+def join_ends_body(idx, mine, side, near, far, out):
+    inner = (idx[0] == 1) | (idx[0] == 2)
+    out[0] = mine[...]
+    out[1] = side[...]
+    for a in range(2):
+        out[2 + a] = pick(inner, near[1 - a], far[a])
+
+
+def join_body(idx, *rest):
+    out = rest[-1]
+    for k, x in enumerate(rest[:-1]):
+        out[k] = x[...]
+
+
+def slice_body(idx, x, out):
+    rows = out.shape[0]
+    out[...] = x[pl.ds(pl.multiple_of(idx[2] * rows, rows), rows), :]
 
 
 def compress_body(n, plane, rows, idx, e_own, e_core, *rest):
@@ -53,13 +102,21 @@
     out[...] = total.astype(BF)
 
 
-def project_body(n, own, idx, *rest):
-    parts, w, keys, values = rest[:n], rest[n], rest[n + 1], rest[n + 2]
+def pick(inner, near, far):
+    return jnp.where(inner, near, far)
+
+
+def project_body(own, idx, mine, side, near, far, w, keys, values, whole):
+    inner = (idx[0] == 1) | (idx[0] == 2)
+    whole[0] = mine[...]
+    whole[1] = side[...]
+    for a in range(2):
+        whole[2 + a] = pick(inner, near[1 - a], far[a])
     for s, out in enumerate((keys, values)):
         total = None
-        for k in range(n):
-            row = pl.multiple_of(lax.rem(idx[0] - k + n, n) * own, own)
-            term = dot(parts[k][s * KP : (s + 1) * KP, :], w[pl.ds(row, own), s * own : (s + 1) * own], 1, 0)
+        for k in range(4):
+            row = pl.multiple_of((idx[0] ^ k) * own, own)
+            term = dot(whole[k, s * KP : (s + 1) * KP, :], w[pl.ds(row, own), s * own : (s + 1) * own], 1, 0)
             total = term if total is None else total + term
         out[...] = total.astype(BF)
 
@@ -97,36 +154,41 @@
     acc[1] = value_part.astype(acc.dtype)
 
 
-def weight_body(n, own, idx, *rest):
-    parts, grad, out = rest[:n], rest[n], rest[n + 1]
-    for k in range(n):
-        row = pl.multiple_of(lax.rem(idx[0] - k + n, n) * own, own)
-        for s in range(2):
-            out[pl.ds(row, own), s * own : (s + 1) * own] = dot(parts[k][s * KP : (s + 1) * KP, :], grad[s], 0, 0)
-
-
-def tail_body(n, nd, own, idx, *rest):
-    grads, w, e, x, input_grad, length_terms, cg = rest[:n], *rest[n:]
-    width = n * own
+def weight_body(own, idx, whole, grad, keep, send):
+    for out, core in ((keep, 0), (send, 1)):
+        for a in range(2):
+            k = (idx[1] ^ (core + 2 * a)) ^ idx[0]
+            for s in range(2):
+                out[a, :, s * own : (s + 1) * own] = dot(whole[k, s * KP : (s + 1) * KP, :], grad[s], 0, 0)
+
+
+def arrange_body(own, idx, w_own, w_core, out):
+    part = w_own.shape[2]
+    for c, w in enumerate((w_own, w_core)):
+        for a in range(w.shape[0]):
+            row = pl.multiple_of((idx[2 + a] ^ c) * part, part)
+            for k in range(w.shape[1]):
+                for s in range(2):
+                    out[s, pl.ds(row, part), k * own : (k + 1) * own] = w[a, k, :, s * own : (s + 1) * own]
+
+
+def tail_body(nd, idx, *rest):
+    grads, (w, e, x, input_grad, length_terms, cg) = rest[:4], rest[4:]
     for s in range(2):
-        total = None
-        for k in range(n):
-            row = pl.multiple_of(lax.rem(idx[0] - k + n, n) * width, width)
-            term = dot(grads[k][s], w[pl.ds(row, width), s * own : (s + 1) * own], 1, 1)
-            total = term if total is None else total + term
-        cg[s * KP : (s + 1) * KP, :] = total.astype(BF)
+        grad = jnp.concatenate([part[s] for part in grads], axis=1)
+        cg[s * KP : (s + 1) * KP, :] = dot(grad, w[s], 1, 1).astype(BF)
     both = cg[...]
-    part = x.shape[0] // nd
+    terms = dot(x[...], both, 1, 1)
+    rows = x.shape[0] // nd
     for a in range(nd):
-        row = pl.multiple_of((idx[1] ^ a) * part, 16)
-        length_terms[a] = dot(x[pl.ds(row, part), :], both, 1, 1)
+        length_terms[idx[1] ^ a] = terms[a * rows : (a + 1) * rows, :]
     input_grad[...] = dot(e[...], both, 1, 0).astype(BF)
 
 
 def place_body(n, own, idx, *rest):
     out = rest[n]
     for k in range(n):
-        col = pl.multiple_of(lax.rem(idx[0] + k, n) * own, own)
+        col = pl.multiple_of((idx[0] ^ k) * own, own)
         out[:, pl.ds(col, own)] = rest[k][...]
 
 
@@ -140,100 +202,145 @@
     flips = [(gy, dx) for gy in range(2) for dx in range(2)]
     idx = jnp.stack([i, d] + [(g ^ gy) * nd + (d ^ (2 * dx)) for gy, dx in flips]).astype(jnp.int32)
 
-    def rot(k):
-        return [(j, (j + k) % n) for j in range(n)]
-
-    def swap(a):
-        return [(j, j ^ a) for j in range(nd)]
-
-    def chunk(x, k):
-        return lax.dynamic_slice_in_dim(x, lax.rem(i + k, n) * own, own, 1)
-
-    def gather(x):
-        return [x] + [lax.ppermute(x, "ctx", rot(k)) for k in range(1, n)]
+    def swap(axis_size, a):
+        return [(j, j ^ a) for j in range(axis_size)]
+
+    def to_line(x, k):
+        return lax.ppermute(x, "ctx", swap(n, k))
+
+    def over_line(x):
+        side = to_line(x, 1)
+        near = jnp.stack(
+            [lax.ppermute(x, "ctx", [(1, 2), (2, 1)]), lax.ppermute(x, "ctx", [(0, 2), (3, 1)])]
+        )
+        far = lax.ppermute(near, "ctx", [(1, 0), (2, 3)])
+        return x, side, near, far
+
+    def over_plane(x):
+        across = [x]
+        for gy, dx in flips[1:]:
+            perm = [
+                (a * nd + b, (a ^ gy) * nd + (b ^ (2 * dx))) for a in range(ng) for b in range(nd)
+            ]
+            across.append(lax.ppermute(x, ("groups", "dp"), perm))
+        return across
+
+    def over_cores(x):
+        return lax.ppermute(x, "dp", swap(nd, 1))
+
+    def join_ends(parts, after, name):
+        return call(
+            join_ends_body, [shape((n, *parts[0].shape), BF)], [idx, *parts], after, name=name
+        )[0]
+
+    def pack_queries(k, after):
+        return call(
+            functools.partial(pack_pair_body, own, k),
+            [shape((2, rows, own), BF)],
+            [idx, query_rows, grad_rows],
+            after,
+            name="pack_queries",
+        )[0]
 
     part = rows // plane
     piece = lax.dynamic_slice_in_dim(length_proj, m * part, part, 0).reshape(part, 2 * KP)
-    line = jnp.stack(gather(piece))
-    across = [line]
-    for gy, dx in flips[1:]:
-        perm = [
-            (a * nd + b, (a ^ gy) * nd + (b ^ (2 * dx))) for a in range(ng) for b in range(nd)
-        ]
-        across.append(lax.ppermute(line, ("groups", "dp"), perm))
-    e_own = jnp.stack(across)
-    e_core = lax.ppermute(e_own, "dp", swap(1))
-
-    blocks = [chunk(tokens, 0)]
-    blocks += [lax.ppermute(chunk(tokens, k), "ctx", rot(k)) for k in range(1, n)]
+    blocks = call(
+        functools.partial(pack_body, n, own), [shape((rows, own), BF)] * n, [idx, tokens], name="pack_inputs"
+    )
+    pieces = [piece] + [to_line(piece, k) for k in range(1, n)]
+    blocks = [blocks[0]] + [to_line(blocks[k], k) for k in range(1, n)]
+    line = call(
+        join_body, [shape((n, part, 2 * KP), BF)], [idx, *pieces], [blocks[1]], name="join_pieces"
+    )[0]
+    across = over_plane(line)
+    packed3 = pack_queries(3, [line])
+    e_own = call(
+        join_body, [shape((n, n, part, 2 * KP), BF)], [idx, *across], [*blocks[2:], packed3], name="join_lines"
+    )[0]
+    packed2 = pack_queries(2, [e_own])
+    e_core = over_cores(e_own)
+    w = key_value_weight.reshape(width, 2 * own)
     compressed = call(
         functools.partial(compress_body, n, plane, rows),
         [shape((2 * KP, own), BF)],
         [idx, e_own, e_core, *blocks],
+        [packed2],
         [pltpu.VMEM((n * rows, 2 * KP), BF)],
-        flops=4 * KP * own * n * rows,
         name="compress",
     )[0]
-    parts = gather(compressed)
-
-    w = key_value_weight.reshape(width, 2 * own)
-    w_piece = lax.dynamic_slice_in_dim(w, m * (width // plane), width // plane, 0)
-    w_all = lax.all_gather(w_piece, ("ctx", "groups", "dp"), axis=0, tiled=True)
-
-    qg = [jnp.stack([chunk(query_rows, k), chunk(grad_rows, k)]) for k in range(n)]
-    qg = [qg[0]] + [lax.ppermute(qg[k], "ctx", rot(k)) for k in range(1, n)]
-
-    keys, values = call(
-        functools.partial(project_body, n, own),
-        [shape((KP, own), BF)] * 2,
+    parts = over_line(compressed)
+
+    packed1 = pack_queries(1, [parts[2]])
+    qg = [pack_queries(0, []), to_line(packed1, 1), to_line(packed2, 2), to_line(packed3, 3)]
+    w_piece = call(
+        slice_body, [shape((width // plane, 2 * own), BF)], [idx, w], [parts[1]], name="slice_weight"
+    )[0]
+    w_line = join_ends(over_line(w_piece), [], "join_weight")
+    keys, values, whole = call(
+        functools.partial(project_body, own),
+        [shape((KP, own), BF)] * 2 + [shape((n, 2 * KP, own), BF)],
         [idx, *parts, w],
-        flops=4 * KP * width * own,
+        [qg[2], packed1, w_line],
         name="project",
     )
+
     heads = own // DH
-    query_grads, acc = [], None
-    for k in range(n):
-        args = [idx, keys, values, qg[k]] + ([] if k == 0 else [acc])
-        grad, acc = call(
-            functools.partial(attention_body, heads, k == 0, k == n - 1),
-            [shape((rows, own), BF), shape((2, KP, own), BF if k == n - 1 else F32)],
-            args,
-            flops=10 * heads * rows * KP * own,
+    query_grads, acc = {}, None
+    order = (0, 2, 3, 1)
+    for k in order:
+        first, last = k == order[0], k == order[-1]
+        query_grads[k], acc = call(
+            functools.partial(attention_body, heads, first, last),
+            [shape((rows, own), BF), shape((2, KP, own), BF if last else F32)],
+            [idx, keys, values, qg[k]] + ([] if first else [acc]),
             name="attention",
         )
-        query_grads.append(grad)
-    grads = gather(acc)
-
-    weight = call(
-        functools.partial(weight_body, n, own),
-        [shape((width, 2 * own), F32)],
-        [idx, *parts, acc],
-        flops=4 * KP * own * width,
+    grads = [acc] + [to_line(acc, k) for k in range(1, n)]
+
+    keep, send = call(
+        functools.partial(weight_body, own),
+        [shape((2, width // nd, 2 * own), F32)] * 2,
+        [idx, whole, acc],
         name="weight",
-    )[0]
-    weight_grad = lax.psum_scatter(weight, "dp", scatter_dimension=0, tiled=True)
+    )
+    w_across = over_plane(w_line)
+    w_own = call(
+        join_body, [shape((n, n, width // plane, 2 * own), BF)], [idx, *w_across], [keep, grads[1], grads[2]], name="join_weights"
+    )[0]
+    w_core = over_cores(w_own)
+    w_all = call(
+        functools.partial(arrange_body, own),
+        [shape((2, width, width), BF)],
+        [idx, w_own, w_core],
+        [grads[2]],
+        name="arrange_weight",
+    )[0]
+
+    pair = keep + lax.ppermute(send, "dp", swap(nd, 1))
+    weight_grad = pair[0] + lax.ppermute(pair[1], "dp", swap(nd, 2))
     weight_grad = weight_grad.reshape(-1, 2, own)
 
-    returned = [query_grads[0]]
-    returned += [lax.ppermute(query_grads[k], "ctx", rot(n - k)) for k in range(1, n)]
+    late = gate([query_grads[k] for k in range(1, n)], [grads[2]], "hold_query_grads")
+    returned = [query_grads[0]] + [to_line(late[k - 1], k) for k in range(1, n)]
 
     input_grad, terms = call(
-        functools.partial(tail_body, n, nd, own),
+        functools.partial(tail_body, nd),
         [shape((rows, width), BF), shape((nd, rows // nd, 2 * KP), F32)],
         [idx, *grads, w_all, length_proj.reshape(rows, 2 * KP), tokens],
+        [],
         [pltpu.VMEM((2 * KP, width), BF)],
-        flops=4 * KP * width * width + 8 * KP * rows * width,
         name="tail",
     )
     length_grad = terms[0]
     for a in range(1, nd):
-        length_grad = length_grad + lax.ppermute(terms[a], "dp", swap(a))
+        length_grad = length_grad + lax.ppermute(terms[a], "dp", swap(nd, a))
     length_grad = length_grad.reshape(-1, 2, KP)
 
     query_grad = call(
         functools.partial(place_body, n, own),
         [shape((rows, width), BF)],
         [idx, *returned],
+        [terms],
         name="place",
     )[0]
     return query_grad[None], input_grad[None], length_grad, weight_grad
@@ -304,7 +411,7 @@
 
     def local(*args):
         rows, width = args[0].shape[1:]
-        fits = ng == 2 and nd == 4 and width % (n * 128) == 0 and HEADS % n == 0 and rows % 128 == 0
+        fits = ng == 2 and n == 4 and nd == 4 and width % (n * 128) == 0 and HEADS % n == 0 and rows % 128 == 0
         if fits:
             return by_heads(ng, n, nd, *args)
         return by_positions(*args)

time: 203 us -> 165 us (0.81)
  waiting for transfers between devices: 119 us -> 75.1 us
  starting transfers between devices: 28.9 us -> 50.3 us
  between operations: 15.7 us -> 1.05 us
  local copies, waits for them, and re-layouts: 14.1 us -> 7.31 us
  Pallas kernels: 24.3 us -> 28.7 us
    ppermute x25 -> x36, waiting for transfers between devices: 119 us -> 75.1 us  [the longest x17 54 us: to_line(): return lax.ppermute(x, 'ctx', swap(n, k))]
    ppermute x25 -> x36, starting transfers between devices: 28.8 us -> 50.3 us  [the longest x17 19.4 us: to_line(): return lax.ppermute(x, 'ctx', swap(n, k))]
    pallas_call x9 -> x21, Pallas kernels: 24.3 us -> 28.7 us  [the longest x20 28.7 us: call(): pl.pallas_call(run, out_shape=outs, in_specs=[pl.BlockSpec(memory_space=p...]
    unnamed x17 -> x37, local copies, waits for them, and re-layouts: 7.07 us -> 3.6 us
    dynamic_slice x3 -> x0, local copies, waits for them, and re-layouts: 3.08 us -> none  [the longest x2 2.43 us: chunk(): return lax.dynamic_slice_in_dim(x, lax.rem(i + k, n) * own, own, 1)]
  transfers between devices with their start and end apart: 27 -> 36, of which waited for: 16 -> 16; matrix products, arithmetic and copies ran while one was open for 3% -> 3% of each run, Pallas kernels for 12% -> 15%
where the time goes in v2:
time: 165 us; the launch traced here: 164 us
  waiting for transfers between devices  75.1 us (46%)
  starting transfers between devices  50.3 us (30%)
  Pallas kernels  28.7 us (17%)
  local copies, waits for them, and re-layouts  7.31 us (4%)
    ppermute x17, waiting for transfers between devices, to_line(): return lax.ppermute(x, 'ctx', swap(n, k))  54 us
    pallas_call x20, Pallas kernels, call(): pl.pallas_call(run, out_shape=outs, in_specs=[pl.BlockSpec(memory_space=p...  28.7 us
    ppermute x17, starting transfers between devices, to_line(): return lax.ppermute(x, 'ctx', swap(n, k))  19.4 us
    ppermute x2, starting transfers between devices, over_cores(): return lax.ppermute(x, 'dp', swap(nd, 1))  9.81 us
    ppermute x2, waiting for transfers between devices, over_line(): lax.ppermute(x, 'ctx', [(0, 2), (3, 1)])  8.42 us
    ppermute x2, waiting for transfers between devices, over_line(): lax.ppermute(x, 'ctx', [(1, 2), (2, 1)])  6.31 us
    ppermute x2, starting transfers between devices, over_line(): lax.ppermute(x, 'ctx', [(1, 2), (2, 1)])  5.36 us
    ppermute x1, waiting for transfers between devices, by_heads(): pair = keep + lax.ppermute(send, 'dp', swap(nd, 1))  5.06 us
  transfers between devices with their start and end apart: 36, of which 16 were waited for; matrix products, arithmetic and copies ran while one was open for 3% of the time, Pallas kernels for 15%

profile of v2, /device:TPU:9, one launch (start us, length us, event | category | flops | bytes accessed | tf_op | source)
XLA Modules:
  0.0 163.9 jit_solution(3970449572256062568)
XLA Ops:
  15.2 8.9 %collective-permute-done.7.refs_5_ = bf16[384,256]{1,0:T(8,128)(2,1)S(1)} collective-permute-done((bf16[384,256]{1,0:T(8,128)(2,1)S(1)}, bf16[384,256]{1,0:T(8,128)(2,1)S(1)}, u32[]{:S(2)}, u32[]{:S(2)}) %collective-permute-start.7) | collective-permute-done | bytes 196640 | tf_op jit(solution)/shard_map/ppermute | solution.py:209
  24.1 5.1 %collective-permute-done.8.refs_6_ = bf16[384,256]{1,0:T(8,128)(2,1)S(1)} collective-permute-done((bf16[384,256]{1,0:T(8,128)(2,1)S(1)}, bf16[384,256]{1,0:T(8,128)(2,1)S(1)}, u32[]{:S(2)}, u32[]{:S(2)}) %collective-permute-start.8) | collective-permute-done | bytes 196640 | tf_op jit(solution)/shard_map/ppermute | solution.py:209
  29.9 4.3 %collective-permute-start.9 = (bf16[4,4,48,512]{3,2,1,0:T(8,128)(2,1)S(1)}, bf16[4,4,48,512]{3,2,1,0:T(8,128)(2,1)S(1)}, u32[]{:S(2)}, u32[]{:S(2)}) collective-permute-start(bf16[4,4,48,512]{3,2,1,0:T(8,128)(2,1)S(1)} %join_lines.1.refs_3_.refs_1_), channel_id=1, source_target_pairs={{0,1},{1,0},{2,3},{3,2},{4,5},{5,4},{6,7},{7,6},{8,9},{9,8},{10,11... | collective-permute-start | bytes 2359304 | tf_op jit(solution)/shard_map/ppermute | solution.py:229
  38.8 2.7 %collective-permute-start.11 = (bf16[512,256]{1,0:T(8,128)(2,1)S(1)}, bf16[512,256]{1,0:T(8,128)(2,1)S(1)}, u32[]{:S(2)}, u32[]{:S(2)}) collective-permute-start(bf16[512,256]{1,0:T(8,128)(2,1)S(1)} %compress.1.refs_1_), channel_id=1, source_target_pairs={{4,8},{8,4},{5,9},{9,5},{6,10},{10,6},{7,11},{11,7},{20,24},{24,20... | collective-permute-start | bytes 786440 | tf_op jit(solution)/shard_map/ppermute | solution.py:214
  42.1 5.7 %collective-permute-done.12 = bf16[512,256]{1,0:T(8,128)(2,1)S(1)} collective-permute-done((bf16[512,256]{1,0:T(8,128)(2,1)S(1)}, bf16[512,256]{1,0:T(8,128)(2,1)S(1)}, u32[]{:S(2)}, u32[]{:S(2)}) %collective-permute-start.12) | collective-permute-done | bytes 262176 | tf_op jit(solution)/shard_map/ppermute | solution.py:214
  47.8 6.3 %collective-permute-done.11 = bf16[512,256]{1,0:T(8,128)(2,1)S(1)} collective-permute-done((bf16[512,256]{1,0:T(8,128)(2,1)S(1)}, bf16[512,256]{1,0:T(8,128)(2,1)S(1)}, u32[]{:S(2)}, u32[]{:S(2)}) %collective-permute-start.11) | collective-permute-done | bytes 262176 | tf_op jit(solution)/shard_map/ppermute | solution.py:214
  56.3 2.7 %collective-permute-start.16 = (bf16[128,512]{1,0:T(8,128)(2,1)S(1)}, bf16[128,512]{1,0:T(8,128)(2,1)S(1)}, u32[]{:S(2)}, u32[]{:S(2)}) collective-permute-start(bf16[128,512]{1,0:T(8,128)(2,1)S(1)} %slice_weight.1.refs_1_), channel_id=1, source_target_pairs={{4,8},{8,4},{5,9},{9,5},{6,10},{10,6},{7,11},{11,7},{20,24},{24,20... | collective-permute-start | bytes 393224 | tf_op jit(solution)/shard_map/ppermute | solution.py:214
  60.3 3.0 %collective-permute-start.14 = (bf16[2,384,256]{2,1,0:T(8,128)(2,1)S(1)}, bf16[2,384,256]{2,1,0:T(8,128)(2,1)S(1)}, u32[]{:S(2)}, u32[]{:S(2)}) collective-permute-start(bf16[2,384,256]{2,1,0:T(8,128)(2,1)S(1)} %pack_queries.5.refs_7_), channel_id=1, source_target_pairs={{0,8},{4,12},{8,0},{12,4},{1,9},{5,13},{9,1},{13,5},{2,10},{6,14},... | collective-permute-start | bytes 1179656 | tf_op jit(solution)/shard_map/ppermute | solution.py:209
  63.4 2.7 %collective-permute-done.17 = bf16[128,512]{1,0:T(8,128)(2,1)S(1)} collective-permute-done((bf16[128,512]{1,0:T(8,128)(2,1)S(1)}, bf16[128,512]{1,0:T(8,128)(2,1)S(1)}, u32[]{:S(2)}, u32[]{:S(2)}) %collective-permute-start.17) | collective-permute-done | bytes 131104 | tf_op jit(solution)/shard_map/ppermute | solution.py:214
  69.0 7.9 %collective-permute-done.15.refs_2_ = bf16[128,512]{1,0:T(8,128)(2,1)S(1)} collective-permute-done((bf16[128,512]{1,0:T(8,128)(2,1)S(1)}, bf16[128,512]{1,0:T(8,128)(2,1)S(1)}, u32[]{:S(2)}, u32[]{:S(2)}) %collective-permute-start.15) | collective-permute-done | bytes 131104 | tf_op jit(solution)/shard_map/ppermute | solution.py:209
  77.9 13.1 %collective-permute-done.14.refs_6_.refs_3_ = bf16[2,384,256]{2,1,0:T(8,128)(2,1)S(1)} collective-permute-done((bf16[2,384,256]{2,1,0:T(8,128)(2,1)S(1)}, bf16[2,384,256]{2,1,0:T(8,128)(2,1)S(1)}, u32[]{:S(2)}, u32[]{:S(2)}) %collective-permute-start.14) | collective-permute-done | bytes 393248 | tf_op jit(solution)/shard_map/ppermute | solution.py:209
  94.2 2.9 %attention.4 = (bf16[384,256]{1,0:T(8,128)(2,1)S(1)}, f32[2,256,256]{2,1,0:T(8,128)S(1)}) custom-call(s32[6]{0:T(128)S(1)} %stack.45.refs_0_, bf16[256,256]{1,0:T(8,128)(2,1)S(1)} %get-tuple-element.30.refs_1_, bf16[256,256]{1,0:T(8,128)(2,1)S(1)} %get-tuple-element.31.refs_2_, bf16[2,384,256]{2,1,0:T(8,128)(2,1)S(1)} %pack_queries.7.refs_3_), custom_call_target="tpu_custom_call" | custom-call | flops 1 | bytes 1 | tf_op jit(solution)/shard_map/attention/pallas_call | solution.py:28
  97.8 2.9 %attention.5 = (bf16[384,256]{1,0:T(8,128)(2,1)S(1)}, f32[2,256,256]{2,1,0:T(8,128)S(1)}) custom-call(s32[6]{0:T(128)S(1)} %stack.45.refs_0_, bf16[256,256]{1,0:T(8,128)(2,1)S(1)} %get-tuple-element.30.refs_1_, bf16[256,256]{1,0:T(8,128)(2,1)S(1)} %get-tuple-element.31.refs_2_, bf16[2,384,256]{2,1,0:T(8,128)(2,1)S(1)} %collective-permute-done.14.refs_6_.refs_3_, ...), custom_call_target="tpu_custom_call" | custom-call | flops 1 | bytes 1 | tf_op jit(solution)/shard_map/attention/pallas_call | solution.py:28
  101.0 2.9 %attention.6 = (bf16[384,256]{1,0:T(8,128)(2,1)S(1)}, f32[2,256,256]{2,1,0:T(8,128)S(1)}) custom-call(s32[6]{0:T(128)S(1)} %stack.45.refs_0_, bf16[256,256]{1,0:T(8,128)(2,1)S(1)} %get-tuple-element.30.refs_1_, bf16[256,256]{1,0:T(8,128)(2,1)S(1)} %get-tuple-element.31.refs_2_, bf16[2,384,256]{2,1,0:T(8,128)(2,1)S(1)} %collective-permute-done.20.refs_3_, ...), custom_call_target="tpu_custom_call" | custom-call | flops 1 | bytes 1 | tf_op jit(solution)/shard_map/attention/pallas_call | solution.py:28
  103.9 2.9 %attention.7 = (bf16[384,256]{1,0:T(8,128)(2,1)S(1)}, bf16[2,256,256]{2,1,0:T(8,128)(2,1)S(1)}) custom-call(s32[6]{0:T(128)S(1)} %stack.45.refs_0_, bf16[256,256]{1,0:T(8,128)(2,1)S(1)} %get-tuple-element.30.refs_1_, bf16[256,256]{1,0:T(8,128)(2,1)S(1)} %get-tuple-element.31.refs_2_, bf16[2,384,256]{2,1,0:T(8,128)(2,1)S(1)} %collective-permute-done.19.refs_3_, ...), custom_call_target="tpu_custom_call" | custom-call | flops 1 | bytes 1 | tf_op jit(solution)/shard_map/attention/pallas_call | solution.py:28
  107.5 2.9 %collective-permute-start.21 = (bf16[2,256,256]{2,1,0:T(8,128)(2,1)S(1)}, bf16[2,256,256]{2,1,0:T(8,128)(2,1)S(1)}, u32[]{:S(2)}, u32[]{:S(2)}) collective-permute-start(bf16[2,256,256]{2,1,0:T(8,128)(2,1)S(1)} %get-tuple-element.39.refs_2_.refs_1_), channel_id=1, source_target_pairs={{0,8},{4,12},{8,0},{12,4},{1,9},{5,13},{9,1},{13,5},{2,10},{6,14},... | collective-permute-start | bytes 786440 | tf_op jit(solution)/shard_map/ppermute | solution.py:209
  111.4 4.9 %collective-permute-done.21.refs_3_.refs_7_ = bf16[2,256,256]{2,1,0:T(8,128)(2,1)S(1)} collective-permute-done((bf16[2,256,256]{2,1,0:T(8,128)(2,1)S(1)}, bf16[2,256,256]{2,1,0:T(8,128)(2,1)S(1)}, u32[]{:S(2)}, u32[]{:S(2)}) %collective-permute-start.21) | collective-permute-done | bytes 262176 | tf_op jit(solution)/shard_map/ppermute | solution.py:209
  118.2 5.5 %collective-permute-start.30 = (bf16[4,4,128,512]{3,2,1,0:T(8,128)(2,1)S(1)}, bf16[4,4,128,512]{3,2,1,0:T(8,128)(2,1)}, u32[]{:S(2)}, u32[]{:S(2)}) collective-permute-start(bf16[4,4,128,512]{3,2,1,0:T(8,128)(2,1)S(1)} %join_weights.1.refs_1_), channel_id=1, source_target_pairs={{0,1},{1,0},{2,3},{3,2},{4,5},{5,4},{6,7},{7,6},{8,9},{9,8},{10,11... | collective-permute-start | bytes 6291464 | tf_op jit(solution)/shard_map/ppermute | solution.py:229
  123.8 5.1 %collective-permute-done.34 = f32[2,256,512]{2,1,0:T(8,128)S(1)} collective-permute-done((f32[2,256,512]{2,1,0:T(8,128)S(1)}, f32[2,256,512]{2,1,0:T(8,128)S(1)}, u32[]{:S(2)}, u32[]{:S(2)}) %collective-permute-start.34) | collective-permute-done | bytes 1048608 | tf_op jit(solution)/shard_map/ppermute | solution.py:319
  131.8 2.8 %collective-permute-start.22 = (bf16[384,256]{1,0:T(8,128)(2,1)}, bf16[384,256]{1,0:T(8,128)(2,1)S(1)}, u32[]{:S(2)}, u32[]{:S(2)}) collective-permute-start(bf16[384,256]{1,0:T(8,128)(2,1)} %get-tuple-element.40), channel_id=1, source_target_pairs={{0,4},{4,0},{8,12},{12,8},{1,5},{5,1},{9,13},{13,9},{2,6},{6,2},{1... | collective-permute-start | bytes 589832 | tf_op jit(solution)/shard_map/ppermute | solution.py:209
  138.0 6.2 %collective-permute-done.26.refs_4_ = bf16[2,256,256]{2,1,0:T(8,128)(2,1)S(1)} collective-permute-done((bf16[2,256,256]{2,1,0:T(8,128)(2,1)S(1)}, bf16[2,256,256]{2,1,0:T(8,128)(2,1)S(1)}, u32[]{:S(2)}, u32[]{:S(2)}) %collective-permute-start.26) | collective-permute-done | bytes 262176 | tf_op jit(solution)/shard_map/ppermute | solution.py:209
  144.2 3.5 %tail.1 = (bf16[384,1024]{1,0:T(8,128)(2,1)}, f32[4,96,512]{2,1,0:T(8,128)S(1)}) custom-call(s32[6]{0:T(128)S(1)} %stack.45.refs_0_, bf16[2,256,256]{2,1,0:T(8,128)(2,1)S(1)} %get-tuple-element.39.refs_2_.refs_1_, bf16[2,256,256]{2,1,0:T(8,128)(2,1)S(1)} %collective-permute-done.25.refs_6_.refs_2_, bf16[2,256,256]{2,1,0:T(8,128)(2,1)S(1)} %copy-done.3, ...), custom_call_target="tpu_custom_call" | custom-call | flops 1 | bytes 1 | tf_op jit(solution)/shard_map/tail/pallas_call | solution.py:28
  147.7 2.8 %collective-permute-start.31 = (f32[96,512]{1,0:T(8,128)S(1)}, f32[96,512]{1,0:T(8,128)S(1)}, u32[]{:S(2)}, u32[]{:S(2)}) collective-permute-start(f32[96,512]{1,0:T(8,128)S(1)} %get-tuple-element.48), channel_id=1, source_target_pairs={{0,1},{1,0},{2,3},{3,2},{4,5},{5,4},{6,7},{7,6},{8,9},{9,8},{10,11... | collective-permute-start | bytes 589832 | tf_op jit(solution)/shard_map/ppermute | solution.py:336
  155.3 5.7 %collective-permute-done.24.refs_4_ = bf16[384,256]{1,0:T(8,128)(2,1)} collective-permute-done((bf16[384,256]{1,0:T(8,128)(2,1)}, bf16[384,256]{1,0:T(8,128)(2,1)}, u32[]{:S(2)}, u32[]{:S(2)}) %collective-permute-start.24) | collective-permute-done | bytes 196640 | tf_op jit(solution)/shard_map/ppermute | solution.py:209
  (117 shorter events, 49.4 us)
Async XLA Ops:
  7.4 16.7 %collective-permute-start.7 = (bf16[384,256]{1,0:T(8,128)(2,1)S(1)}, bf16[384,256]{1,0:T(8,128)(2,1)S(1)}, u32[]{:S(2)}, u32[]{:S(2)}) collective-permute-start(bf16[384,256]{1,0:T(8,128)(2,1)S(1)} %get-tuple-element.27), channel_id=1, source_target_pairs={{0,8},{4,12},{8,0},{12,4},{1,9},{5,13},{9,1},{13,5},{2,10},{6,14},... | collective-permute-start | bytes 589832 | tf_op jit(solution)/shard_map/ppermute | solution.py:209
  9.6 19.6 %collective-permute-start.8 = (bf16[384,256]{1,0:T(8,128)(2,1)S(1)}, bf16[384,256]{1,0:T(8,128)(2,1)S(1)}, u32[]{:S(2)}, u32[]{:S(2)}) collective-permute-start(bf16[384,256]{1,0:T(8,128)(2,1)S(1)} %get-tuple-element.28), channel_id=1, source_target_pairs={{0,12},{4,8},{8,4},{12,0},{1,13},{5,9},{9,5},{13,1},{2,14},{6,10},... | collective-permute-start | bytes 589832 | tf_op jit(solution)/shard_map/ppermute | solution.py:209
  11.9 17.4 %collective-permute-start.4 = (bf16[4,48,512]{2,1,0:T(8,128)(2,1)S(1)}, bf16[4,48,512]{2,1,0:T(8,128)(2,1)S(1)}, u32[]{:S(2)}, u32[]{:S(2)}) collective-permute-start(bf16[4,48,512]{2,1,0:T(8,128)(2,1)S(1)} %join_pieces.1.refs_3_.refs_1_), channel_id=1, source_target_pairs={{0,2},{1,3},{2,0},{3,1},{16,18},{17,19},{18,16},{19,17},{4,6},{5,7... | collective-permute-start | bytes 589832 | tf_op jit(solution)/shard_map/ppermute | solution.py:225
  13.1 16.1 %collective-permute-start.5 = (bf16[4,48,512]{2,1,0:T(8,128)(2,1)S(1)}, bf16[4,48,512]{2,1,0:T(8,128)(2,1)S(1)}, u32[]{:S(2)}, u32[]{:S(2)}) collective-permute-start(bf16[4,48,512]{2,1,0:T(8,128)(2,1)S(1)} %join_pieces.1.refs_3_.refs_1_), channel_id=1, source_target_pairs={{0,16},{1,17},{2,18},{3,19},{16,0},{17,1},{18,2},{19,3},{4,20},{5,... | collective-permute-start | bytes 589832 | tf_op jit(solution)/shard_map/ppermute | solution.py:225
  14.4 14.9 %collective-permute-start.6 = (bf16[4,48,512]{2,1,0:T(8,128)(2,1)S(1)}, bf16[4,48,512]{2,1,0:T(8,128)(2,1)S(1)}, u32[]{:S(2)}, u32[]{:S(2)}) collective-permute-start(bf16[4,48,512]{2,1,0:T(8,128)(2,1)S(1)} %join_pieces.1.refs_3_.refs_1_), channel_id=1, source_target_pairs={{0,18},{1,19},{2,16},{3,17},{16,2},{17,3},{18,0},{19,1},{4,22},{5,... | collective-permute-start | bytes 589832 | tf_op jit(solution)/shard_map/ppermute | solution.py:225
  38.8 15.4 %collective-permute-start.11 = (bf16[512,256]{1,0:T(8,128)(2,1)S(1)}, bf16[512,256]{1,0:T(8,128)(2,1)S(1)}, u32[]{:S(2)}, u32[]{:S(2)}) collective-permute-start(bf16[512,256]{1,0:T(8,128)(2,1)S(1)} %compress.1.refs_1_), channel_id=1, source_target_pairs={{4,8},{8,4},{5,9},{9,5},{6,10},{10,6},{7,11},{11,7},{20,24},{24,20... | collective-permute-start | bytes 786440 | tf_op jit(solution)/shard_map/ppermute | solution.py:214
  41.5 14.3 %collective-permute-start.10 = (bf16[512,256]{1,0:T(8,128)(2,1)S(1)}, bf16[512,256]{1,0:T(8,128)(2,1)S(1)}, u32[]{:S(2)}, u32[]{:S(2)}) collective-permute-start(bf16[512,256]{1,0:T(8,128)(2,1)S(1)} %compress.1.refs_1_), channel_id=1, source_target_pairs={{0,4},{4,0},{8,12},{12,8},{1,5},{5,1},{9,13},{13,9},{2,6},{6,2},{1... | collective-permute-start | bytes 786440 | tf_op jit(solution)/shard_map/ppermute | solution.py:209
  54.2 37.8 %collective-permute-start.13 = (bf16[2,512,256]{2,1,0:T(8,128)(2,1)S(1)}, bf16[2,512,256]{2,1,0:T(8,128)(2,1)S(1)}, u32[]{:S(2)}, u32[]{:S(2)}) collective-permute-start(bf16[2,512,256]{2,1,0:T(8,128)(2,1)S(1)} %pad_maximum_fusion.refs_3_), channel_id=1, source_target_pairs={{4,0},{8,12},{5,1},{9,13},{6,2},{10,14},{7,3},{11,15},{20,16},{24,... | collective-permute-start | bytes 1572872 | tf_op jit(solution)/shard_map/ppermute | solution.py:216
  60.3 30.7 %collective-permute-start.14 = (bf16[2,384,256]{2,1,0:T(8,128)(2,1)S(1)}, bf16[2,384,256]{2,1,0:T(8,128)(2,1)S(1)}, u32[]{:S(2)}, u32[]{:S(2)}) collective-permute-start(bf16[2,384,256]{2,1,0:T(8,128)(2,1)S(1)} %pack_queries.5.refs_7_), channel_id=1, source_target_pairs={{0,8},{4,12},{8,0},{12,4},{1,9},{5,13},{9,1},{13,5},{2,10},{6,14},... | collective-permute-start | bytes 1179656 | tf_op jit(solution)/shard_map/ppermute | solution.py:209
  63.4 13.5 %collective-permute-start.15 = (bf16[128,512]{1,0:T(8,128)(2,1)S(1)}, bf16[128,512]{1,0:T(8,128)(2,1)S(1)}, u32[]{:S(2)}, u32[]{:S(2)}) collective-permute-start(bf16[128,512]{1,0:T(8,128)(2,1)S(1)} %slice_weight.1.refs_1_), channel_id=1, source_target_pairs={{0,4},{4,0},{8,12},{12,8},{1,5},{5,1},{9,13},{13,9},{2,6},{6,2},{1... | collective-permute-start | bytes 393224 | tf_op jit(solution)/shard_map/ppermute | solution.py:209
  67.6 33.4 %collective-permute-start.20 = (bf16[2,384,256]{2,1,0:T(8,128)(2,1)S(1)}, bf16[2,384,256]{2,1,0:T(8,128)(2,1)S(1)}, u32[]{:S(2)}, u32[]{:S(2)}) collective-permute-start(bf16[2,384,256]{2,1,0:T(8,128)(2,1)S(1)} %pack_queries.4.refs_7_), channel_id=1, source_target_pairs={{0,12},{4,8},{8,4},{12,0},{1,13},{5,9},{9,5},{13,1},{2,14},{6,10},... | collective-permute-start | bytes 1179656 | tf_op jit(solution)/shard_map/ppermute | solution.py:209
  76.9 27.0 %collective-permute-start.19 = (bf16[2,384,256]{2,1,0:T(8,128)(2,1)S(1)}, bf16[2,384,256]{2,1,0:T(8,128)(2,1)S(1)}, u32[]{:S(2)}, u32[]{:S(2)}) collective-permute-start(bf16[2,384,256]{2,1,0:T(8,128)(2,1)S(1)} %pack_queries.6.refs_7_), channel_id=1, source_target_pairs={{0,4},{4,0},{8,12},{12,8},{1,5},{5,1},{9,13},{13,9},{2,6},{6,2},{1... | collective-permute-start | bytes 1179656 | tf_op jit(solution)/shard_map/ppermute | solution.py:209
  77.5 40.0 %collective-permute-start.27 = (bf16[4,128,512]{2,1,0:T(8,128)(2,1)S(1)}, bf16[4,128,512]{2,1,0:T(8,128)(2,1)S(1)}, u32[]{:S(2)}, u32[]{:S(2)}) collective-permute-start(bf16[4,128,512]{2,1,0:T(8,128)(2,1)S(1)} %join_weight.1.refs_8_.refs_1_), channel_id=1, source_target_pairs={{0,2},{1,3},{2,0},{3,1},{16,18},{17,19},{18,16},{19,17},{4,6},{5,7... | collective-permute-start | bytes 1572872 | tf_op jit(solution)/shard_map/ppermute | solution.py:225
  91.0 26.4 %collective-permute-start.28 = (bf16[4,128,512]{2,1,0:T(8,128)(2,1)S(1)}, bf16[4,128,512]{2,1,0:T(8,128)(2,1)S(1)}, u32[]{:S(2)}, u32[]{:S(2)}) collective-permute-start(bf16[4,128,512]{2,1,0:T(8,128)(2,1)S(1)} %join_weight.1.refs_8_.refs_1_), channel_id=1, source_target_pairs={{0,16},{1,17},{2,18},{3,19},{16,0},{17,1},{18,2},{19,3},{4,20},{5,... | collective-permute-start | bytes 1572872 | tf_op jit(solution)/shard_map/ppermute | solution.py:225
  92.0 25.5 %collective-permute-start.29 = (bf16[4,128,512]{2,1,0:T(8,128)(2,1)S(1)}, bf16[4,128,512]{2,1,0:T(8,128)(2,1)S(1)}, u32[]{:S(2)}, u32[]{:S(2)}) collective-permute-start(bf16[4,128,512]{2,1,0:T(8,128)(2,1)S(1)} %join_weight.1.refs_8_.refs_1_), channel_id=1, source_target_pairs={{0,18},{1,19},{2,16},{3,17},{16,2},{17,3},{18,0},{19,1},{4,22},{5,... | collective-permute-start | bytes 1572872 | tf_op jit(solution)/shard_map/ppermute | solution.py:225
  118.2 16.9 %collective-permute-start.30 = (bf16[4,4,128,512]{3,2,1,0:T(8,128)(2,1)S(1)}, bf16[4,4,128,512]{3,2,1,0:T(8,128)(2,1)}, u32[]{:S(2)}, u32[]{:S(2)}) collective-permute-start(bf16[4,4,128,512]{3,2,1,0:T(8,128)(2,1)S(1)} %join_weights.1.refs_1_), channel_id=1, source_target_pairs={{0,1},{1,0},{2,3},{3,2},{4,5},{5,4},{6,7},{7,6},{8,9},{9,8},{10,11... | collective-permute-start | bytes 6291464 | tf_op jit(solution)/shard_map/ppermute | solution.py:229
  129.9 21.6 %collective-permute-start.35 = (f32[256,512]{1,0:T(8,128)}, f32[256,512]{1,0:T(8,128)}, u32[]{:S(2)}, u32[]{:S(2)}) collective-permute-start(f32[256,512]{1,0:T(8,128)} %slice_bitcast_fusion), channel_id=1, source_target_pairs={{0,2},{1,3},{2,0},{3,1},{4,6},{5,7},{6,4},{7,5},{8,10},{9,11},{10,... | collective-permute-start | bytes 1572872 | tf_op jit(solution)/shard_map/ppermute | solution.py:320
  131.0 13.2 %collective-permute-start.26 = (bf16[2,256,256]{2,1,0:T(8,128)(2,1)S(1)}, bf16[2,256,256]{2,1,0:T(8,128)(2,1)S(1)}, u32[]{:S(2)}, u32[]{:S(2)}) collective-permute-start(bf16[2,256,256]{2,1,0:T(8,128)(2,1)S(1)} %get-tuple-element.39.refs_2_.refs_1_), channel_id=1, source_target_pairs={{0,12},{4,8},{8,4},{12,0},{1,13},{5,9},{9,5},{13,1},{2,14},{6,10},... | collective-permute-start | bytes 786440 | tf_op jit(solution)/shard_map/ppermute | solution.py:209
  131.8 18.7 %collective-permute-start.22 = (bf16[384,256]{1,0:T(8,128)(2,1)}, bf16[384,256]{1,0:T(8,128)(2,1)S(1)}, u32[]{:S(2)}, u32[]{:S(2)}) collective-permute-start(bf16[384,256]{1,0:T(8,128)(2,1)} %get-tuple-element.40), channel_id=1, source_target_pairs={{0,4},{4,0},{8,12},{12,8},{1,5},{5,1},{9,13},{13,9},{2,6},{6,2},{1... | collective-permute-start | bytes 589832 | tf_op jit(solution)/shard_map/ppermute | solution.py:209
  134.6 20.7 %collective-permute-start.23 = (bf16[384,256]{1,0:T(8,128)(2,1)}, bf16[384,256]{1,0:T(8,128)(2,1)}, u32[]{:S(2)}, u32[]{:S(2)}) collective-permute-start(bf16[384,256]{1,0:T(8,128)(2,1)} %get-tuple-element.41), channel_id=1, source_target_pairs={{0,8},{4,12},{8,0},{12,4},{1,9},{5,13},{9,1},{13,5},{2,10},{6,14},... | collective-permute-start | bytes 589832 | tf_op jit(solution)/shard_map/ppermute | solution.py:209
  135.1 25.9 %collective-permute-start.24 = (bf16[384,256]{1,0:T(8,128)(2,1)}, bf16[384,256]{1,0:T(8,128)(2,1)}, u32[]{:S(2)}, u32[]{:S(2)}) collective-permute-start(bf16[384,256]{1,0:T(8,128)(2,1)} %get-tuple-element.42), channel_id=1, source_target_pairs={{0,12},{4,8},{8,4},{12,0},{1,13},{5,9},{9,5},{13,1},{2,14},{6,10},... | collective-permute-start | bytes 589832 | tf_op jit(solution)/shard_map/ppermute | solution.py:209
  147.7 15.3 %collective-permute-start.31 = (f32[96,512]{1,0:T(8,128)S(1)}, f32[96,512]{1,0:T(8,128)S(1)}, u32[]{:S(2)}, u32[]{:S(2)}) collective-permute-start(f32[96,512]{1,0:T(8,128)S(1)} %get-tuple-element.48), channel_id=1, source_target_pairs={{0,1},{1,0},{2,3},{3,2},{4,5},{5,4},{6,7},{7,6},{8,9},{9,8},{10,11... | collective-permute-start | bytes 589832 | tf_op jit(solution)/shard_map/ppermute | solution.py:336
  151.2 11.9 %collective-permute-start.32 = (f32[96,512]{1,0:T(8,128)S(1)}, f32[96,512]{1,0:T(8,128)S(1)}, u32[]{:S(2)}, u32[]{:S(2)}) collective-permute-start(f32[96,512]{1,0:T(8,128)S(1)} %get-tuple-element.50), channel_id=1, source_target_pairs={{0,2},{1,3},{2,0},{3,1},{4,6},{5,7},{6,4},{7,5},{8,10},{9,11},{10,... | collective-permute-start | bytes 589832 | tf_op jit(solution)/shard_map/ppermute | solution.py:336
  151.5 11.5 %collective-permute-start.33 = (f32[96,512]{1,0:T(8,128)S(1)}, f32[96,512]{1,0:T(8,128)S(1)}, u32[]{:S(2)}, u32[]{:S(2)}) collective-permute-start(f32[96,512]{1,0:T(8,128)S(1)} %get-tuple-element.49), channel_id=1, source_target_pairs={{0,3},{1,2},{2,1},{3,0},{4,7},{5,6},{6,5},{7,4},{8,11},{9,10},{10,... | collective-permute-start | bytes 589832 | tf_op jit(solution)/shard_map/ppermute | solution.py:336
  (29 other events, 215.6 us)

commit v3 on v2

--- a/solution.py
+++ b/solution.py
@@ -11,6 +11,7 @@
 DH = 64
 KP = 256
 BF = jnp.bfloat16
+OPT = {'farsplit': 0, 'att': 'blocks', 'wz': 'relay', 'wslice': 'side', 'wreq': 'project', 'preq': 'two', 'jw': 'g12', 'rs': 'direct', 'agp': 'direct', 'late': 'g2', 'p1': 'line', 'p3': 'line2'}
 F32 = jnp.float32
 VMEM_LIMIT = 24 * 1024 * 1024
 
@@ -154,12 +155,62 @@
     acc[1] = value_part.astype(acc.dtype)
 
 
-def weight_body(own, idx, whole, grad, keep, send):
+def halves_body(n, half, idx, keys, values, *rest):
+    pairs, outs, (out, q_all, g_all, p_all, ds_all) = rest[:n], rest[n : 2 * n], rest[2 * n :]
+    rows = pairs[0].shape[1]
+    width = out.shape[2]
+    cols = slice(half * width, (half + 1) * width)
+    kk, vv = keys[:, cols], values[:, cols]
+    for k in range(n):
+        q_all[k * rows : (k + 1) * rows, :] = pairs[k][0, :, cols]
+        g_all[k * rows : (k + 1) * rows, :] = pairs[k][1, :, cols]
+    scale = DH**-0.5
+    lane = lax.broadcasted_iota(jnp.int32, kk.shape, 1)
+    grad_q = [None] * n
+    key_part = value_part = None
+    for h in range(width // DH):
+        mask = (lane >= h * DH) & (lane < (h + 1) * DH)
+        k_h = jnp.where(mask, kk, jnp.zeros_like(kk))
+        v_h = jnp.where(mask, vv, jnp.zeros_like(vv))
+        for k in range(n):
+            block = slice(k * rows, (k + 1) * rows)
+            scores = dot(k_h, q_all[block, :], 1, 1)
+            e = jnp.exp((scores - jnp.max(scores, axis=0, keepdims=True)) * scale)
+            p = e * (1.0 / jnp.sum(e, axis=0, keepdims=True))
+            dp = dot(v_h, g_all[block, :], 1, 1)
+            delta = jnp.sum(p * dp, axis=0, keepdims=True)
+            ds = (p * (dp - delta) * scale).astype(BF)
+            p_all[:, block] = p.astype(BF)
+            ds_all[:, block] = ds
+            term = dot(ds, k_h, 0, 0)
+            grad_q[k] = term if h == 0 else grad_q[k] + term
+        term_k = jnp.where(mask, dot(ds_all[...], q_all[...], 1, 0), 0.0)
+        term_v = jnp.where(mask, dot(p_all[...], g_all[...], 1, 0), 0.0)
+        key_part = term_k if h == 0 else key_part + term_k
+        value_part = term_v if h == 0 else value_part + term_v
+    for k in range(n):
+        outs[k][...] = grad_q[k].astype(BF)
+    out[0] = key_part.astype(BF)
+    out[1] = value_part.astype(BF)
+
+
+def weight_body(own, nacc, idx, whole, *rest):
+    accs, outs = rest[:nacc], rest[nacc:]
+    for a, out in enumerate(outs):
+        k = (idx[1] ^ a) ^ idx[0]
+        for s in range(2):
+            grad = jnp.concatenate([x[s] for x in accs], axis=1) if nacc > 1 else accs[0][s]
+            out[:, s * own : (s + 1) * own] = dot(whole[k, s * KP : (s + 1) * KP, :], grad, 0, 0)
+
+
+def weight_pairs_body(own, nacc, idx, whole, *rest):
+    accs, (keep, send) = rest[:nacc], rest[nacc:]
     for out, core in ((keep, 0), (send, 1)):
         for a in range(2):
             k = (idx[1] ^ (core + 2 * a)) ^ idx[0]
             for s in range(2):
-                out[a, :, s * own : (s + 1) * own] = dot(whole[k, s * KP : (s + 1) * KP, :], grad[s], 0, 0)
+                grad = jnp.concatenate([x[s] for x in accs], axis=1) if nacc > 1 else accs[0][s]
+                out[a, :, s * own : (s + 1) * own] = dot(whole[k, s * KP : (s + 1) * KP, :], grad, 0, 0)
 
 
 def arrange_body(own, idx, w_own, w_core, out):
@@ -173,7 +224,7 @@
 
 
 def tail_body(nd, idx, *rest):
-    grads, (w, e, x, input_grad, length_terms, cg) = rest[:4], rest[4:]
+    grads, (w, e, x, length_terms, input_grad, cg) = rest[:-6], rest[-6:]
     for s in range(2):
         grad = jnp.concatenate([part[s] for part in grads], axis=1)
         cg[s * KP : (s + 1) * KP, :] = dot(grad, w[s], 1, 1).astype(BF)
@@ -186,10 +237,13 @@
 
 
 def place_body(n, own, idx, *rest):
-    out = rest[n]
+    out = rest[-1]
+    parts = (len(rest) - 1) // n
+    width = own // parts
     for k in range(n):
         col = pl.multiple_of((idx[0] ^ k) * own, own)
-        out[:, pl.ds(col, own)] = rest[k][...]
+        for a in range(parts):
+            out[:, pl.ds(col + a * width, width)] = rest[k * parts + a][...]
 
 
 def by_heads(ng, n, nd, inputs, queries, cotangent, length_proj, key_value_weight):
@@ -213,7 +267,10 @@
         near = jnp.stack(
             [lax.ppermute(x, "ctx", [(1, 2), (2, 1)]), lax.ppermute(x, "ctx", [(0, 2), (3, 1)])]
         )
-        far = lax.ppermute(near, "ctx", [(1, 0), (2, 3)])
+        if OPT["farsplit"]:
+            far = jnp.stack([lax.ppermute(near[a], "ctx", [(1, 0), (2, 3)]) for a in range(2)])
+        else:
+            far = lax.ppermute(near, "ctx", [(1, 0), (2, 3)])
         return x, side, near, far
 
     def over_plane(x):
@@ -253,82 +310,176 @@
         join_body, [shape((n, part, 2 * KP), BF)], [idx, *pieces], [blocks[1]], name="join_pieces"
     )[0]
     across = over_plane(line)
-    packed3 = pack_queries(3, [line])
+    o = OPT
+    packed3 = pack_queries(3, [line]) if o["p3"] == "line" else None
+    packed1 = pack_queries(1, [line]) if o["p1"] == "line" else None
+    packed2 = pack_queries(2, [line]) if o["p3"] == "line2" else None
     e_own = call(
-        join_body, [shape((n, n, part, 2 * KP), BF)], [idx, *across], [*blocks[2:], packed3], name="join_lines"
+        join_body,
+        [shape((n, n, part, 2 * KP), BF)],
+        [idx, *across],
+        [*blocks[2:], *[p for p in (packed1, packed2, packed3) if p is not None]],
+        name="join_lines",
     )[0]
-    packed2 = pack_queries(2, [e_own])
+    if packed3 is None:
+        packed3 = pack_queries(3, [e_own])
+    if packed2 is None:
+        packed2 = pack_queries(2, [e_own])
+    if packed1 is None and o["p1"] == "e":
+        packed1 = pack_queries(1, [e_own])
     e_core = over_cores(e_own)
     w = key_value_weight.reshape(width, 2 * own)
+    w_rows = width // plane
+
+    def slice_weight(after):
+        return call(slice_body, [shape((w_rows, 2 * own), BF)], [idx, w], after, name="slice_weight")[0]
+
+    w_piece = slice_weight([e_own]) if o["wslice"] == "e" else None
     compressed = call(
         functools.partial(compress_body, n, plane, rows),
         [shape((2 * KP, own), BF)],
         [idx, e_own, e_core, *blocks],
-        [packed2],
+        [p for p in (packed1, packed2, packed3, w_piece) if p is not None],
         [pltpu.VMEM((n * rows, 2 * KP), BF)],
         name="compress",
     )[0]
     parts = over_line(compressed)
-
-    packed1 = pack_queries(1, [parts[2]])
+    if packed1 is None:
+        packed1 = pack_queries(1, [parts[2]])
     qg = [pack_queries(0, []), to_line(packed1, 1), to_line(packed2, 2), to_line(packed3, 3)]
-    w_piece = call(
-        slice_body, [shape((width // plane, 2 * own), BF)], [idx, w], [parts[1]], name="slice_weight"
-    )[0]
-    w_line = join_ends(over_line(w_piece), [], "join_weight")
+    if w_piece is None:
+        gates = dict(side=parts[1], c=compressed, near=parts[2], far=parts[3], q2=qg[2])
+        w_piece = slice_weight([gates[o["wslice"]]])
+    if o["wz"] == "relay":
+        w_parts = over_line(w_piece)
+
+        def join_weight(after):
+            return join_ends(w_parts, after, "join_weight")
+    else:
+        w_parts = [w_piece] + [to_line(w_piece, k) for k in range(1, n)]
+
+        def join_weight(after):
+            return call(join_body, [shape((n, w_rows, 2 * own), BF)], [idx, *w_parts], after, name="join_weight")[0]
+
+    w_line = join_weight([]) if o["wreq"] != "late" else None
+    req = dict(two=[qg[2], packed1], all=qg[1:], none=[packed1], q12=[qg[1], qg[2]], q23=[qg[2], qg[3]])[o["preq"]]
     keys, values, whole = call(
         functools.partial(project_body, own),
         [shape((KP, own), BF)] * 2 + [shape((n, 2 * KP, own), BF)],
         [idx, *parts, w],
-        [qg[2], packed1, w_line],
+        [*req, *([w_line] if o["wreq"] == "project" else [])],
         name="project",
     )
+    if w_line is None:
+        w_line = join_weight([keys])
 
     heads = own // DH
-    query_grads, acc = {}, None
-    order = (0, 2, 3, 1)
-    for k in order:
-        first, last = k == order[0], k == order[-1]
-        query_grads[k], acc = call(
-            functools.partial(attention_body, heads, first, last),
-            [shape((rows, own), BF), shape((2, KP, own), BF if last else F32)],
-            [idx, keys, values, qg[k]] + ([] if first else [acc]),
+    accs = []
+    if o["att"] == "halves":
+        query_grads = []
+        for half in range(2):
+            *parts_q, acc = call(
+                functools.partial(halves_body, n, half),
+                [shape((rows, own // 2), BF)] * n + [shape((2, KP, own // 2), BF)],
+                [idx, keys, values, *qg],
+                [accs[0]] if half else [],
+                scratch=[pltpu.VMEM((n * rows, own // 2), BF)] * 2 + [pltpu.VMEM((KP, n * rows), BF)] * 2,
+                name="attention",
+            )
+            query_grads.append(parts_q)
+            accs.append(acc)
+    elif o["att"] == "single":
+        *parts_q, acc = call(
+            functools.partial(halves_body, n, 0),
+            [shape((rows, own), BF)] * n + [shape((2, KP, own), BF)],
+            [idx, keys, values, *qg],
+            scratch=[pltpu.VMEM((n * rows, own), BF)] * 2 + [pltpu.VMEM((KP, n * rows), BF)] * 2,
             name="attention",
         )
-    grads = [acc] + [to_line(acc, k) for k in range(1, n)]
-
-    keep, send = call(
-        functools.partial(weight_body, own),
-        [shape((2, width // nd, 2 * own), F32)] * 2,
-        [idx, whole, acc],
-        name="weight",
-    )
+        query_grads = [parts_q]
+        accs.append(acc)
+    else:
+        order, by_block, acc = o.get("order", (0, 2, 3, 1)), {}, None
+        for k in order:
+            first, last = k == order[0], k == order[-1]
+            by_block[k], acc = call(
+                functools.partial(attention_body, heads, first, last),
+                [shape((rows, own), BF), shape((2, KP, own), BF if last else F32)],
+                [idx, keys, values, qg[k]] + ([] if first else [acc]),
+                name="attention",
+            )
+        query_grads = [[by_block[k] for k in range(n)]]
+        accs.append(acc)
+    na = len(accs)
+    grads = []
+    for a, acc in enumerate(accs):
+        if o["agp"] == "relay" or (o["agp"] == "mixed" and a == 0):
+            g_parts = over_line(acc)
+            inner = jnp.logical_or(i == 1, i == 2)
+            grads.append([acc, g_parts[1], jnp.where(inner, g_parts[2][1], g_parts[3][0]), jnp.where(inner, g_parts[2][0], g_parts[3][1])])
+        else:
+            grads.append([acc] + [to_line(acc, k) for k in range(1, n)])
+
+    if o["rs"] == "two":
+        keep, send = call(
+            functools.partial(weight_pairs_body, own, na),
+            [shape((2, width // nd, 2 * own), F32)] * 2,
+            [idx, whole, *accs],
+            name="weight",
+        )
+        pair = keep + lax.ppermute(send, "dp", swap(nd, 1))
+        weight_grad = pair[0] + lax.ppermute(pair[1], "dp", swap(nd, 2))
+    else:
+        weight = call(
+            functools.partial(weight_body, own, na),
+            [shape((width // nd, 2 * own), F32)] * nd,
+            [idx, whole, *accs],
+            [grads[-1][1]] if o["rs"] == "late" else [],
+            name="weight",
+        )
+        keep = weight[0]
+        weight_grad = weight[0]
+        for a in range(1, nd):
+            weight_grad = weight_grad + lax.ppermute(weight[a], "dp", swap(nd, a))
+    weight_grad = weight_grad.reshape(-1, 2, own)
+
+    last = grads[-1]
+    jw = dict(
+        g12=[keep, last[1], last[2]],
+        g1=[keep, last[1]],
+        g0=[keep, *grads[0][1:]],
+        g0l=[keep, *grads[0][1:], last[1], last[2]],
+        gall=[keep, *grads[0][1:], *last[1:]],
+        keys=[keys],
+        acc=[keep],
+    )[o["jw"]]
     w_across = over_plane(w_line)
     w_own = call(
-        join_body, [shape((n, n, width // plane, 2 * own), BF)], [idx, *w_across], [keep, grads[1], grads[2]], name="join_weights"
+        join_body, [shape((n, n, w_rows, 2 * own), BF)], [idx, *w_across], jw, name="join_weights"
     )[0]
     w_core = over_cores(w_own)
     w_all = call(
         functools.partial(arrange_body, own),
         [shape((2, width, width), BF)],
         [idx, w_own, w_core],
-        [grads[2]],
+        [keep, last[1]],
         name="arrange_weight",
     )[0]
 
-    pair = keep + lax.ppermute(send, "dp", swap(nd, 1))
-    weight_grad = pair[0] + lax.ppermute(pair[1], "dp", swap(nd, 2))
-    weight_grad = weight_grad.reshape(-1, 2, own)
-
-    late = gate([query_grads[k] for k in range(1, n)], [grads[2]], "hold_query_grads")
-    returned = [query_grads[0]] + [to_line(late[k - 1], k) for k in range(1, n)]
-
-    input_grad, terms = call(
+    gate_on = dict(g2=[last[2]], g1=[last[1]], g3=[last[3]], none=[])[o["late"]]
+    flat = [x for parts_q in query_grads for x in parts_q[1:]]
+    late = gate(flat, gate_on, "hold_query_grads") if gate_on else flat
+    returned = []
+    for k in range(n):
+        for a in range(na):
+            returned.append(to_line(late[a * (n - 1) + k - 1], k) if k else query_grads[a][0])
+
+    tail_in = [idx, *(grads[a][k] for k in range(n) for a in range(na)), w_all, length_proj.reshape(rows, 2 * KP), tokens]
+    terms, input_grad = call(
         functools.partial(tail_body, nd),
-        [shape((rows, width), BF), shape((nd, rows // nd, 2 * KP), F32)],
-        [idx, *grads, w_all, length_proj.reshape(rows, 2 * KP), tokens],
-        [],
-        [pltpu.VMEM((2 * KP, width), BF)],
+        [shape((nd, rows // nd, 2 * KP), F32), shape((rows, width), BF)],
+        tail_in,
+        scratch=[pltpu.VMEM((2 * KP, width), BF)],
         name="tail",
     )
     length_grad = terms[0]

time: 165 us -> 163 us (0.988)
  starting transfers between devices: 50.3 us -> 47.6 us
  local copies, waits for them, and re-layouts: 7.31 us -> 5.14 us
    ppermute x2 -> x3, waiting for transfers between devices: 5.07 us -> 2.23 us  [by_heads(): weight_grad = weight_grad + lax.ppermute(weight[a], 'dp', swap(nd, a))]
    ppermute x3, starting transfers between devices: 4.41 us -> 2.48 us  [by_heads(): length_grad = length_grad + lax.ppermute(terms[a], 'dp', swap(nd, a))]
    ppermute x2, waiting for transfers between devices: 1.3 us -> 3.06 us  [over_cores(): return lax.ppermute(x, 'dp', swap(nd, 1))]
    ppermute x17, starting transfers between devices: 19.4 us -> 17.7 us  [to_line(): return lax.ppermute(x, 'ctx', swap(n, k))]
    unnamed x37 -> x33, local copies, waits for them, and re-layouts: 3.6 us -> 2.25 us
  transfers between devices with their start and end apart: 36 -> 37, of which waited for: 16 -> 16; matrix products, arithmetic and copies ran while one was open for 3% -> 2% of each run, Pallas kernels for 15% -> 17%
where the time goes in v3:
time: 163 us; the launch traced here: 161 us
  waiting for transfers between devices  73.8 us (45%)
  starting transfers between devices  47.6 us (29%)
  Pallas kernels  30.2 us (19%)
  local copies, waits for them, and re-layouts  5.14 us (3%)
  other arithmetic  2.82 us (2%)
    ppermute x17, waiting for transfers between devices, to_line(): return lax.ppermute(x, 'ctx', swap(n, k))  53.7 us
    pallas_call x20, Pallas kernels, call(): pl.pallas_call(run, out_shape=outs, in_specs=[pl.BlockSpec(memory_space=p...  30.2 us
    ppermute x17, starting transfers between devices, to_line(): return lax.ppermute(x, 'ctx', swap(n, k))  17.7 us
    ppermute x2, starting transfers between devices, over_cores(): return lax.ppermute(x, 'dp', swap(nd, 1))  9.8 us
    ppermute x2, waiting for transfers between devices, over_line(): lax.ppermute(x, 'ctx', [(0, 2), (3, 1)])  8.42 us
    ppermute x2, waiting for transfers between devices, over_line(): lax.ppermute(x, 'ctx', [(1, 2), (2, 1)])  6.31 us
    ppermute x2, starting transfers between devices, over_line(): lax.ppermute(x, 'ctx', [(1, 2), (2, 1)])  5.37 us
    ppermute x6, starting transfers between devices, over_plane(): across.append(lax.ppermute(x, ('groups', 'dp'), perm))  4.68 us
  transfers between devices with their start and end apart: 37, of which 16 were waited for; matrix products, arithmetic and copies ran while one was open for 2% of the time, Pallas kernels for 17%

profile of v3, /device:TPU:9, one launch (start us, length us, event | category | flops | bytes accessed | tf_op | source)
XLA Modules:
  0.0 160.6 jit_solution(16430358722297068464)
XLA Ops:
  5.1 2.3 %collective-permute-start.1 = (bf16[48,512]{1,0:T(8,128)(2,1)S(1)}, bf16[48,512]{1,0:T(8,128)(2,1)S(1)}, u32[]{:S(2)}, u32[]{:S(2)}) collective-permute-start(bf16[48,512]{1,0:T(8,128)(2,1)S(1)} %bitcast.47), channel_id=1, source_target_pairs={{0,8},{4,12},{8,0},{12,4},{1,9},{5,13},{9,1},{13,5},{2,10},{6,14},... | collective-permute-start | bytes 147464 | tf_op jit(solution)/shard_map/ppermute | solution.py:263
  7.4 2.2 %collective-permute-start.7 = (bf16[384,256]{1,0:T(8,128)(2,1)S(1)}, bf16[384,256]{1,0:T(8,128)(2,1)S(1)}, u32[]{:S(2)}, u32[]{:S(2)}) collective-permute-start(bf16[384,256]{1,0:T(8,128)(2,1)S(1)} %get-tuple-element.29), channel_id=1, source_target_pairs={{0,8},{4,12},{8,0},{12,4},{1,9},{5,13},{9,1},{13,5},{2,10},{6,14},... | collective-permute-start | bytes 589832 | tf_op jit(solution)/shard_map/ppermute | solution.py:263
  15.8 8.3 %collective-permute-done.7.refs_5_ = bf16[384,256]{1,0:T(8,128)(2,1)S(1)} collective-permute-done((bf16[384,256]{1,0:T(8,128)(2,1)S(1)}, bf16[384,256]{1,0:T(8,128)(2,1)S(1)}, u32[]{:S(2)}, u32[]{:S(2)}) %collective-permute-start.7) | collective-permute-done | bytes 196640 | tf_op jit(solution)/shard_map/ppermute | solution.py:263
  24.1 5.1 %collective-permute-done.8.refs_6_ = bf16[384,256]{1,0:T(8,128)(2,1)S(1)} collective-permute-done((bf16[384,256]{1,0:T(8,128)(2,1)S(1)}, bf16[384,256]{1,0:T(8,128)(2,1)S(1)}, u32[]{:S(2)}, u32[]{:S(2)}) %collective-permute-start.8) | collective-permute-done | bytes 196640 | tf_op jit(solution)/shard_map/ppermute | solution.py:263
  29.9 4.3 %collective-permute-start.9 = (bf16[4,4,48,512]{3,2,1,0:T(8,128)(2,1)S(1)}, bf16[4,4,48,512]{3,2,1,0:T(8,128)(2,1)S(1)}, u32[]{:S(2)}, u32[]{:S(2)}) collective-permute-start(bf16[4,4,48,512]{3,2,1,0:T(8,128)(2,1)S(1)} %join_lines.1.refs_3_.refs_1_), channel_id=1, source_target_pairs={{0,1},{1,0},{2,3},{3,2},{4,5},{5,4},{6,7},{7,6},{8,9},{9,8},{10,11... | collective-permute-start | bytes 2359304 | tf_op jit(solution)/shard_map/ppermute | solution.py:286
  38.8 2.7 %collective-permute-start.11 = (bf16[512,256]{1,0:T(8,128)(2,1)S(1)}, bf16[512,256]{1,0:T(8,128)(2,1)S(1)}, u32[]{:S(2)}, u32[]{:S(2)}) collective-permute-start(bf16[512,256]{1,0:T(8,128)(2,1)S(1)} %compress.1.refs_1_), channel_id=1, source_target_pairs={{4,8},{8,4},{5,9},{9,5},{6,10},{10,6},{7,11},{11,7},{20,24},{24,20... | collective-permute-start | bytes 786440 | tf_op jit(solution)/shard_map/ppermute | solution.py:268
  42.1 5.7 %collective-permute-done.12 = bf16[512,256]{1,0:T(8,128)(2,1)S(1)} collective-permute-done((bf16[512,256]{1,0:T(8,128)(2,1)S(1)}, bf16[512,256]{1,0:T(8,128)(2,1)S(1)}, u32[]{:S(2)}, u32[]{:S(2)}) %collective-permute-start.12) | collective-permute-done | bytes 262176 | tf_op jit(solution)/shard_map/ppermute | solution.py:268
  47.8 6.3 %collective-permute-done.11 = bf16[512,256]{1,0:T(8,128)(2,1)S(1)} collective-permute-done((bf16[512,256]{1,0:T(8,128)(2,1)S(1)}, bf16[512,256]{1,0:T(8,128)(2,1)S(1)}, u32[]{:S(2)}, u32[]{:S(2)}) %collective-permute-start.11) | collective-permute-done | bytes 262176 | tf_op jit(solution)/shard_map/ppermute | solution.py:268
  56.3 2.7 %collective-permute-start.16 = (bf16[128,512]{1,0:T(8,128)(2,1)S(1)}, bf16[128,512]{1,0:T(8,128)(2,1)S(1)}, u32[]{:S(2)}, u32[]{:S(2)}) collective-permute-start(bf16[128,512]{1,0:T(8,128)(2,1)S(1)} %slice_weight.1.refs_1_), channel_id=1, source_target_pairs={{4,8},{8,4},{5,9},{9,5},{6,10},{10,6},{7,11},{11,7},{20,24},{24,20... | collective-permute-start | bytes 393224 | tf_op jit(solution)/shard_map/ppermute | solution.py:268
  60.3 3.0 %collective-permute-start.14 = (bf16[2,384,256]{2,1,0:T(8,128)(2,1)S(1)}, bf16[2,384,256]{2,1,0:T(8,128)(2,1)S(1)}, u32[]{:S(2)}, u32[]{:S(2)}) collective-permute-start(bf16[2,384,256]{2,1,0:T(8,128)(2,1)S(1)} %pack_queries.5.refs_8_), channel_id=1, source_target_pairs={{0,8},{4,12},{8,0},{12,4},{1,9},{5,13},{9,1},{13,5},{2,10},{6,14},... | collective-permute-start | bytes 1179656 | tf_op jit(solution)/shard_map/ppermute | solution.py:263
  63.4 2.7 %collective-permute-done.17 = bf16[128,512]{1,0:T(8,128)(2,1)S(1)} collective-permute-done((bf16[128,512]{1,0:T(8,128)(2,1)S(1)}, bf16[128,512]{1,0:T(8,128)(2,1)S(1)}, u32[]{:S(2)}, u32[]{:S(2)}) %collective-permute-start.17) | collective-permute-done | bytes 131104 | tf_op jit(solution)/shard_map/ppermute | solution.py:268
  68.4 8.5 %collective-permute-done.15.refs_2_ = bf16[128,512]{1,0:T(8,128)(2,1)S(1)} collective-permute-done((bf16[128,512]{1,0:T(8,128)(2,1)S(1)}, bf16[128,512]{1,0:T(8,128)(2,1)S(1)}, u32[]{:S(2)}, u32[]{:S(2)}) %collective-permute-start.15) | collective-permute-done | bytes 131104 | tf_op jit(solution)/shard_map/ppermute | solution.py:263
  77.9 13.1 %collective-permute-done.14.refs_6_.refs_3_ = bf16[2,384,256]{2,1,0:T(8,128)(2,1)S(1)} collective-permute-done((bf16[2,384,256]{2,1,0:T(8,128)(2,1)S(1)}, bf16[2,384,256]{2,1,0:T(8,128)(2,1)S(1)}, u32[]{:S(2)}, u32[]{:S(2)}) %collective-permute-start.14) | collective-permute-done | bytes 393248 | tf_op jit(solution)/shard_map/ppermute | solution.py:263
  94.2 2.9 %attention.4 = (bf16[384,256]{1,0:T(8,128)(2,1)S(1)}, f32[2,256,256]{2,1,0:T(8,128)S(1)}) custom-call(s32[6]{0:T(128)S(1)} %stack.45.refs_0_, bf16[256,256]{1,0:T(8,128)(2,1)S(1)} %get-tuple-element.32.refs_1_, bf16[256,256]{1,0:T(8,128)(2,1)S(1)} %get-tuple-element.33.refs_2_, bf16[2,384,256]{2,1,0:T(8,128)(2,1)S(1)} %pack_queries.7.refs_3_), custom_call_target="tpu_custom_call" | custom-call | flops 1 | bytes 1 | tf_op jit(solution)/shard_map/attention/pallas_call | solution.py:29
  97.1 3.5 %attention.5 = (bf16[384,256]{1,0:T(8,128)(2,1)}, f32[2,256,256]{2,1,0:T(8,128)S(1)}) custom-call(s32[6]{0:T(128)S(1)} %stack.45.refs_0_, bf16[256,256]{1,0:T(8,128)(2,1)S(1)} %get-tuple-element.32.refs_1_, bf16[256,256]{1,0:T(8,128)(2,1)S(1)} %get-tuple-element.33.refs_2_, bf16[2,384,256]{2,1,0:T(8,128)(2,1)S(1)} %collective-permute-done.14.refs_6_.refs_3_, ...), custom_call_target="tpu_custom_call" | custom-call | flops 1 | bytes 1 | tf_op jit(solution)/shard_map/attention/pallas_call | solution.py:29
  101.0 2.9 %attention.6 = (bf16[384,256]{1,0:T(8,128)(2,1)S(1)}, f32[2,256,256]{2,1,0:T(8,128)S(1)}) custom-call(s32[6]{0:T(128)S(1)} %stack.45.refs_0_, bf16[256,256]{1,0:T(8,128)(2,1)S(1)} %get-tuple-element.32.refs_1_, bf16[256,256]{1,0:T(8,128)(2,1)S(1)} %get-tuple-element.33.refs_2_, bf16[2,384,256]{2,1,0:T(8,128)(2,1)S(1)} %collective-permute-done.20.refs_3_, ...), custom_call_target="tpu_custom_call" | custom-call | flops 1 | bytes 1 | tf_op jit(solution)/shard_map/attention/pallas_call | solution.py:29
  103.9 2.9 %attention.7 = (bf16[384,256]{1,0:T(8,128)(2,1)S(1)}, bf16[2,256,256]{2,1,0:T(8,128)(2,1)S(1)}) custom-call(s32[6]{0:T(128)S(1)} %stack.45.refs_0_, bf16[256,256]{1,0:T(8,128)(2,1)S(1)} %get-tuple-element.32.refs_1_, bf16[256,256]{1,0:T(8,128)(2,1)S(1)} %get-tuple-element.33.refs_2_, bf16[2,384,256]{2,1,0:T(8,128)(2,1)S(1)} %collective-permute-done.19.refs_3_, ...), custom_call_target="tpu_custom_call" | custom-call | flops 1 | bytes 1 | tf_op jit(solution)/shard_map/attention/pallas_call | solution.py:29
  106.9 2.8 %collective-permute-start.21 = (bf16[2,256,256]{2,1,0:T(8,128)(2,1)S(1)}, bf16[2,256,256]{2,1,0:T(8,128)(2,1)S(1)}, u32[]{:S(2)}, u32[]{:S(2)}) collective-permute-start(bf16[2,256,256]{2,1,0:T(8,128)(2,1)S(1)} %get-tuple-element.41.refs_2_.refs_1_), channel_id=1, source_target_pairs={{0,8},{4,12},{8,0},{12,4},{1,9},{5,13},{9,1},{13,5},{2,10},{6,14},... | collective-permute-start | bytes 786440 | tf_op jit(solution)/shard_map/ppermute | solution.py:263
  111.7 3.9 %collective-permute-done.21.refs_3_.refs_7_ = bf16[2,256,256]{2,1,0:T(8,128)(2,1)S(1)} collective-permute-done((bf16[2,256,256]{2,1,0:T(8,128)(2,1)S(1)}, bf16[2,256,256]{2,1,0:T(8,128)(2,1)S(1)}, u32[]{:S(2)}, u32[]{:S(2)}) %collective-permute-start.21) | collective-permute-done | bytes 262176 | tf_op jit(solution)/shard_map/ppermute | solution.py:263
  117.5 5.5 %collective-permute-start.30 = (bf16[4,4,128,512]{3,2,1,0:T(8,128)(2,1)S(1)}, bf16[4,4,128,512]{3,2,1,0:T(8,128)(2,1)}, u32[]{:S(2)}, u32[]{:S(2)}) collective-permute-start(bf16[4,4,128,512]{3,2,1,0:T(8,128)(2,1)S(1)} %join_weights.1.refs_1_), channel_id=1, source_target_pairs={{0,1},{1,0},{2,3},{3,2},{4,5},{5,4},{6,7},{7,6},{8,9},{9,8},{10,11... | collective-permute-start | bytes 6291464 | tf_op jit(solution)/shard_map/ppermute | solution.py:286
  131.6 7.3 %collective-permute-done.26.refs_4_ = bf16[2,256,256]{2,1,0:T(8,128)(2,1)} collective-permute-done((bf16[2,256,256]{2,1,0:T(8,128)(2,1)S(1)}, bf16[2,256,256]{2,1,0:T(8,128)(2,1)}, u32[]{:S(2)}, u32[]{:S(2)}) %collective-permute-start.26) | collective-permute-done | bytes 262176 | tf_op jit(solution)/shard_map/ppermute | solution.py:263
  138.9 4.0 %tail.1 = (f32[4,96,512]{2,1,0:T(8,128)S(1)}, bf16[384,1024]{1,0:T(8,128)(2,1)}) custom-call(s32[6]{0:T(128)S(1)} %stack.45.refs_0_, bf16[2,256,256]{2,1,0:T(8,128)(2,1)S(1)} %get-tuple-element.41.refs_2_.refs_1_, bf16[2,256,256]{2,1,0:T(8,128)(2,1)S(1)} %collective-permute-done.25.refs_6_.refs_4_.refs_2_, bf16[2,256,256]{2,1,0:T(8,128)(2,1)S(1)} %copy-done.5, ...), custom_call_target="tpu_custom_call" | custom-call | flops 1 | bytes 1 | tf_op jit(solution)/shard_map/tail/pallas_call | solution.py:29
  146.4 2.2 %collective-permute-done.36 = f32[256,512]{1,0:T(8,128)} collective-permute-done((f32[256,512]{1,0:T(8,128)}, f32[256,512]{1,0:T(8,128)}, u32[]{:S(2)}, u32[]{:S(2)}) %collective-permute-start.36) | collective-permute-done | bytes 524320 | tf_op jit(solution)/shard_map/ppermute | solution.py:443
  151.8 5.3 %collective-permute-done.24.refs_4_ = bf16[384,256]{1,0:T(8,128)(2,1)S(1)} collective-permute-done((bf16[384,256]{1,0:T(8,128)(2,1)S(1)}, bf16[384,256]{1,0:T(8,128)(2,1)S(1)}, u32[]{:S(2)}, u32[]{:S(2)}) %collective-permute-start.24) | collective-permute-done | bytes 196640 | tf_op jit(solution)/shard_map/ppermute | solution.py:263
  (113 shorter events, 49.2 us)
Async XLA Ops:
  7.4 16.7 %collective-permute-start.7 = (bf16[384,256]{1,0:T(8,128)(2,1)S(1)}, bf16[384,256]{1,0:T(8,128)(2,1)S(1)}, u32[]{:S(2)}, u32[]{:S(2)}) collective-permute-start(bf16[384,256]{1,0:T(8,128)(2,1)S(1)} %get-tuple-element.29), channel_id=1, source_target_pairs={{0,8},{4,12},{8,0},{12,4},{1,9},{5,13},{9,1},{13,5},{2,10},{6,14},... | collective-permute-start | bytes 589832 | tf_op jit(solution)/shard_map/ppermute | solution.py:263
  9.6 19.6 %collective-permute-start.8 = (bf16[384,256]{1,0:T(8,128)(2,1)S(1)}, bf16[384,256]{1,0:T(8,128)(2,1)S(1)}, u32[]{:S(2)}, u32[]{:S(2)}) collective-permute-start(bf16[384,256]{1,0:T(8,128)(2,1)S(1)} %get-tuple-element.30), channel_id=1, source_target_pairs={{0,12},{4,8},{8,4},{12,0},{1,13},{5,9},{9,5},{13,1},{2,14},{6,10},... | collective-permute-start | bytes 589832 | tf_op jit(solution)/shard_map/ppermute | solution.py:263
  11.9 17.4 %collective-permute-start.4 = (bf16[4,48,512]{2,1,0:T(8,128)(2,1)S(1)}, bf16[4,48,512]{2,1,0:T(8,128)(2,1)S(1)}, u32[]{:S(2)}, u32[]{:S(2)}) collective-permute-start(bf16[4,48,512]{2,1,0:T(8,128)(2,1)S(1)} %join_pieces.1.refs_3_.refs_1_), channel_id=1, source_target_pairs={{0,2},{1,3},{2,0},{3,1},{16,18},{17,19},{18,16},{19,17},{4,6},{5,7... | collective-permute-start | bytes 589832 | tf_op jit(solution)/shard_map/ppermute | solution.py:282
  13.1 16.1 %collective-permute-start.5 = (bf16[4,48,512]{2,1,0:T(8,128)(2,1)S(1)}, bf16[4,48,512]{2,1,0:T(8,128)(2,1)S(1)}, u32[]{:S(2)}, u32[]{:S(2)}) collective-permute-start(bf16[4,48,512]{2,1,0:T(8,128)(2,1)S(1)} %join_pieces.1.refs_3_.refs_1_), channel_id=1, source_target_pairs={{0,16},{1,17},{2,18},{3,19},{16,0},{17,1},{18,2},{19,3},{4,20},{5,... | collective-permute-start | bytes 589832 | tf_op jit(solution)/shard_map/ppermute | solution.py:282
  14.4 14.9 %collective-permute-start.6 = (bf16[4,48,512]{2,1,0:T(8,128)(2,1)S(1)}, bf16[4,48,512]{2,1,0:T(8,128)(2,1)S(1)}, u32[]{:S(2)}, u32[]{:S(2)}) collective-permute-start(bf16[4,48,512]{2,1,0:T(8,128)(2,1)S(1)} %join_pieces.1.refs_3_.refs_1_), channel_id=1, source_target_pairs={{0,18},{1,19},{2,16},{3,17},{16,2},{17,3},{18,0},{19,1},{4,22},{5,... | collective-permute-start | bytes 589832 | tf_op jit(solution)/shard_map/ppermute | solution.py:282
  38.8 15.4 %collective-permute-start.11 = (bf16[512,256]{1,0:T(8,128)(2,1)S(1)}, bf16[512,256]{1,0:T(8,128)(2,1)S(1)}, u32[]{:S(2)}, u32[]{:S(2)}) collective-permute-start(bf16[512,256]{1,0:T(8,128)(2,1)S(1)} %compress.1.refs_1_), channel_id=1, source_target_pairs={{4,8},{8,4},{5,9},{9,5},{6,10},{10,6},{7,11},{11,7},{20,24},{24,20... | collective-permute-start | bytes 786440 | tf_op jit(solution)/shard_map/ppermute | solution.py:268
  41.5 14.3 %collective-permute-start.10 = (bf16[512,256]{1,0:T(8,128)(2,1)S(1)}, bf16[512,256]{1,0:T(8,128)(2,1)S(1)}, u32[]{:S(2)}, u32[]{:S(2)}) collective-permute-start(bf16[512,256]{1,0:T(8,128)(2,1)S(1)} %compress.1.refs_1_), channel_id=1, source_target_pairs={{0,4},{4,0},{8,12},{12,8},{1,5},{5,1},{9,13},{13,9},{2,6},{6,2},{1... | collective-permute-start | bytes 786440 | tf_op jit(solution)/shard_map/ppermute | solution.py:263
  54.2 37.8 %collective-permute-start.13 = (bf16[2,512,256]{2,1,0:T(8,128)(2,1)S(1)}, bf16[2,512,256]{2,1,0:T(8,128)(2,1)S(1)}, u32[]{:S(2)}, u32[]{:S(2)}) collective-permute-start(bf16[2,512,256]{2,1,0:T(8,128)(2,1)S(1)} %pad_maximum_fusion.refs_3_), channel_id=1, source_target_pairs={{4,0},{8,12},{5,1},{9,13},{6,2},{10,14},{7,3},{11,15},{20,16},{24,... | collective-permute-start | bytes 1572872 | tf_op jit(solution)/shard_map/ppermute | solution.py:273
  60.3 30.7 %collective-permute-start.14 = (bf16[2,384,256]{2,1,0:T(8,128)(2,1)S(1)}, bf16[2,384,256]{2,1,0:T(8,128)(2,1)S(1)}, u32[]{:S(2)}, u32[]{:S(2)}) collective-permute-start(bf16[2,384,256]{2,1,0:T(8,128)(2,1)S(1)} %pack_queries.5.refs_8_), channel_id=1, source_target_pairs={{0,8},{4,12},{8,0},{12,4},{1,9},{5,13},{9,1},{13,5},{2,10},{6,14},... | collective-permute-start | bytes 1179656 | tf_op jit(solution)/shard_map/ppermute | solution.py:263
  63.4 13.5 %collective-permute-start.15 = (bf16[128,512]{1,0:T(8,128)(2,1)S(1)}, bf16[128,512]{1,0:T(8,128)(2,1)S(1)}, u32[]{:S(2)}, u32[]{:S(2)}) collective-permute-start(bf16[128,512]{1,0:T(8,128)(2,1)S(1)} %slice_weight.1.refs_1_), channel_id=1, source_target_pairs={{0,4},{4,0},{8,12},{12,8},{1,5},{5,1},{9,13},{13,9},{2,6},{6,2},{1... | collective-permute-start | bytes 393224 | tf_op jit(solution)/shard_map/ppermute | solution.py:263
  67.6 33.4 %collective-permute-start.20 = (bf16[2,384,256]{2,1,0:T(8,128)(2,1)S(1)}, bf16[2,384,256]{2,1,0:T(8,128)(2,1)S(1)}, u32[]{:S(2)}, u32[]{:S(2)}) collective-permute-start(bf16[2,384,256]{2,1,0:T(8,128)(2,1)S(1)} %pack_queries.6.refs_9_), channel_id=1, source_target_pairs={{0,12},{4,8},{8,4},{12,0},{1,13},{5,9},{9,5},{13,1},{2,14},{6,10},... | collective-permute-start | bytes 1179656 | tf_op jit(solution)/shard_map/ppermute | solution.py:263
  76.9 27.0 %collective-permute-start.19 = (bf16[2,384,256]{2,1,0:T(8,128)(2,1)S(1)}, bf16[2,384,256]{2,1,0:T(8,128)(2,1)S(1)}, u32[]{:S(2)}, u32[]{:S(2)}) collective-permute-start(bf16[2,384,256]{2,1,0:T(8,128)(2,1)S(1)} %pack_queries.4.refs_7_), channel_id=1, source_target_pairs={{0,4},{4,0},{8,12},{12,8},{1,5},{5,1},{9,13},{13,9},{2,6},{6,2},{1... | collective-permute-start | bytes 1179656 | tf_op jit(solution)/shard_map/ppermute | solution.py:263
  77.5 39.3 %collective-permute-start.27 = (bf16[4,128,512]{2,1,0:T(8,128)(2,1)S(1)}, bf16[4,128,512]{2,1,0:T(8,128)(2,1)S(1)}, u32[]{:S(2)}, u32[]{:S(2)}) collective-permute-start(bf16[4,128,512]{2,1,0:T(8,128)(2,1)S(1)} %join_weight.1.refs_8_.refs_1_), channel_id=1, source_target_pairs={{0,2},{1,3},{2,0},{3,1},{16,18},{17,19},{18,16},{19,17},{4,6},{5,7... | collective-permute-start | bytes 1572872 | tf_op jit(solution)/shard_map/ppermute | solution.py:282
  91.1 25.7 %collective-permute-start.28 = (bf16[4,128,512]{2,1,0:T(8,128)(2,1)S(1)}, bf16[4,128,512]{2,1,0:T(8,128)(2,1)S(1)}, u32[]{:S(2)}, u32[]{:S(2)}) collective-permute-start(bf16[4,128,512]{2,1,0:T(8,128)(2,1)S(1)} %join_weight.1.refs_8_.refs_1_), channel_id=1, source_target_pairs={{0,16},{1,17},{2,18},{3,19},{16,0},{17,1},{18,2},{19,3},{4,20},{5,... | collective-permute-start | bytes 1572872 | tf_op jit(solution)/shard_map/ppermute | solution.py:282
  92.0 24.8 %collective-permute-start.29 = (bf16[4,128,512]{2,1,0:T(8,128)(2,1)S(1)}, bf16[4,128,512]{2,1,0:T(8,128)(2,1)S(1)}, u32[]{:S(2)}, u32[]{:S(2)}) collective-permute-start(bf16[4,128,512]{2,1,0:T(8,128)(2,1)S(1)} %join_weight.1.refs_8_.refs_1_), channel_id=1, source_target_pairs={{0,18},{1,19},{2,16},{3,17},{16,2},{17,3},{18,0},{19,1},{4,22},{5,... | collective-permute-start | bytes 1572872 | tf_op jit(solution)/shard_map/ppermute | solution.py:282
  123.0 21.4 %collective-permute-start.34 = (f32[256,512]{1,0:T(8,128)}, f32[256,512]{1,0:T(8,128)}, u32[]{:S(2)}, u32[]{:S(2)}) collective-permute-start(f32[256,512]{1,0:T(8,128)} %get-tuple-element.49), channel_id=1, source_target_pairs={{0,1},{1,0},{2,3},{3,2},{4,5},{5,4},{6,7},{7,6},{8,9},{9,8},{10,11... | collective-permute-start | bytes 1572872 | tf_op jit(solution)/shard_map/ppermute | solution.py:443
  123.1 22.2 %collective-permute-start.35 = (f32[256,512]{1,0:T(8,128)}, f32[256,512]{1,0:T(8,128)}, u32[]{:S(2)}, u32[]{:S(2)}) collective-permute-start(f32[256,512]{1,0:T(8,128)} %get-tuple-element.50), channel_id=1, source_target_pairs={{0,2},{1,3},{2,0},{3,1},{4,6},{5,7},{6,4},{7,5},{8,10},{9,11},{10,... | collective-permute-start | bytes 1572872 | tf_op jit(solution)/shard_map/ppermute | solution.py:443
  124.2 24.5 %collective-permute-start.36 = (f32[256,512]{1,0:T(8,128)}, f32[256,512]{1,0:T(8,128)}, u32[]{:S(2)}, u32[]{:S(2)}) collective-permute-start(f32[256,512]{1,0:T(8,128)} %get-tuple-element.51), channel_id=1, source_target_pairs={{0,3},{1,2},{2,1},{3,0},{4,7},{5,6},{6,5},{7,4},{8,11},{9,10},{10,... | collective-permute-start | bytes 1572872 | tf_op jit(solution)/shard_map/ppermute | solution.py:443
  125.1 13.8 %collective-permute-start.26 = (bf16[2,256,256]{2,1,0:T(8,128)(2,1)S(1)}, bf16[2,256,256]{2,1,0:T(8,128)(2,1)}, u32[]{:S(2)}, u32[]{:S(2)}) collective-permute-start(bf16[2,256,256]{2,1,0:T(8,128)(2,1)S(1)} %get-tuple-element.41.refs_2_.refs_1_), channel_id=1, source_target_pairs={{0,12},{4,8},{8,4},{12,0},{1,13},{5,9},{9,5},{13,1},{2,14},{6,10},... | collective-permute-start | bytes 786440 | tf_op jit(solution)/shard_map/ppermute | solution.py:263
  127.7 15.3 %collective-permute-start.22 = (bf16[384,256]{1,0:T(8,128)(2,1)}, bf16[384,256]{1,0:T(8,128)(2,1)S(1)}, u32[]{:S(2)}, u32[]{:S(2)}) collective-permute-start(bf16[384,256]{1,0:T(8,128)(2,1)} %get-tuple-element.42), channel_id=1, source_target_pairs={{0,4},{4,0},{8,12},{12,8},{1,5},{5,1},{9,13},{13,9},{2,6},{6,2},{1... | collective-permute-start | bytes 589832 | tf_op jit(solution)/shard_map/ppermute | solution.py:263
  138.9 12.9 %collective-permute-start.23 = (bf16[384,256]{1,0:T(8,128)(2,1)}, bf16[384,256]{1,0:T(8,128)(2,1)S(1)}, u32[]{:S(2)}, u32[]{:S(2)}) collective-permute-start(bf16[384,256]{1,0:T(8,128)(2,1)} %get-tuple-element.43), channel_id=1, source_target_pairs={{0,8},{4,12},{8,0},{12,4},{1,9},{5,13},{9,1},{13,5},{2,10},{6,14},... | collective-permute-start | bytes 589832 | tf_op jit(solution)/shard_map/ppermute | solution.py:263
  143.7 13.5 %collective-permute-start.24 = (bf16[384,256]{1,0:T(8,128)(2,1)S(1)}, bf16[384,256]{1,0:T(8,128)(2,1)S(1)}, u32[]{:S(2)}, u32[]{:S(2)}) collective-permute-start(bf16[384,256]{1,0:T(8,128)(2,1)S(1)} %copy-done.11), channel_id=1, source_target_pairs={{0,12},{4,8},{8,4},{12,0},{1,13},{5,9},{9,5},{13,1},{2,14},{6,10},... | collective-permute-start | bytes 589832 | tf_op jit(solution)/shard_map/ppermute | solution.py:263
  144.4 14.3 %collective-permute-start.31 = (f32[96,512]{1,0:T(8,128)S(1)}, f32[96,512]{1,0:T(8,128)}, u32[]{:S(2)}, u32[]{:S(2)}) collective-permute-start(f32[96,512]{1,0:T(8,128)S(1)} %get-tuple-element.52), channel_id=1, source_target_pairs={{0,1},{1,0},{2,3},{3,2},{4,5},{5,4},{6,7},{7,6},{8,9},{9,8},{10,11... | collective-permute-start | bytes 589832 | tf_op jit(solution)/shard_map/ppermute | solution.py:487
  145.3 13.3 %collective-permute-start.32 = (f32[96,512]{1,0:T(8,128)S(1)}, f32[96,512]{1,0:T(8,128)}, u32[]{:S(2)}, u32[]{:S(2)}) collective-permute-start(f32[96,512]{1,0:T(8,128)S(1)} %get-tuple-element.54), channel_id=1, source_target_pairs={{0,2},{1,3},{2,0},{3,1},{4,6},{5,7},{6,4},{7,5},{8,10},{9,11},{10,... | collective-permute-start | bytes 589832 | tf_op jit(solution)/shard_map/ppermute | solution.py:487
  (28 other events, 262.5 us)

commit v4 on v3

--- a/solution.py
+++ b/solution.py
@@ -11,7 +11,7 @@
 DH = 64
 KP = 256
 BF = jnp.bfloat16
-OPT = {'farsplit': 0, 'att': 'blocks', 'wz': 'relay', 'wslice': 'side', 'wreq': 'project', 'preq': 'two', 'jw': 'g12', 'rs': 'direct', 'agp': 'direct', 'late': 'g2', 'p1': 'line', 'p3': 'line2'}
+OPT = {'farsplit': 0, 'att': 'single', 'wz': 'direct', 'wslice': 'side', 'wreq': 'project', 'preq': 'two', 'jw': 'g12', 'rs': 'direct', 'agp': 'direct', 'late': 'none', 'p1': 'line', 'p3': 'line2', 'q1': 'no', 'sum': 'pallas', 'pad': 0, 'ws': 'none', 'lq': 0, 'nq': 1, 'pad2': 0, 'xj': 0, 'order': 'b0231'}
 F32 = jnp.float32
 VMEM_LIMIT = 24 * 1024 * 1024
 
@@ -147,7 +147,10 @@
         grad_q = term_q if h == 0 else grad_q + term_q
         key_part = term_k if h == 0 else key_part + term_k
         value_part = term_v if h == 0 else value_part + term_v
-    query_grad[...] = grad_q.astype(BF)
+    rows = grad_q.shape[0]
+    query_grad[:rows, :] = grad_q.astype(BF)
+    if query_grad.shape[0] > rows:
+        query_grad[rows:, :] = jnp.zeros_like(query_grad[rows:, :])
     if not first:
         key_part = key_part + before[0]
         value_part = value_part + before[1]
@@ -224,16 +227,26 @@
 
 
 def tail_body(nd, idx, *rest):
-    grads, (w, e, x, length_terms, input_grad, cg) = rest[:-6], rest[-6:]
+    length_terms, (input_grad, cg, terms) = rest[-3 - nd : -3], rest[-3:]
+    grads, (w, e, x) = rest[: -6 - nd], rest[-6 - nd : -3 - nd]
     for s in range(2):
         grad = jnp.concatenate([part[s] for part in grads], axis=1)
         cg[s * KP : (s + 1) * KP, :] = dot(grad, w[s], 1, 1).astype(BF)
     both = cg[...]
-    terms = dot(x[...], both, 1, 1)
+    terms[...] = dot(x[...], both, 1, 1)
     rows = x.shape[0] // nd
     for a in range(nd):
-        length_terms[idx[1] ^ a] = terms[a * rows : (a + 1) * rows, :]
+        length_terms[a][...] = terms[pl.ds(pl.multiple_of((idx[1] ^ a) * rows, 16), rows), :]
     input_grad[...] = dot(e[...], both, 1, 0).astype(BF)
+
+
+def sum_body(idx, *rest):
+    out = rest[-1]
+    total = rest[0][...]
+    for x in rest[1:-1]:
+        total = total + x[...]
+    for s in range(2):
+        out[:, s, :] = total[:, s * KP : (s + 1) * KP]
 
 
 def place_body(n, own, idx, *rest):
@@ -243,7 +256,7 @@
     for k in range(n):
         col = pl.multiple_of((idx[0] ^ k) * own, own)
         for a in range(parts):
-            out[:, pl.ds(col + a * width, width)] = rest[k * parts + a][...]
+            out[:, pl.ds(col + a * width, width)] = rest[k * parts + a][: out.shape[0], :]
 
 
 def by_heads(ng, n, nd, inputs, queries, cotangent, length_proj, key_value_weight):
@@ -262,11 +275,13 @@
     def to_line(x, k):
         return lax.ppermute(x, "ctx", swap(n, k))
 
-    def over_line(x):
+    def over_line(x, after=()):
         side = to_line(x, 1)
-        near = jnp.stack(
-            [lax.ppermute(x, "ctx", [(1, 2), (2, 1)]), lax.ppermute(x, "ctx", [(0, 2), (3, 1)])]
-        )
+        near = [lax.ppermute(x, "ctx", [(1, 2), (2, 1)]), lax.ppermute(x, "ctx", [(0, 2), (3, 1)])]
+        if after:
+            near = call(join_body, [shape((2, *x.shape), BF)], [idx, *near], after, name="join_near")[0]
+        else:
+            near = jnp.stack(near)
         if OPT["farsplit"]:
             far = jnp.stack([lax.ppermute(near[a], "ctx", [(1, 0), (2, 3)]) for a in range(2)])
         else:
@@ -307,10 +322,11 @@
     pieces = [piece] + [to_line(piece, k) for k in range(1, n)]
     blocks = [blocks[0]] + [to_line(blocks[k], k) for k in range(1, n)]
     line = call(
-        join_body, [shape((n, part, 2 * KP), BF)], [idx, *pieces], [blocks[1]], name="join_pieces"
+        join_body, [shape((n, part, 2 * KP), BF)], [idx, *pieces], [blocks[1]] if OPT["xj"] else [], name="join_pieces"
     )[0]
     across = over_plane(line)
     o = OPT
+    packed0 = pack_queries(0, [line])
     packed3 = pack_queries(3, [line]) if o["p3"] == "line" else None
     packed1 = pack_queries(1, [line]) if o["p1"] == "line" else None
     packed2 = pack_queries(2, [line]) if o["p3"] == "line2" else None
@@ -318,7 +334,7 @@
         join_body,
         [shape((n, n, part, 2 * KP), BF)],
         [idx, *across],
-        [*blocks[2:], *[p for p in (packed1, packed2, packed3) if p is not None]],
+        [*blocks[2:], *[p for p in (packed0, packed1, packed2, packed3) if p is not None]],
         name="join_lines",
     )[0]
     if packed3 is None:
@@ -343,10 +359,11 @@
         [pltpu.VMEM((n * rows, 2 * KP), BF)],
         name="compress",
     )[0]
-    parts = over_line(compressed)
+    early = to_line(packed1, 1) if o["nq"] else None
+    parts = over_line(compressed, [early] if o["nq"] else [])
     if packed1 is None:
         packed1 = pack_queries(1, [parts[2]])
-    qg = [pack_queries(0, []), to_line(packed1, 1), to_line(packed2, 2), to_line(packed3, 3)]
+    qg = [packed0, to_line(packed1, 1) if early is None else early, to_line(packed2, 2), to_line(packed3, 3)]
     if w_piece is None:
         gates = dict(side=parts[1], c=compressed, near=parts[2], far=parts[3], q2=qg[2])
         w_piece = slice_weight([gates[o["wslice"]]])
@@ -399,12 +416,12 @@
         query_grads = [parts_q]
         accs.append(acc)
     else:
-        order, by_block, acc = o.get("order", (0, 2, 3, 1)), {}, None
+        order, by_block, acc = [int(c) for c in str(o["order"])[1:]], {}, None
         for k in order:
             first, last = k == order[0], k == order[-1]
             by_block[k], acc = call(
                 functools.partial(attention_body, heads, first, last),
-                [shape((rows, own), BF), shape((2, KP, own), BF if last else F32)],
+                [shape((rows + (o["pad2"] if k == 2 and o["pad2"] else o["pad"]), own), BF), shape((2, KP, own), BF if last else F32)],
                 [idx, keys, values, qg[k]] + ([] if first else [acc]),
                 name="attention",
             )
@@ -438,12 +455,10 @@
             name="weight",
         )
         keep = weight[0]
-        weight_grad = weight[0]
-        for a in range(1, nd):
-            weight_grad = weight_grad + lax.ppermute(weight[a], "dp", swap(nd, a))
-    weight_grad = weight_grad.reshape(-1, 2, own)
+        weight = [weight[0]] + [lax.ppermute(weight[a], "dp", swap(nd, a)) for a in range(1, nd)]
 
     last = grads[-1]
+    ret2 = to_line(query_grads[0][2], 2) if o["pad2"] else None
     jw = dict(
         g12=[keep, last[1], last[2]],
         g1=[keep, last[1]],
@@ -452,7 +467,7 @@
         gall=[keep, *grads[0][1:], *last[1:]],
         keys=[keys],
         acc=[keep],
-    )[o["jw"]]
+    )[o["jw"]] + ([ret2] if o["pad2"] else [])
     w_across = over_plane(w_line)
     w_own = call(
         join_body, [shape((n, n, w_rows, 2 * own), BF)], [idx, *w_across], jw, name="join_weights"
@@ -472,28 +487,37 @@
     returned = []
     for k in range(n):
         for a in range(na):
-            returned.append(to_line(late[a * (n - 1) + k - 1], k) if k else query_grads[a][0])
+            if k == 2 and o["pad2"]:
+                returned.append(ret2)
+            else:
+                returned.append(to_line(late[a * (n - 1) + k - 1], k) if k else query_grads[a][0])
 
     tail_in = [idx, *(grads[a][k] for k in range(n) for a in range(na)), w_all, length_proj.reshape(rows, 2 * KP), tokens]
-    terms, input_grad = call(
+    *terms, input_grad = call(
         functools.partial(tail_body, nd),
-        [shape((nd, rows // nd, 2 * KP), F32), shape((rows, width), BF)],
+        [shape((rows // nd, 2 * KP), F32)] * nd + [shape((rows, width), BF)],
         tail_in,
-        scratch=[pltpu.VMEM((2 * KP, width), BF)],
+        scratch=[pltpu.VMEM((2 * KP, width), BF), pltpu.VMEM((rows, 2 * KP), F32)],
         name="tail",
     )
-    length_grad = terms[0]
-    for a in range(1, nd):
-        length_grad = length_grad + lax.ppermute(terms[a], "dp", swap(nd, a))
-    length_grad = length_grad.reshape(-1, 2, KP)
-
+    terms = [terms[0]] + [lax.ppermute(terms[a], "dp", swap(nd, a)) for a in range(1, nd)]
     query_grad = call(
         functools.partial(place_body, n, own),
         [shape((rows, width), BF)],
         [idx, *returned],
-        [terms],
+        [terms[0]],
         name="place",
     )[0]
+    if o["sum"] == "pallas":
+        length_grad = call(sum_body, [shape((rows // nd, 2, KP), F32)], [idx, *terms], [query_grad] if o["lq"] else [], name="sum_terms")[0]
+    else:
+        length_grad = (terms[0] + terms[1] + terms[2] + terms[3]).reshape(-1, 2, KP)
+
+    if o["rs"] != "two":
+        hold = dict(place=[query_grad], lt=[length_grad], none=[], t1=[terms[1]])[o["ws"]]
+        weight_grad = call(sum_body, [shape((width // nd, 2, own), F32)], [idx, *weight], hold, name="sum_weight")[0]
+    else:
+        weight_grad = weight_grad.reshape(-1, 2, own)
     return query_grad[None], input_grad[None], length_grad, weight_grad
 
 

time: 163 us -> 157 us (0.963)
  waiting for transfers between devices: 73.8 us -> 83.8 us
  starting transfers between devices: 47.6 us -> 39 us
  Pallas kernels: 30.2 us -> 27.2 us
  other arithmetic: 2.82 us -> 0 us
    ppermute x17 -> x19, waiting for transfers between devices: 53.7 us -> 74.5 us  [to_line(): return lax.ppermute(x, 'ctx', swap(n, k))]
    ppermute x2 -> x1, waiting for transfers between devices: 8.42 us -> 0.01 us  [over_line(): lax.ppermute(x, 'ctx', [(0, 2), (3, 1)])]
    ppermute x2, starting transfers between devices: 9.8 us -> 4.58 us  [over_cores(): return lax.ppermute(x, 'dp', swap(nd, 1))]
    pallas_call x20, Pallas kernels: 30.2 us -> 27.2 us  [call(): pl.pallas_call(run, out_shape=outs, in_specs=[pl.BlockSpec(memory_space=p...]
    add x2 -> x0, other arithmetic: 2.74 us -> none  [the longest x1 1.57 us: by_heads(): weight_grad = weight_grad + lax.ppermute(weight[a], 'dp', swap(nd, a))]
    ppermute x2 -> x1, starting transfers between devices: 5.37 us -> 2.73 us  [over_line(): lax.ppermute(x, 'ctx', [(1, 2), (2, 1)])]
    ppermute x2, waiting for transfers between devices: 3.06 us -> 0.99 us  [over_cores(): return lax.ppermute(x, 'dp', swap(nd, 1))]
    reshape x2 -> x0, local copies, waits for them, and re-layouts: 1.92 us -> none  [the longest x1 1.12 us: by_heads(): weight_grad = weight_grad.reshape(-1, 2, own)]
  transfers between devices with their start and end apart: 37 -> 36, of which waited for: 16 -> 16; matrix products, arithmetic and copies ran while one was open for 2% -> 0% of each run, Pallas kernels for 17% -> 16%
where the time goes in v4:
time: 157 us; the launch traced here: 156 us
  waiting for transfers between devices  83.8 us (53%)
  starting transfers between devices  39 us (25%)
  Pallas kernels  27.2 us (17%)
  local copies, waits for them, and re-layouts  4.64 us (3%)
    ppermute x19, waiting for transfers between devices, to_line(): return lax.ppermute(x, 'ctx', swap(n, k))  74.5 us
    pallas_call x20, Pallas kernels, call(): pl.pallas_call(run, out_shape=outs, in_specs=[pl.BlockSpec(memory_space=p...  27.2 us
    ppermute x19, starting transfers between devices, to_line(): return lax.ppermute(x, 'ctx', swap(n, k))  19.2 us
    ppermute x6, starting transfers between devices, over_plane(): across.append(lax.ppermute(x, ('groups', 'dp'), perm))  5.43 us
    ppermute x1, waiting for transfers between devices, over_line(): lax.ppermute(x, 'ctx', [(1, 2), (2, 1)])  4.64 us
    ppermute x2, starting transfers between devices, over_cores(): return lax.ppermute(x, 'dp', swap(nd, 1))  4.58 us
    unnamed x19, local copies, waits for them, and re-layouts  3.72 us
    ppermute x3, waiting for transfers between devices, by_heads(): lax.ppermute(weight[a], 'dp', swap(nd, a))  3.67 us
  transfers between devices with their start and end apart: 36, of which 16 were waited for; matrix products, arithmetic and copies ran while one was open for 0% of the time, Pallas kernels for 16%

profile of v4, /device:TPU:9, one launch (start us, length us, event | category | flops | bytes accessed | tf_op | source)
XLA Modules:
  0.0 155.7 jit_solution(1923293966609112616)
XLA Ops:
  1.6 2.5 %collective-permute-start.1 = (bf16[48,512]{1,0:T(8,128)(2,1)S(1)}, bf16[48,512]{1,0:T(8,128)(2,1)S(1)}, u32[]{:S(2)}, u32[]{:S(2)}) collective-permute-start(bf16[48,512]{1,0:T(8,128)(2,1)S(1)} %bitcast.31), channel_id=1, source_target_pairs={{0,8},{4,12},{8,0},{12,4},{1,9},{5,13},{9,1},{13,5},{2,10},{6,14},... | collective-permute-start | bytes 147464 | tf_op jit(solution)/shard_map/ppermute | solution.py:276
  6.1 3.3 %collective-permute-start.6 = (bf16[384,256]{1,0:T(8,128)(2,1)S(1)}, bf16[384,256]{1,0:T(8,128)(2,1)S(1)}, u32[]{:S(2)}, u32[]{:S(2)}) collective-permute-start(bf16[384,256]{1,0:T(8,128)(2,1)S(1)} %get-tuple-element.25), channel_id=1, source_target_pairs={{0,8},{4,12},{8,0},{12,4},{1,9},{5,13},{9,1},{13,5},{2,10},{6,14},... | collective-permute-start | bytes 589832 | tf_op jit(solution)/shard_map/ppermute | solution.py:276
  16.8 4.6 %collective-permute-done.6.refs_5_ = bf16[384,256]{1,0:T(8,128)(2,1)S(1)} collective-permute-done((bf16[384,256]{1,0:T(8,128)(2,1)S(1)}, bf16[384,256]{1,0:T(8,128)(2,1)S(1)}, u32[]{:S(2)}, u32[]{:S(2)}) %collective-permute-start.6) | collective-permute-done | bytes 196640 | tf_op jit(solution)/shard_map/ppermute | solution.py:276
  21.4 4.9 %collective-permute-done.7.refs_6_ = bf16[384,256]{1,0:T(8,128)(2,1)S(1)} collective-permute-done((bf16[384,256]{1,0:T(8,128)(2,1)S(1)}, bf16[384,256]{1,0:T(8,128)(2,1)S(1)}, u32[]{:S(2)}, u32[]{:S(2)}) %collective-permute-start.7) | collective-permute-done | bytes 196640 | tf_op jit(solution)/shard_map/ppermute | solution.py:276
  30.3 4.4 %collective-permute-done.9.refs_4_ = bf16[384,256]{1,0:T(8,128)(2,1)S(1)} collective-permute-done((bf16[384,256]{1,0:T(8,128)(2,1)S(1)}, bf16[384,256]{1,0:T(8,128)(2,1)S(1)}, u32[]{:S(2)}, u32[]{:S(2)}) %collective-permute-start.9) | collective-permute-done | bytes 196640 | tf_op jit(solution)/shard_map/ppermute | solution.py:276
  36.0 2.7 %collective-permute-start.11 = (bf16[512,256]{1,0:T(8,128)(2,1)S(1)}, bf16[512,256]{1,0:T(8,128)(2,1)S(1)}, u32[]{:S(2)}, u32[]{:S(2)}) collective-permute-start(bf16[512,256]{1,0:T(8,128)(2,1)S(1)} %compress.1.refs_1_), channel_id=1, source_target_pairs={{4,8},{8,4},{5,9},{9,5},{6,10},{10,6},{7,11},{11,7},{20,24},{24,20... | collective-permute-start | bytes 786440 | tf_op jit(solution)/shard_map/ppermute | solution.py:280
  40.1 2.5 %collective-permute-start.10 = (bf16[512,256]{1,0:T(8,128)(2,1)S(1)}, bf16[512,256]{1,0:T(8,128)(2,1)S(1)}, u32[]{:S(2)}, u32[]{:S(2)}) collective-permute-start(bf16[512,256]{1,0:T(8,128)(2,1)S(1)} %compress.1.refs_1_), channel_id=1, source_target_pairs={{0,4},{4,0},{8,12},{12,8},{1,5},{5,1},{9,13},{13,9},{2,6},{6,2},{1... | collective-permute-start | bytes 786440 | tf_op jit(solution)/shard_map/ppermute | solution.py:276
  43.5 4.6 %collective-permute-done.11.refs_1_ = bf16[512,256]{1,0:T(8,128)(2,1)S(1)} collective-permute-done((bf16[512,256]{1,0:T(8,128)(2,1)S(1)}, bf16[512,256]{1,0:T(8,128)(2,1)S(1)}, u32[]{:S(2)}, u32[]{:S(2)}) %collective-permute-start.11) | collective-permute-done | bytes 262176 | tf_op jit(solution)/shard_map/ppermute | solution.py:280
  50.2 2.8 %collective-permute-done.10.refs_2_ = bf16[512,256]{1,0:T(8,128)(2,1)S(1)} collective-permute-done((bf16[512,256]{1,0:T(8,128)(2,1)S(1)}, bf16[512,256]{1,0:T(8,128)(2,1)S(1)}, u32[]{:S(2)}, u32[]{:S(2)}) %collective-permute-start.10) | collective-permute-done | bytes 262176 | tf_op jit(solution)/shard_map/ppermute | solution.py:276
  53.6 2.0 %collective-permute-start.17 = (bf16[128,512]{1,0:T(8,128)(2,1)S(1)}, bf16[128,512]{1,0:T(8,128)(2,1)S(1)}, u32[]{:S(2)}, u32[]{:S(2)}) collective-permute-start(bf16[128,512]{1,0:T(8,128)(2,1)S(1)} %slice_weight.1.refs_1_), channel_id=1, source_target_pairs={{0,8},{4,12},{8,0},{12,4},{1,9},{5,13},{9,1},{13,5},{2,10},{6,14},... | collective-permute-start | bytes 393224 | tf_op jit(solution)/shard_map/ppermute | solution.py:276
  56.3 9.0 %collective-permute-done.16.refs_2_ = bf16[128,512]{1,0:T(8,128)(2,1)S(1)} collective-permute-done((bf16[128,512]{1,0:T(8,128)(2,1)S(1)}, bf16[128,512]{1,0:T(8,128)(2,1)S(1)}, u32[]{:S(2)}, u32[]{:S(2)}) %collective-permute-start.16) | collective-permute-done | bytes 131104 | tf_op jit(solution)/shard_map/ppermute | solution.py:276
  65.9 12.3 %collective-permute-done.17.refs_3_ = bf16[128,512]{1,0:T(8,128)(2,1)S(1)} collective-permute-done((bf16[128,512]{1,0:T(8,128)(2,1)S(1)}, bf16[128,512]{1,0:T(8,128)(2,1)S(1)}, u32[]{:S(2)}, u32[]{:S(2)}) %collective-permute-start.17) | collective-permute-done | bytes 131104 | tf_op jit(solution)/shard_map/ppermute | solution.py:276
  78.3 3.9 %collective-permute-done.18.refs_4_ = bf16[128,512]{1,0:T(8,128)(2,1)S(1)} collective-permute-done((bf16[128,512]{1,0:T(8,128)(2,1)S(1)}, bf16[128,512]{1,0:T(8,128)(2,1)S(1)}, u32[]{:S(2)}, u32[]{:S(2)}) %collective-permute-start.18) | collective-permute-done | bytes 131104 | tf_op jit(solution)/shard_map/ppermute | solution.py:276
  86.5 8.6 %collective-permute-done.19.refs_6_ = bf16[2,384,256]{2,1,0:T(8,128)(2,1)S(1)} collective-permute-done((bf16[2,384,256]{2,1,0:T(8,128)(2,1)S(1)}, bf16[2,384,256]{2,1,0:T(8,128)(2,1)S(1)}, u32[]{:S(2)}, u32[]{:S(2)}) %collective-permute-start.19) | collective-permute-done | bytes 393248 | tf_op jit(solution)/shard_map/ppermute | solution.py:276
  95.1 8.3 %attention.1 = (bf16[384,256]{1,0:T(8,128)(2,1)S(1)}, bf16[384,256]{1,0:T(8,128)(2,1)S(1)}, bf16[384,256]{1,0:T(8,128)(2,1)S(1)}, bf16[384,256]{1,0:T(8,128)(2,1)S(1)}, bf16[2,256,256]{2,1,0:T(8,128)(2,1)S(1)}) custom-call(s32[6]{0:T(128)S(1)} %stack.27.refs_0_, bf16[256,256]{1,0:T(8,128)(2,1)S(1)} %get-tuple-element.29.refs_1_, ...), custom_call_target="tpu_custom_call" | custom-call | flops 1 | bytes 1 | tf_op jit(solution)/shard_map/attention/pallas_call | solution.py:29
  103.5 2.0 %collective-permute-start.24 = (bf16[2,256,256]{2,1,0:T(8,128)(2,1)S(1)}, bf16[2,256,256]{2,1,0:T(8,128)(2,1)S(1)}, u32[]{:S(2)}, u32[]{:S(2)}) collective-permute-start(bf16[2,256,256]{2,1,0:T(8,128)(2,1)S(1)} %get-tuple-element.35.refs_2_.refs_1_), channel_id=1, source_target_pairs={{0,8},{4,12},{8,0},{12,4},{1,9},{5,13},{9,1},{13,5},{2,10},{6,14},... | collective-permute-start | bytes 786440 | tf_op jit(solution)/shard_map/ppermute | solution.py:276
  106.5 3.1 %collective-permute-done.23.refs_6_.refs_4_.refs_2_ = bf16[2,256,256]{2,1,0:T(8,128)(2,1)S(1)} collective-permute-done((bf16[2,256,256]{2,1,0:T(8,128)(2,1)S(1)}, bf16[2,256,256]{2,1,0:T(8,128)(2,1)S(1)}, u32[]{:S(2)}, u32[]{:S(2)}) %collective-permute-start.23) | collective-permute-done | bytes 262176 | tf_op jit(solution)/shard_map/ppermute | solution.py:276
  109.6 5.6 %collective-permute-done.24.refs_7_.refs_3_ = bf16[2,256,256]{2,1,0:T(8,128)(2,1)S(1)} collective-permute-done((bf16[2,256,256]{2,1,0:T(8,128)(2,1)S(1)}, bf16[2,256,256]{2,1,0:T(8,128)(2,1)S(1)}, u32[]{:S(2)}, u32[]{:S(2)}) %collective-permute-start.24) | collective-permute-done | bytes 262176 | tf_op jit(solution)/shard_map/ppermute | solution.py:276
  115.9 3.3 %collective-permute-start.29 = (bf16[4,4,128,512]{3,2,1,0:T(8,128)(2,1)S(1)}, bf16[4,4,128,512]{3,2,1,0:T(8,128)(2,1)S(1)}, u32[]{:S(2)}, u32[]{:S(2)}) collective-permute-start(bf16[4,4,128,512]{3,2,1,0:T(8,128)(2,1)S(1)} %join_weights.1.refs_1_), channel_id=1, source_target_pairs={{0,1},{1,0},{2,3},{3,2},{4,5},{5,4},{6,7},{7,6},{8,9},{9,8},{10,11... | collective-permute-start | bytes 6291464 | tf_op jit(solution)/shard_map/ppermute | solution.py:301
  123.0 1.9 %collective-permute-start.20 = (bf16[384,256]{1,0:T(8,128)(2,1)S(1)}, bf16[384,256]{1,0:T(8,128)(2,1)S(1)}, u32[]{:S(2)}, u32[]{:S(2)}) collective-permute-start(bf16[384,256]{1,0:T(8,128)(2,1)S(1)} %get-tuple-element.32), channel_id=1, source_target_pairs={{0,4},{4,0},{8,12},{12,8},{1,5},{5,1},{9,13},{13,9},{2,6},{6,2},{1... | collective-permute-start | bytes 589832 | tf_op jit(solution)/shard_map/ppermute | solution.py:276
  126.0 9.0 %collective-permute-done.25.refs_4_ = bf16[2,256,256]{2,1,0:T(8,128)(2,1)S(1)} collective-permute-done((bf16[2,256,256]{2,1,0:T(8,128)(2,1)S(1)}, bf16[2,256,256]{2,1,0:T(8,128)(2,1)S(1)}, u32[]{:S(2)}, u32[]{:S(2)}) %collective-permute-start.25) | collective-permute-done | bytes 262176 | tf_op jit(solution)/shard_map/ppermute | solution.py:276
  135.0 3.6 %tail.1 = (f32[96,512]{1,0:T(8,128)S(1)}, f32[96,512]{1,0:T(8,128)S(1)}, f32[96,512]{1,0:T(8,128)S(1)}, f32[96,512]{1,0:T(8,128)S(1)}, bf16[384,1024]{1,0:T(8,128)(2,1)}) custom-call(s32[6]{0:T(128)S(1)} %stack.27.refs_0_, bf16[2,256,256]{2,1,0:T(8,128)(2,1)S(1)} %get-tuple-element.35.refs_2_.refs_1_, ...), custom_call_target="tpu_custom_call" | custom-call | flops 1 | bytes 1 | tf_op jit(solution)/shard_map/tail/pallas_call | solution.py:29
  141.4 3.7 %collective-permute-done.35.refs_4_ = f32[256,512]{1,0:T(8,128)S(1)} collective-permute-done((f32[256,512]{1,0:T(8,128)S(1)}, f32[256,512]{1,0:T(8,128)S(1)}, u32[]{:S(2)}, u32[]{:S(2)}) %collective-permute-start.35) | collective-permute-done | bytes 524320 | tf_op jit(solution)/shard_map/ppermute | solution.py:458
  147.1 5.8 %collective-permute-done.22.refs_4_ = bf16[384,256]{1,0:T(8,128)(2,1)S(1)} collective-permute-done((bf16[384,256]{1,0:T(8,128)(2,1)S(1)}, bf16[384,256]{1,0:T(8,128)(2,1)S(1)}, u32[]{:S(2)}, u32[]{:S(2)}) %collective-permute-start.22) | collective-permute-done | bytes 196640 | tf_op jit(solution)/shard_map/ppermute | solution.py:276
  (89 shorter events, 40.5 us)
Async XLA Ops:
  6.1 15.3 %collective-permute-start.6 = (bf16[384,256]{1,0:T(8,128)(2,1)S(1)}, bf16[384,256]{1,0:T(8,128)(2,1)S(1)}, u32[]{:S(2)}, u32[]{:S(2)}) collective-permute-start(bf16[384,256]{1,0:T(8,128)(2,1)S(1)} %get-tuple-element.25), channel_id=1, source_target_pairs={{0,8},{4,12},{8,0},{12,4},{1,9},{5,13},{9,1},{13,5},{2,10},{6,14},... | collective-permute-start | bytes 589832 | tf_op jit(solution)/shard_map/ppermute | solution.py:276
  9.4 16.9 %collective-permute-start.7 = (bf16[384,256]{1,0:T(8,128)(2,1)S(1)}, bf16[384,256]{1,0:T(8,128)(2,1)S(1)}, u32[]{:S(2)}, u32[]{:S(2)}) collective-permute-start(bf16[384,256]{1,0:T(8,128)(2,1)S(1)} %get-tuple-element.26), channel_id=1, source_target_pairs={{0,12},{4,8},{8,4},{12,0},{1,13},{5,9},{9,5},{13,1},{2,14},{6,10},... | collective-permute-start | bytes 589832 | tf_op jit(solution)/shard_map/ppermute | solution.py:276
  9.9 16.3 %collective-permute-start.3 = (bf16[4,48,512]{2,1,0:T(8,128)(2,1)S(1)}, bf16[4,48,512]{2,1,0:T(8,128)(2,1)S(1)}, u32[]{:S(2)}, u32[]{:S(2)}) collective-permute-start(bf16[4,48,512]{2,1,0:T(8,128)(2,1)S(1)} %join_pieces.1.refs_3_.refs_1_), channel_id=1, source_target_pairs={{0,2},{1,3},{2,0},{3,1},{16,18},{17,19},{18,16},{19,17},{4,6},{5,7... | collective-permute-start | bytes 589832 | tf_op jit(solution)/shard_map/ppermute | solution.py:297
  11.2 15.1 %collective-permute-start.4 = (bf16[4,48,512]{2,1,0:T(8,128)(2,1)S(1)}, bf16[4,48,512]{2,1,0:T(8,128)(2,1)S(1)}, u32[]{:S(2)}, u32[]{:S(2)}) collective-permute-start(bf16[4,48,512]{2,1,0:T(8,128)(2,1)S(1)} %join_pieces.1.refs_3_.refs_1_), channel_id=1, source_target_pairs={{0,16},{1,17},{2,18},{3,19},{16,0},{17,1},{18,2},{19,3},{4,20},{5,... | collective-permute-start | bytes 589832 | tf_op jit(solution)/shard_map/ppermute | solution.py:297
  12.5 13.8 %collective-permute-start.5 = (bf16[4,48,512]{2,1,0:T(8,128)(2,1)S(1)}, bf16[4,48,512]{2,1,0:T(8,128)(2,1)S(1)}, u32[]{:S(2)}, u32[]{:S(2)}) collective-permute-start(bf16[4,48,512]{2,1,0:T(8,128)(2,1)S(1)} %join_pieces.1.refs_3_.refs_1_), channel_id=1, source_target_pairs={{0,18},{1,19},{2,16},{3,17},{16,2},{17,3},{18,0},{19,1},{4,22},{5,... | collective-permute-start | bytes 589832 | tf_op jit(solution)/shard_map/ppermute | solution.py:297
  28.2 15.3 %collective-permute-start.13 = (bf16[2,384,256]{2,1,0:T(8,128)(2,1)S(1)}, bf16[2,384,256]{2,1,0:T(8,128)(2,1)S(1)}, u32[]{:S(2)}, u32[]{:S(2)}) collective-permute-start(bf16[2,384,256]{2,1,0:T(8,128)(2,1)S(1)} %pack_queries.5.refs_8_.refs_7_), channel_id=1, source_target_pairs={{0,4},{4,0},{8,12},{12,8},{1,5},{5,1},{9,13},{13,9},{2,6},{6,2},{1... | collective-permute-start | bytes 1179656 | tf_op jit(solution)/shard_map/ppermute | solution.py:276
  40.1 12.9 %collective-permute-start.10 = (bf16[512,256]{1,0:T(8,128)(2,1)S(1)}, bf16[512,256]{1,0:T(8,128)(2,1)S(1)}, u32[]{:S(2)}, u32[]{:S(2)}) collective-permute-start(bf16[512,256]{1,0:T(8,128)(2,1)S(1)} %compress.1.refs_1_), channel_id=1, source_target_pairs={{0,4},{4,0},{8,12},{12,8},{1,5},{5,1},{9,13},{13,9},{2,6},{6,2},{1... | collective-permute-start | bytes 786440 | tf_op jit(solution)/shard_map/ppermute | solution.py:276
  42.6 42.6 %collective-permute-start.15 = (bf16[2,384,256]{2,1,0:T(8,128)(2,1)S(1)}, bf16[2,384,256]{2,1,0:T(8,128)(2,1)S(1)}, u32[]{:S(2)}, u32[]{:S(2)}) collective-permute-start(bf16[2,384,256]{2,1,0:T(8,128)(2,1)S(1)} %pack_queries.6.refs_9_.refs_8_), channel_id=1, source_target_pairs={{0,8},{4,12},{8,0},{12,4},{1,9},{5,13},{9,1},{13,5},{2,10},{6,14},... | collective-permute-start | bytes 1179656 | tf_op jit(solution)/shard_map/ppermute | solution.py:276
  48.7 36.8 %collective-permute-start.14 = (bf16[2,512,256]{2,1,0:T(8,128)(2,1)S(1)}, bf16[2,512,256]{2,1,0:T(8,128)(2,1)S(1)}, u32[]{:S(2)}, u32[]{:S(2)}) collective-permute-start(bf16[2,512,256]{2,1,0:T(8,128)(2,1)S(1)} %join_near.1.refs_3_), channel_id=1, source_target_pairs={{4,0},{8,12},{5,1},{9,13},{6,2},{10,14},{7,3},{11,15},{20,16},{24,... | collective-permute-start | bytes 1572872 | tf_op jit(solution)/shard_map/ppermute | solution.py:288
  53.6 24.6 %collective-permute-start.17 = (bf16[128,512]{1,0:T(8,128)(2,1)S(1)}, bf16[128,512]{1,0:T(8,128)(2,1)S(1)}, u32[]{:S(2)}, u32[]{:S(2)}) collective-permute-start(bf16[128,512]{1,0:T(8,128)(2,1)S(1)} %slice_weight.1.refs_1_), channel_id=1, source_target_pairs={{0,8},{4,12},{8,0},{12,4},{1,9},{5,13},{9,1},{13,5},{2,10},{6,14},... | collective-permute-start | bytes 393224 | tf_op jit(solution)/shard_map/ppermute | solution.py:276
  55.6 26.6 %collective-permute-start.18 = (bf16[128,512]{1,0:T(8,128)(2,1)S(1)}, bf16[128,512]{1,0:T(8,128)(2,1)S(1)}, u32[]{:S(2)}, u32[]{:S(2)}) collective-permute-start(bf16[128,512]{1,0:T(8,128)(2,1)S(1)} %slice_weight.1.refs_1_), channel_id=1, source_target_pairs={{0,12},{4,8},{8,4},{12,0},{1,13},{5,9},{9,5},{13,1},{2,14},{6,10},... | collective-permute-start | bytes 393224 | tf_op jit(solution)/shard_map/ppermute | solution.py:276
  65.3 29.8 %collective-permute-start.19 = (bf16[2,384,256]{2,1,0:T(8,128)(2,1)S(1)}, bf16[2,384,256]{2,1,0:T(8,128)(2,1)S(1)}, u32[]{:S(2)}, u32[]{:S(2)}) collective-permute-start(bf16[2,384,256]{2,1,0:T(8,128)(2,1)S(1)} %pack_queries.7.refs_9_), channel_id=1, source_target_pairs={{0,12},{4,8},{8,4},{12,0},{1,13},{5,9},{9,5},{13,1},{2,14},{6,10},... | collective-permute-start | bytes 1179656 | tf_op jit(solution)/shard_map/ppermute | solution.py:276
  82.7 23.8 %collective-permute-start.26 = (bf16[4,128,512]{2,1,0:T(8,128)(2,1)S(1)}, bf16[4,128,512]{2,1,0:T(8,128)(2,1)S(1)}, u32[]{:S(2)}, u32[]{:S(2)}) collective-permute-start(bf16[4,128,512]{2,1,0:T(8,128)(2,1)S(1)} %join_weight.1.refs_8_.refs_1_), channel_id=1, source_target_pairs={{0,2},{1,3},{2,0},{3,1},{16,18},{17,19},{18,16},{19,17},{4,6},{5,7... | collective-permute-start | bytes 1572872 | tf_op jit(solution)/shard_map/ppermute | solution.py:297
  84.0 22.5 %collective-permute-start.27 = (bf16[4,128,512]{2,1,0:T(8,128)(2,1)S(1)}, bf16[4,128,512]{2,1,0:T(8,128)(2,1)S(1)}, u32[]{:S(2)}, u32[]{:S(2)}) collective-permute-start(bf16[4,128,512]{2,1,0:T(8,128)(2,1)S(1)} %join_weight.1.refs_8_.refs_1_), channel_id=1, source_target_pairs={{0,16},{1,17},{2,18},{3,19},{16,0},{17,1},{18,2},{19,3},{4,20},{5,... | collective-permute-start | bytes 1572872 | tf_op jit(solution)/shard_map/ppermute | solution.py:297
  85.2 21.3 %collective-permute-start.28 = (bf16[4,128,512]{2,1,0:T(8,128)(2,1)S(1)}, bf16[4,128,512]{2,1,0:T(8,128)(2,1)S(1)}, u32[]{:S(2)}, u32[]{:S(2)}) collective-permute-start(bf16[4,128,512]{2,1,0:T(8,128)(2,1)S(1)} %join_weight.1.refs_8_.refs_1_), channel_id=1, source_target_pairs={{0,18},{1,19},{2,16},{3,17},{16,2},{17,3},{18,0},{19,1},{4,22},{5,... | collective-permute-start | bytes 1572872 | tf_op jit(solution)/shard_map/ppermute | solution.py:297
  119.2 20.0 %collective-permute-start.33 = (f32[256,512]{1,0:T(8,128)S(1)}, f32[256,512]{1,0:T(8,128)S(1)}, u32[]{:S(2)}, u32[]{:S(2)}) collective-permute-start(f32[256,512]{1,0:T(8,128)S(1)} %get-tuple-element.43), channel_id=1, source_target_pairs={{0,1},{1,0},{2,3},{3,2},{4,5},{5,4},{6,7},{7,6},{8,9},{9,8},{10,11... | collective-permute-start | bytes 1572872 | tf_op jit(solution)/shard_map/ppermute | solution.py:458
  119.3 20.9 %collective-permute-start.34 = (f32[256,512]{1,0:T(8,128)S(1)}, f32[256,512]{1,0:T(8,128)S(1)}, u32[]{:S(2)}, u32[]{:S(2)}) collective-permute-start(f32[256,512]{1,0:T(8,128)S(1)} %get-tuple-element.44), channel_id=1, source_target_pairs={{0,2},{1,3},{2,0},{3,1},{4,6},{5,7},{6,4},{7,5},{8,10},{9,11},{10,... | collective-permute-start | bytes 1572872 | tf_op jit(solution)/shard_map/ppermute | solution.py:458
  120.5 24.6 %collective-permute-start.35 = (f32[256,512]{1,0:T(8,128)S(1)}, f32[256,512]{1,0:T(8,128)S(1)}, u32[]{:S(2)}, u32[]{:S(2)}) collective-permute-start(f32[256,512]{1,0:T(8,128)S(1)} %get-tuple-element.45), channel_id=1, source_target_pairs={{0,3},{1,2},{2,1},{3,0},{4,7},{5,6},{6,5},{7,4},{8,11},{9,10},{10,... | collective-permute-start | bytes 1572872 | tf_op jit(solution)/shard_map/ppermute | solution.py:458
  121.3 13.6 %collective-permute-start.25 = (bf16[2,256,256]{2,1,0:T(8,128)(2,1)S(1)}, bf16[2,256,256]{2,1,0:T(8,128)(2,1)S(1)}, u32[]{:S(2)}, u32[]{:S(2)}) collective-permute-start(bf16[2,256,256]{2,1,0:T(8,128)(2,1)S(1)} %get-tuple-element.35.refs_2_.refs_1_), channel_id=1, source_target_pairs={{0,12},{4,8},{8,4},{12,0},{1,13},{5,9},{9,5},{13,1},{2,14},{6,10},... | collective-permute-start | bytes 786440 | tf_op jit(solution)/shard_map/ppermute | solution.py:276
  123.0 15.5 %collective-permute-start.20 = (bf16[384,256]{1,0:T(8,128)(2,1)S(1)}, bf16[384,256]{1,0:T(8,128)(2,1)S(1)}, u32[]{:S(2)}, u32[]{:S(2)}) collective-permute-start(bf16[384,256]{1,0:T(8,128)(2,1)S(1)} %get-tuple-element.32), channel_id=1, source_target_pairs={{0,4},{4,0},{8,12},{12,8},{1,5},{5,1},{9,13},{13,9},{2,6},{6,2},{1... | collective-permute-start | bytes 589832 | tf_op jit(solution)/shard_map/ppermute | solution.py:276
  135.0 12.1 %collective-permute-start.21 = (bf16[384,256]{1,0:T(8,128)(2,1)S(1)}, bf16[384,256]{1,0:T(8,128)(2,1)S(1)}, u32[]{:S(2)}, u32[]{:S(2)}) collective-permute-start(bf16[384,256]{1,0:T(8,128)(2,1)S(1)} %get-tuple-element.33), channel_id=1, source_target_pairs={{0,8},{4,12},{8,0},{12,4},{1,9},{5,13},{9,1},{13,5},{2,10},{6,14},... | collective-permute-start | bytes 589832 | tf_op jit(solution)/shard_map/ppermute | solution.py:276
  138.5 14.4 %collective-permute-start.22 = (bf16[384,256]{1,0:T(8,128)(2,1)S(1)}, bf16[384,256]{1,0:T(8,128)(2,1)S(1)}, u32[]{:S(2)}, u32[]{:S(2)}) collective-permute-start(bf16[384,256]{1,0:T(8,128)(2,1)S(1)} %get-tuple-element.34), channel_id=1, source_target_pairs={{0,12},{4,8},{8,4},{12,0},{1,13},{5,9},{9,5},{13,1},{2,14},{6,10},... | collective-permute-start | bytes 589832 | tf_op jit(solution)/shard_map/ppermute | solution.py:276
  139.2 15.2 %collective-permute-start.30 = (f32[96,512]{1,0:T(8,128)S(1)}, f32[96,512]{1,0:T(8,128)S(1)}, u32[]{:S(2)}, u32[]{:S(2)}) collective-permute-start(f32[96,512]{1,0:T(8,128)S(1)} %get-tuple-element.40), channel_id=1, source_target_pairs={{0,1},{1,0},{2,3},{3,2},{4,5},{5,4},{6,7},{7,6},{8,9},{9,8},{10,11... | collective-permute-start | bytes 589832 | tf_op jit(solution)/shard_map/ppermute | solution.py:503
  140.2 14.2 %collective-permute-start.31 = (f32[96,512]{1,0:T(8,128)S(1)}, f32[96,512]{1,0:T(8,128)S(1)}, u32[]{:S(2)}, u32[]{:S(2)}) collective-permute-start(f32[96,512]{1,0:T(8,128)S(1)} %get-tuple-element.41), channel_id=1, source_target_pairs={{0,2},{1,3},{2,0},{3,1},{4,6},{5,7},{6,4},{7,5},{8,10},{9,11},{10,... | collective-permute-start | bytes 589832 | tf_op jit(solution)/shard_map/ppermute | solution.py:503
  (20 other events, 164.6 us)

commit v5 on v2

--- a/solution.py
+++ b/solution.py
@@ -39,18 +39,6 @@
     )(*args, *after)
 
 
-def gate(arrays, after, name):
-    return pl.pallas_call(
-        lambda *refs: None,
-        out_shape=[shape(a.shape, a.dtype) for a in arrays],
-        in_specs=[pl.BlockSpec(memory_space=pl.ANY)] * (len(arrays) + len(after)),
-        out_specs=[pl.BlockSpec(memory_space=pl.ANY)] * len(arrays),
-        input_output_aliases={k: k for k in range(len(arrays))},
-        cost_estimate=pl.CostEstimate(flops=1, bytes_accessed=1, transcendentals=0),
-        name=name,
-    )(*arrays, *after)
-
-
 def shape(dims, dtype):
     return jax.ShapeDtypeStruct(dims, dtype)
 
@@ -66,14 +54,6 @@
     col = pl.multiple_of((idx[0] ^ k) * own, own)
     out[0] = q[:, pl.ds(col, own)]
     out[1] = g[:, pl.ds(col, own)]
-
-
-def join_ends_body(idx, mine, side, near, far, out):
-    inner = (idx[0] == 1) | (idx[0] == 2)
-    out[0] = mine[...]
-    out[1] = side[...]
-    for a in range(2):
-        out[2 + a] = pick(inner, near[1 - a], far[a])
 
 
 def join_body(idx, *rest):
@@ -121,45 +101,50 @@
         out[...] = total.astype(BF)
 
 
-def attention_body(heads, first, last, idx, keys, values, qg, *rest):
-    if first:
-        query_grad, acc = rest
-    else:
-        before, query_grad, acc = rest
-    q, g, kk, vv = qg[0], qg[1], keys[...], values[...]
+def attention_body(n, half, idx, keys, values, *rest):
+    pairs, outs, (out, q_all, g_all, p_all, ds_all) = rest[:n], rest[n : 2 * n], rest[2 * n :]
+    rows = pairs[0].shape[1]
+    width = out.shape[2]
+    cols = slice(half * width, (half + 1) * width)
+    kk, vv = keys[:, cols], values[:, cols]
+    for k in range(n):
+        q_all[k * rows : (k + 1) * rows, :] = pairs[k][0, :, cols]
+        g_all[k * rows : (k + 1) * rows, :] = pairs[k][1, :, cols]
     scale = DH**-0.5
     lane = lax.broadcasted_iota(jnp.int32, kk.shape, 1)
-    grad_q = key_part = value_part = None
-    for h in range(heads):
+    grad_q = [None] * n
+    key_part = value_part = None
+    for h in range(width // DH):
         mask = (lane >= h * DH) & (lane < (h + 1) * DH)
         k_h = jnp.where(mask, kk, jnp.zeros_like(kk))
         v_h = jnp.where(mask, vv, jnp.zeros_like(vv))
-        scores = dot(k_h, q, 1, 1)
-        e = jnp.exp((scores - jnp.max(scores, axis=0, keepdims=True)) * scale)
-        p = e * (1.0 / jnp.sum(e, axis=0, keepdims=True))
-        dp = dot(v_h, g, 1, 1)
-        delta = jnp.sum(p * dp, axis=0, keepdims=True)
-        ds = (p * (dp - delta) * scale).astype(BF)
-        term_q = dot(ds, k_h, 0, 0)
-        term_k = jnp.where(mask, dot(ds, q, 1, 0), 0.0)
-        term_v = jnp.where(mask, dot(p.astype(BF), g, 1, 0), 0.0)
-        grad_q = term_q if h == 0 else grad_q + term_q
+        for k in range(n):
+            block = slice(k * rows, (k + 1) * rows)
+            scores = dot(k_h, q_all[block, :], 1, 1)
+            e = jnp.exp((scores - jnp.max(scores, axis=0, keepdims=True)) * scale)
+            p = e * (1.0 / jnp.sum(e, axis=0, keepdims=True))
+            dp = dot(v_h, g_all[block, :], 1, 1)
+            delta = jnp.sum(p * dp, axis=0, keepdims=True)
+            ds = (p * (dp - delta) * scale).astype(BF)
+            p_all[:, block] = p.astype(BF)
+            ds_all[:, block] = ds
+            term = dot(ds, k_h, 0, 0)
+            grad_q[k] = term if h == 0 else grad_q[k] + term
+        term_k = jnp.where(mask, dot(ds_all[...], q_all[...], 1, 0), 0.0)
+        term_v = jnp.where(mask, dot(p_all[...], g_all[...], 1, 0), 0.0)
         key_part = term_k if h == 0 else key_part + term_k
         value_part = term_v if h == 0 else value_part + term_v
-    query_grad[...] = grad_q.astype(BF)
-    if not first:
-        key_part = key_part + before[0]
-        value_part = value_part + before[1]
-    acc[0] = key_part.astype(acc.dtype)
-    acc[1] = value_part.astype(acc.dtype)
-
-
-def weight_body(own, idx, whole, grad, keep, send):
-    for out, core in ((keep, 0), (send, 1)):
-        for a in range(2):
-            k = (idx[1] ^ (core + 2 * a)) ^ idx[0]
-            for s in range(2):
-                out[a, :, s * own : (s + 1) * own] = dot(whole[k, s * KP : (s + 1) * KP, :], grad[s], 0, 0)
+    for k in range(n):
+        outs[k][...] = grad_q[k].astype(BF)
+    out[0] = key_part.astype(BF)
+    out[1] = value_part.astype(BF)
+
+
+def weight_body(own, idx, whole, grad, *outs):
+    for a, out in enumerate(outs):
+        k = (idx[1] ^ a) ^ idx[0]
+        for s in range(2):
+            out[:, s * own : (s + 1) * own] = dot(whole[k, s * KP : (s + 1) * KP, :], grad[s], 0, 0)
 
 
 def arrange_body(own, idx, w_own, w_core, out):
@@ -173,23 +158,36 @@
 
 
 def tail_body(nd, idx, *rest):
-    grads, (w, e, x, input_grad, length_terms, cg) = rest[:4], rest[4:]
+    length_terms, (input_grad, cg, terms) = rest[-3 - nd : -3], rest[-3:]
+    grads, (w, e, x) = rest[: -6 - nd], rest[-6 - nd : -3 - nd]
     for s in range(2):
         grad = jnp.concatenate([part[s] for part in grads], axis=1)
         cg[s * KP : (s + 1) * KP, :] = dot(grad, w[s], 1, 1).astype(BF)
     both = cg[...]
-    terms = dot(x[...], both, 1, 1)
+    terms[...] = dot(x[...], both, 1, 1)
     rows = x.shape[0] // nd
     for a in range(nd):
-        length_terms[idx[1] ^ a] = terms[a * rows : (a + 1) * rows, :]
+        length_terms[a][...] = terms[pl.ds(pl.multiple_of((idx[1] ^ a) * rows, 16), rows), :]
     input_grad[...] = dot(e[...], both, 1, 0).astype(BF)
 
 
+def sum_body(idx, *rest):
+    out = rest[-1]
+    total = rest[0][...]
+    for x in rest[1:-1]:
+        total = total + x[...]
+    for s in range(2):
+        out[:, s, :] = total[:, s * KP : (s + 1) * KP]
+
+
 def place_body(n, own, idx, *rest):
-    out = rest[n]
+    out = rest[-1]
+    parts = (len(rest) - 1) // n
+    width = own // parts
     for k in range(n):
         col = pl.multiple_of((idx[0] ^ k) * own, own)
-        out[:, pl.ds(col, own)] = rest[k][...]
+        for a in range(parts):
+            out[:, pl.ds(col + a * width, width)] = rest[k * parts + a][: out.shape[0], :]
 
 
 def by_heads(ng, n, nd, inputs, queries, cotangent, length_proj, key_value_weight):
@@ -208,11 +206,10 @@
     def to_line(x, k):
         return lax.ppermute(x, "ctx", swap(n, k))
 
-    def over_line(x):
+    def over_line(x, after):
         side = to_line(x, 1)
-        near = jnp.stack(
-            [lax.ppermute(x, "ctx", [(1, 2), (2, 1)]), lax.ppermute(x, "ctx", [(0, 2), (3, 1)])]
-        )
+        near = [lax.ppermute(x, "ctx", [(1, 2), (2, 1)]), lax.ppermute(x, "ctx", [(0, 2), (3, 1)])]
+        near = call(join_body, [shape((2, *x.shape), BF)], [idx, *near], after, name="join_near")[0]
         far = lax.ppermute(near, "ctx", [(1, 0), (2, 3)])
         return x, side, near, far
 
@@ -228,11 +225,6 @@
     def over_cores(x):
         return lax.ppermute(x, "dp", swap(nd, 1))
 
-    def join_ends(parts, after, name):
-        return call(
-            join_ends_body, [shape((n, *parts[0].shape), BF)], [idx, *parts], after, name=name
-        )[0]
-
     def pack_queries(k, after):
         return call(
             functools.partial(pack_pair_body, own, k),
@@ -250,99 +242,97 @@
     pieces = [piece] + [to_line(piece, k) for k in range(1, n)]
     blocks = [blocks[0]] + [to_line(blocks[k], k) for k in range(1, n)]
     line = call(
-        join_body, [shape((n, part, 2 * KP), BF)], [idx, *pieces], [blocks[1]], name="join_pieces"
+        join_body, [shape((n, part, 2 * KP), BF)], [idx, *pieces], name="join_pieces"
     )[0]
     across = over_plane(line)
-    packed3 = pack_queries(3, [line])
+    packed = [pack_queries(k, [line]) for k in range(n)]
     e_own = call(
-        join_body, [shape((n, n, part, 2 * KP), BF)], [idx, *across], [*blocks[2:], packed3], name="join_lines"
-    )[0]
-    packed2 = pack_queries(2, [e_own])
+        join_body,
+        [shape((n, n, part, 2 * KP), BF)],
+        [idx, *across],
+        [*blocks[2:], *packed],
+        name="join_lines",
+    )[0]
     e_core = over_cores(e_own)
     w = key_value_weight.reshape(width, 2 * own)
+    w_rows = width // plane
     compressed = call(
         functools.partial(compress_body, n, plane, rows),
         [shape((2 * KP, own), BF)],
         [idx, e_own, e_core, *blocks],
-        [packed2],
+        packed[1:],
         [pltpu.VMEM((n * rows, 2 * KP), BF)],
         name="compress",
     )[0]
-    parts = over_line(compressed)
-
-    packed1 = pack_queries(1, [parts[2]])
-    qg = [pack_queries(0, []), to_line(packed1, 1), to_line(packed2, 2), to_line(packed3, 3)]
-    w_piece = call(
-        slice_body, [shape((width // plane, 2 * own), BF)], [idx, w], [parts[1]], name="slice_weight"
-    )[0]
-    w_line = join_ends(over_line(w_piece), [], "join_weight")
+    qg = [packed[0]] + [to_line(packed[k], k) for k in range(1, n)]
+    parts = over_line(compressed, [qg[1]])
+
+    w_piece = call(slice_body, [shape((w_rows, 2 * own), BF)], [idx, w], [parts[1]], name="slice_weight")[0]
+    w_parts = [w_piece] + [to_line(w_piece, k) for k in range(1, n)]
+    w_line = call(join_body, [shape((n, w_rows, 2 * own), BF)], [idx, *w_parts], name="join_weight")[0]
     keys, values, whole = call(
         functools.partial(project_body, own),
         [shape((KP, own), BF)] * 2 + [shape((n, 2 * KP, own), BF)],
         [idx, *parts, w],
-        [qg[2], packed1, w_line],
+        [qg[2], packed[1], w_line],
         name="project",
     )
 
-    heads = own // DH
-    query_grads, acc = {}, None
-    order = (0, 2, 3, 1)
-    for k in order:
-        first, last = k == order[0], k == order[-1]
-        query_grads[k], acc = call(
-            functools.partial(attention_body, heads, first, last),
-            [shape((rows, own), BF), shape((2, KP, own), BF if last else F32)],
-            [idx, keys, values, qg[k]] + ([] if first else [acc]),
-            name="attention",
-        )
+    *query_grads, acc = call(
+        functools.partial(attention_body, n, 0),
+        [shape((rows, own), BF)] * n + [shape((2, KP, own), BF)],
+        [idx, keys, values, *qg],
+        scratch=[pltpu.VMEM((n * rows, own), BF)] * 2 + [pltpu.VMEM((KP, n * rows), BF)] * 2,
+        name="attention",
+    )
     grads = [acc] + [to_line(acc, k) for k in range(1, n)]
 
-    keep, send = call(
+    weight = call(
         functools.partial(weight_body, own),
-        [shape((2, width // nd, 2 * own), F32)] * 2,
+        [shape((width // nd, 2 * own), F32)] * nd,
         [idx, whole, acc],
         name="weight",
     )
+    keep = weight[0]
+    weight = [keep] + [lax.ppermute(weight[a], "dp", swap(nd, a)) for a in range(1, nd)]
+
     w_across = over_plane(w_line)
     w_own = call(
-        join_body, [shape((n, n, width // plane, 2 * own), BF)], [idx, *w_across], [keep, grads[1], grads[2]], name="join_weights"
+        join_body,
+        [shape((n, n, w_rows, 2 * own), BF)],
+        [idx, *w_across],
+        [keep, grads[1], grads[2]],
+        name="join_weights",
     )[0]
     w_core = over_cores(w_own)
     w_all = call(
         functools.partial(arrange_body, own),
         [shape((2, width, width), BF)],
         [idx, w_own, w_core],
-        [grads[2]],
+        [keep, grads[1]],
         name="arrange_weight",
     )[0]
 
-    pair = keep + lax.ppermute(send, "dp", swap(nd, 1))
-    weight_grad = pair[0] + lax.ppermute(pair[1], "dp", swap(nd, 2))
-    weight_grad = weight_grad.reshape(-1, 2, own)
-
-    late = gate([query_grads[k] for k in range(1, n)], [grads[2]], "hold_query_grads")
-    returned = [query_grads[0]] + [to_line(late[k - 1], k) for k in range(1, n)]
-
-    input_grad, terms = call(
+    returned = [query_grads[0]] + [to_line(query_grads[k], k) for k in range(1, n)]
+
+    tail_in = [idx, *grads, w_all, length_proj.reshape(rows, 2 * KP), tokens]
+    *terms, input_grad = call(
         functools.partial(tail_body, nd),
-        [shape((rows, width), BF), shape((nd, rows // nd, 2 * KP), F32)],
-        [idx, *grads, w_all, length_proj.reshape(rows, 2 * KP), tokens],
-        [],
-        [pltpu.VMEM((2 * KP, width), BF)],
+        [shape((rows // nd, 2 * KP), F32)] * nd + [shape((rows, width), BF)],
+        tail_in,
+        scratch=[pltpu.VMEM((2 * KP, width), BF), pltpu.VMEM((rows, 2 * KP), F32)],
         name="tail",
     )
-    length_grad = terms[0]
-    for a in range(1, nd):
-        length_grad = length_grad + lax.ppermute(terms[a], "dp", swap(nd, a))
-    length_grad = length_grad.reshape(-1, 2, KP)
-
+    terms = [terms[0]] + [lax.ppermute(terms[a], "dp", swap(nd, a)) for a in range(1, nd)]
     query_grad = call(
         functools.partial(place_body, n, own),
         [shape((rows, width), BF)],
         [idx, *returned],
-        [terms],
+        [terms[0]],
         name="place",
     )[0]
+    length_grad = call(sum_body, [shape((rows // nd, 2, KP), F32)], [idx, *terms], name="sum_terms")[0]
+    weight_grad = call(sum_body, [shape((width // nd, 2, own), F32)], [idx, *weight], name="sum_weight")[0]
     return query_grad[None], input_grad[None], length_grad, weight_grad
 
 

time: 165 us -> 157 us (0.952)
  starting transfers between devices: 50.3 us -> 39.1 us
  waiting for transfers between devices: 75.1 us -> 83.7 us
  local copies, waits for them, and re-layouts: 7.31 us -> 4.63 us
    ppermute x17 -> x19, waiting for transfers between devices: 54 us -> 74.4 us  [to_line(): return lax.ppermute(x, 'ctx', swap(n, k))]
    ppermute x2 -> x1, waiting for transfers between devices: 8.42 us -> 0.01 us  [over_line(): lax.ppermute(x, 'ctx', [(0, 2), (3, 1)])]
    ppermute x2, starting transfers between devices: 9.81 us -> 4.59 us  [over_cores(): return lax.ppermute(x, 'dp', swap(nd, 1))]
    ppermute x2 -> x1, starting transfers between devices: 5.36 us -> 2.73 us  [over_line(): lax.ppermute(x, 'ctx', [(1, 2), (2, 1)])]
    reshape x2 -> x0, local copies, waits for them, and re-layouts: 1.92 us -> none  [the longest x1 1.12 us: by_heads(): weight_grad = weight_grad.reshape(-1, 2, own)]
    ppermute x2 -> x1, waiting for transfers between devices: 6.31 us -> 4.62 us  [over_line(): lax.ppermute(x, 'ctx', [(1, 2), (2, 1)])]
    ppermute x5 -> x6, waiting for transfers between devices: 5.07 us -> 3.65 us  [the longest x3 3.64 us: by_heads(): lax.ppermute(weight[a], 'dp', swap(nd, a))]
    ppermute x5 -> x6, starting transfers between devices: 5.6 us -> 4.42 us  [the longest x3 2.28 us: by_heads(): lax.ppermute(terms[a], 'dp', swap(nd, a))]
  transfers between devices with their start and end apart: 36 -> 36, of which waited for: 16 -> 16; matrix products, arithmetic and copies ran while one was open for 3% -> 0% of each run, Pallas kernels for 15% -> 16%
where the time goes in v5:
time: 157 us; the launch traced here: 156 us
  waiting for transfers between devices  83.7 us (53%)
  starting transfers between devices  39.1 us (25%)
  Pallas kernels  27.2 us (17%)
  local copies, waits for them, and re-layouts  4.63 us (3%)
    ppermute x19, waiting for transfers between devices, to_line(): return lax.ppermute(x, 'ctx', swap(n, k))  74.4 us
    pallas_call x20, Pallas kernels, call(): pl.pallas_call(run, out_shape=outs, in_specs=[pl.BlockSpec(memory_space=p...  27.2 us
    ppermute x19, starting transfers between devices, to_line(): return lax.ppermute(x, 'ctx', swap(n, k))  19.1 us
    ppermute x6, starting transfers between devices, over_plane(): across.append(lax.ppermute(x, ('groups', 'dp'), perm))  5.43 us
    ppermute x1, waiting for transfers between devices, over_line(): lax.ppermute(x, 'ctx', [(1, 2), (2, 1)])  4.62 us
    ppermute x2, starting transfers between devices, over_cores(): return lax.ppermute(x, 'dp', swap(nd, 1))  4.59 us
    unnamed x15, local copies, waits for them, and re-layouts  3.71 us
    ppermute x3, waiting for transfers between devices, by_heads(): lax.ppermute(weight[a], 'dp', swap(nd, a))  3.64 us
  transfers between devices with their start and end apart: 36, of which 16 were waited for; matrix products, arithmetic and copies ran while one was open for 0% of the time, Pallas kernels for 16%

profile of v5, /device:TPU:9, one launch (start us, length us, event | category | flops | bytes accessed | tf_op | source)
XLA Modules:
  0.0 155.6 jit_solution(5597610635930023305)
XLA Ops:
  1.6 2.5 %collective-permute-start.1 = (bf16[48,512]{1,0:T(8,128)(2,1)S(1)}, bf16[48,512]{1,0:T(8,128)(2,1)S(1)}, u32[]{:S(2)}, u32[]{:S(2)}) collective-permute-start(bf16[48,512]{1,0:T(8,128)(2,1)S(1)} %bitcast.31), channel_id=1, source_target_pairs={{0,8},{4,12},{8,0},{12,4},{1,9},{5,13},{9,1},{13,5},{2,10},{6,14},... | collective-permute-start | bytes 147464 | tf_op jit(solution)/shard_map/ppermute | solution.py:207
  6.1 3.3 %collective-permute-start.6 = (bf16[384,256]{1,0:T(8,128)(2,1)S(1)}, bf16[384,256]{1,0:T(8,128)(2,1)S(1)}, u32[]{:S(2)}, u32[]{:S(2)}) collective-permute-start(bf16[384,256]{1,0:T(8,128)(2,1)S(1)} %get-tuple-element.25), channel_id=1, source_target_pairs={{0,8},{4,12},{8,0},{12,4},{1,9},{5,13},{9,1},{13,5},{2,10},{6,14},... | collective-permute-start | bytes 589832 | tf_op jit(solution)/shard_map/ppermute | solution.py:207
  17.4 4.0 %collective-permute-done.6.refs_5_ = bf16[384,256]{1,0:T(8,128)(2,1)S(1)} collective-permute-done((bf16[384,256]{1,0:T(8,128)(2,1)S(1)}, bf16[384,256]{1,0:T(8,128)(2,1)S(1)}, u32[]{:S(2)}, u32[]{:S(2)}) %collective-permute-start.6) | collective-permute-done | bytes 196640 | tf_op jit(solution)/shard_map/ppermute | solution.py:207
  21.4 4.9 %collective-permute-done.7.refs_6_ = bf16[384,256]{1,0:T(8,128)(2,1)S(1)} collective-permute-done((bf16[384,256]{1,0:T(8,128)(2,1)S(1)}, bf16[384,256]{1,0:T(8,128)(2,1)S(1)}, u32[]{:S(2)}, u32[]{:S(2)}) %collective-permute-start.7) | collective-permute-done | bytes 196640 | tf_op jit(solution)/shard_map/ppermute | solution.py:207
  29.7 5.0 %collective-permute-done.9.refs_4_ = bf16[384,256]{1,0:T(8,128)(2,1)S(1)} collective-permute-done((bf16[384,256]{1,0:T(8,128)(2,1)S(1)}, bf16[384,256]{1,0:T(8,128)(2,1)S(1)}, u32[]{:S(2)}, u32[]{:S(2)}) %collective-permute-start.9) | collective-permute-done | bytes 196640 | tf_op jit(solution)/shard_map/ppermute | solution.py:207
  36.1 2.7 %collective-permute-start.11 = (bf16[512,256]{1,0:T(8,128)(2,1)S(1)}, bf16[512,256]{1,0:T(8,128)(2,1)S(1)}, u32[]{:S(2)}, u32[]{:S(2)}) collective-permute-start(bf16[512,256]{1,0:T(8,128)(2,1)S(1)} %compress.1.refs_1_), channel_id=1, source_target_pairs={{4,8},{8,4},{5,9},{9,5},{6,10},{10,6},{7,11},{11,7},{20,24},{24,20... | collective-permute-start | bytes 786440 | tf_op jit(solution)/shard_map/ppermute | solution.py:211
  40.1 2.5 %collective-permute-start.10 = (bf16[512,256]{1,0:T(8,128)(2,1)S(1)}, bf16[512,256]{1,0:T(8,128)(2,1)S(1)}, u32[]{:S(2)}, u32[]{:S(2)}) collective-permute-start(bf16[512,256]{1,0:T(8,128)(2,1)S(1)} %compress.1.refs_1_), channel_id=1, source_target_pairs={{0,4},{4,0},{8,12},{12,8},{1,5},{5,1},{9,13},{13,9},{2,6},{6,2},{1... | collective-permute-start | bytes 786440 | tf_op jit(solution)/shard_map/ppermute | solution.py:207
  43.5 4.6 %collective-permute-done.11.refs_1_ = bf16[512,256]{1,0:T(8,128)(2,1)S(1)} collective-permute-done((bf16[512,256]{1,0:T(8,128)(2,1)S(1)}, bf16[512,256]{1,0:T(8,128)(2,1)S(1)}, u32[]{:S(2)}, u32[]{:S(2)}) %collective-permute-start.11) | collective-permute-done | bytes 262176 | tf_op jit(solution)/shard_map/ppermute | solution.py:211
  50.2 2.8 %collective-permute-done.10.refs_2_ = bf16[512,256]{1,0:T(8,128)(2,1)S(1)} collective-permute-done((bf16[512,256]{1,0:T(8,128)(2,1)S(1)}, bf16[512,256]{1,0:T(8,128)(2,1)S(1)}, u32[]{:S(2)}, u32[]{:S(2)}) %collective-permute-start.10) | collective-permute-done | bytes 262176 | tf_op jit(solution)/shard_map/ppermute | solution.py:207
  53.6 2.0 %collective-permute-start.17 = (bf16[128,512]{1,0:T(8,128)(2,1)S(1)}, bf16[128,512]{1,0:T(8,128)(2,1)S(1)}, u32[]{:S(2)}, u32[]{:S(2)}) collective-permute-start(bf16[128,512]{1,0:T(8,128)(2,1)S(1)} %slice_weight.1.refs_1_), channel_id=1, source_target_pairs={{0,8},{4,12},{8,0},{12,4},{1,9},{5,13},{9,1},{13,5},{2,10},{6,14},... | collective-permute-start | bytes 393224 | tf_op jit(solution)/shard_map/ppermute | solution.py:207
  56.2 9.1 %collective-permute-done.16.refs_2_ = bf16[128,512]{1,0:T(8,128)(2,1)S(1)} collective-permute-done((bf16[128,512]{1,0:T(8,128)(2,1)S(1)}, bf16[128,512]{1,0:T(8,128)(2,1)S(1)}, u32[]{:S(2)}, u32[]{:S(2)}) %collective-permute-start.16) | collective-permute-done | bytes 131104 | tf_op jit(solution)/shard_map/ppermute | solution.py:207
  66.0 12.3 %collective-permute-done.17.refs_3_ = bf16[128,512]{1,0:T(8,128)(2,1)S(1)} collective-permute-done((bf16[128,512]{1,0:T(8,128)(2,1)S(1)}, bf16[128,512]{1,0:T(8,128)(2,1)S(1)}, u32[]{:S(2)}, u32[]{:S(2)}) %collective-permute-start.17) | collective-permute-done | bytes 131104 | tf_op jit(solution)/shard_map/ppermute | solution.py:207
  78.3 3.9 %collective-permute-done.18.refs_4_ = bf16[128,512]{1,0:T(8,128)(2,1)S(1)} collective-permute-done((bf16[128,512]{1,0:T(8,128)(2,1)S(1)}, bf16[128,512]{1,0:T(8,128)(2,1)S(1)}, u32[]{:S(2)}, u32[]{:S(2)}) %collective-permute-start.18) | collective-permute-done | bytes 131104 | tf_op jit(solution)/shard_map/ppermute | solution.py:207
  86.5 8.6 %collective-permute-done.19.refs_6_ = bf16[2,384,256]{2,1,0:T(8,128)(2,1)S(1)} collective-permute-done((bf16[2,384,256]{2,1,0:T(8,128)(2,1)S(1)}, bf16[2,384,256]{2,1,0:T(8,128)(2,1)S(1)}, u32[]{:S(2)}, u32[]{:S(2)}) %collective-permute-start.19) | collective-permute-done | bytes 393248 | tf_op jit(solution)/shard_map/ppermute | solution.py:207
  95.1 8.3 %attention.1 = (bf16[384,256]{1,0:T(8,128)(2,1)S(1)}, bf16[384,256]{1,0:T(8,128)(2,1)S(1)}, bf16[384,256]{1,0:T(8,128)(2,1)S(1)}, bf16[384,256]{1,0:T(8,128)(2,1)S(1)}, bf16[2,256,256]{2,1,0:T(8,128)(2,1)S(1)}) custom-call(s32[6]{0:T(128)S(1)} %stack.27.refs_0_, bf16[256,256]{1,0:T(8,128)(2,1)S(1)} %get-tuple-element.29.refs_1_, ...), custom_call_target="tpu_custom_call" | custom-call | flops 1 | bytes 1 | tf_op jit(solution)/shard_map/attention/pallas_call | solution.py:28
  103.5 2.0 %collective-permute-start.24 = (bf16[2,256,256]{2,1,0:T(8,128)(2,1)S(1)}, bf16[2,256,256]{2,1,0:T(8,128)(2,1)S(1)}, u32[]{:S(2)}, u32[]{:S(2)}) collective-permute-start(bf16[2,256,256]{2,1,0:T(8,128)(2,1)S(1)} %get-tuple-element.35.refs_2_.refs_1_), channel_id=1, source_target_pairs={{0,8},{4,12},{8,0},{12,4},{1,9},{5,13},{9,1},{13,5},{2,10},{6,14},... | collective-permute-start | bytes 786440 | tf_op jit(solution)/shard_map/ppermute | solution.py:207
  106.5 3.0 %collective-permute-done.23.refs_6_.refs_4_.refs_2_ = bf16[2,256,256]{2,1,0:T(8,128)(2,1)S(1)} collective-permute-done((bf16[2,256,256]{2,1,0:T(8,128)(2,1)S(1)}, bf16[2,256,256]{2,1,0:T(8,128)(2,1)S(1)}, u32[]{:S(2)}, u32[]{:S(2)}) %collective-permute-start.23) | collective-permute-done | bytes 262176 | tf_op jit(solution)/shard_map/ppermute | solution.py:207
  109.6 5.6 %collective-permute-done.24.refs_7_.refs_3_ = bf16[2,256,256]{2,1,0:T(8,128)(2,1)S(1)} collective-permute-done((bf16[2,256,256]{2,1,0:T(8,128)(2,1)S(1)}, bf16[2,256,256]{2,1,0:T(8,128)(2,1)S(1)}, u32[]{:S(2)}, u32[]{:S(2)}) %collective-permute-start.24) | collective-permute-done | bytes 262176 | tf_op jit(solution)/shard_map/ppermute | solution.py:207
  115.9 3.3 %collective-permute-start.29 = (bf16[4,4,128,512]{3,2,1,0:T(8,128)(2,1)S(1)}, bf16[4,4,128,512]{3,2,1,0:T(8,128)(2,1)S(1)}, u32[]{:S(2)}, u32[]{:S(2)}) collective-permute-start(bf16[4,4,128,512]{3,2,1,0:T(8,128)(2,1)S(1)} %join_weights.1.refs_1_), channel_id=1, source_target_pairs={{0,1},{1,0},{2,3},{3,2},{4,5},{5,4},{6,7},{7,6},{8,9},{9,8},{10,11... | collective-permute-start | bytes 6291464 | tf_op jit(solution)/shard_map/ppermute | solution.py:226
  123.0 1.9 %collective-permute-start.20 = (bf16[384,256]{1,0:T(8,128)(2,1)S(1)}, bf16[384,256]{1,0:T(8,128)(2,1)S(1)}, u32[]{:S(2)}, u32[]{:S(2)}) collective-permute-start(bf16[384,256]{1,0:T(8,128)(2,1)S(1)} %get-tuple-element.32), channel_id=1, source_target_pairs={{0,4},{4,0},{8,12},{12,8},{1,5},{5,1},{9,13},{13,9},{2,6},{6,2},{1... | collective-permute-start | bytes 589832 | tf_op jit(solution)/shard_map/ppermute | solution.py:207
  126.0 9.0 %collective-permute-done.25.refs_4_ = bf16[2,256,256]{2,1,0:T(8,128)(2,1)S(1)} collective-permute-done((bf16[2,256,256]{2,1,0:T(8,128)(2,1)S(1)}, bf16[2,256,256]{2,1,0:T(8,128)(2,1)S(1)}, u32[]{:S(2)}, u32[]{:S(2)}) %collective-permute-start.25) | collective-permute-done | bytes 262176 | tf_op jit(solution)/shard_map/ppermute | solution.py:207
  135.0 3.6 %tail.1 = (f32[96,512]{1,0:T(8,128)S(1)}, f32[96,512]{1,0:T(8,128)S(1)}, f32[96,512]{1,0:T(8,128)S(1)}, f32[96,512]{1,0:T(8,128)S(1)}, bf16[384,1024]{1,0:T(8,128)(2,1)}) custom-call(s32[6]{0:T(128)S(1)} %stack.27.refs_0_, bf16[2,256,256]{2,1,0:T(8,128)(2,1)S(1)} %get-tuple-element.35.refs_2_.refs_1_, ...), custom_call_target="tpu_custom_call" | custom-call | flops 1 | bytes 1 | tf_op jit(solution)/shard_map/tail/pallas_call | solution.py:28
  141.4 3.6 %collective-permute-done.35.refs_4_ = f32[256,512]{1,0:T(8,128)S(1)} collective-permute-done((f32[256,512]{1,0:T(8,128)S(1)}, f32[256,512]{1,0:T(8,128)S(1)}, u32[]{:S(2)}, u32[]{:S(2)}) %collective-permute-start.35) | collective-permute-done | bytes 524320 | tf_op jit(solution)/shard_map/ppermute | solution.py:297
  147.1 5.7 %collective-permute-done.22.refs_4_ = bf16[384,256]{1,0:T(8,128)(2,1)S(1)} collective-permute-done((bf16[384,256]{1,0:T(8,128)(2,1)S(1)}, bf16[384,256]{1,0:T(8,128)(2,1)S(1)}, u32[]{:S(2)}, u32[]{:S(2)}) %collective-permute-start.22) | collective-permute-done | bytes 196640 | tf_op jit(solution)/shard_map/ppermute | solution.py:207
  (85 shorter events, 40.5 us)
Async XLA Ops:
  6.1 15.3 %collective-permute-start.6 = (bf16[384,256]{1,0:T(8,128)(2,1)S(1)}, bf16[384,256]{1,0:T(8,128)(2,1)S(1)}, u32[]{:S(2)}, u32[]{:S(2)}) collective-permute-start(bf16[384,256]{1,0:T(8,128)(2,1)S(1)} %get-tuple-element.25), channel_id=1, source_target_pairs={{0,8},{4,12},{8,0},{12,4},{1,9},{5,13},{9,1},{13,5},{2,10},{6,14},... | collective-permute-start | bytes 589832 | tf_op jit(solution)/shard_map/ppermute | solution.py:207
  9.4 16.9 %collective-permute-start.7 = (bf16[384,256]{1,0:T(8,128)(2,1)S(1)}, bf16[384,256]{1,0:T(8,128)(2,1)S(1)}, u32[]{:S(2)}, u32[]{:S(2)}) collective-permute-start(bf16[384,256]{1,0:T(8,128)(2,1)S(1)} %get-tuple-element.26), channel_id=1, source_target_pairs={{0,12},{4,8},{8,4},{12,0},{1,13},{5,9},{9,5},{13,1},{2,14},{6,10},... | collective-permute-start | bytes 589832 | tf_op jit(solution)/shard_map/ppermute | solution.py:207
  9.9 16.3 %collective-permute-start.3 = (bf16[4,48,512]{2,1,0:T(8,128)(2,1)S(1)}, bf16[4,48,512]{2,1,0:T(8,128)(2,1)S(1)}, u32[]{:S(2)}, u32[]{:S(2)}) collective-permute-start(bf16[4,48,512]{2,1,0:T(8,128)(2,1)S(1)} %join_pieces.1.refs_3_.refs_1_), channel_id=1, source_target_pairs={{0,2},{1,3},{2,0},{3,1},{16,18},{17,19},{18,16},{19,17},{4,6},{5,7... | collective-permute-start | bytes 589832 | tf_op jit(solution)/shard_map/ppermute | solution.py:222
  11.2 15.1 %collective-permute-start.4 = (bf16[4,48,512]{2,1,0:T(8,128)(2,1)S(1)}, bf16[4,48,512]{2,1,0:T(8,128)(2,1)S(1)}, u32[]{:S(2)}, u32[]{:S(2)}) collective-permute-start(bf16[4,48,512]{2,1,0:T(8,128)(2,1)S(1)} %join_pieces.1.refs_3_.refs_1_), channel_id=1, source_target_pairs={{0,16},{1,17},{2,18},{3,19},{16,0},{17,1},{18,2},{19,3},{4,20},{5,... | collective-permute-start | bytes 589832 | tf_op jit(solution)/shard_map/ppermute | solution.py:222
  12.5 13.8 %collective-permute-start.5 = (bf16[4,48,512]{2,1,0:T(8,128)(2,1)S(1)}, bf16[4,48,512]{2,1,0:T(8,128)(2,1)S(1)}, u32[]{:S(2)}, u32[]{:S(2)}) collective-permute-start(bf16[4,48,512]{2,1,0:T(8,128)(2,1)S(1)} %join_pieces.1.refs_3_.refs_1_), channel_id=1, source_target_pairs={{0,18},{1,19},{2,16},{3,17},{16,2},{17,3},{18,0},{19,1},{4,22},{5,... | collective-permute-start | bytes 589832 | tf_op jit(solution)/shard_map/ppermute | solution.py:222
  28.2 15.3 %collective-permute-start.13 = (bf16[2,384,256]{2,1,0:T(8,128)(2,1)S(1)}, bf16[2,384,256]{2,1,0:T(8,128)(2,1)S(1)}, u32[]{:S(2)}, u32[]{:S(2)}) collective-permute-start(bf16[2,384,256]{2,1,0:T(8,128)(2,1)S(1)} %pack_queries.5.refs_8_.refs_7_), channel_id=1, source_target_pairs={{0,4},{4,0},{8,12},{12,8},{1,5},{5,1},{9,13},{13,9},{2,6},{6,2},{1... | collective-permute-start | bytes 1179656 | tf_op jit(solution)/shard_map/ppermute | solution.py:207
  40.1 12.9 %collective-permute-start.10 = (bf16[512,256]{1,0:T(8,128)(2,1)S(1)}, bf16[512,256]{1,0:T(8,128)(2,1)S(1)}, u32[]{:S(2)}, u32[]{:S(2)}) collective-permute-start(bf16[512,256]{1,0:T(8,128)(2,1)S(1)} %compress.1.refs_1_), channel_id=1, source_target_pairs={{0,4},{4,0},{8,12},{12,8},{1,5},{5,1},{9,13},{13,9},{2,6},{6,2},{1... | collective-permute-start | bytes 786440 | tf_op jit(solution)/shard_map/ppermute | solution.py:207
  42.6 42.7 %collective-permute-start.15 = (bf16[2,384,256]{2,1,0:T(8,128)(2,1)S(1)}, bf16[2,384,256]{2,1,0:T(8,128)(2,1)S(1)}, u32[]{:S(2)}, u32[]{:S(2)}) collective-permute-start(bf16[2,384,256]{2,1,0:T(8,128)(2,1)S(1)} %pack_queries.6.refs_9_.refs_8_), channel_id=1, source_target_pairs={{0,8},{4,12},{8,0},{12,4},{1,9},{5,13},{9,1},{13,5},{2,10},{6,14},... | collective-permute-start | bytes 1179656 | tf_op jit(solution)/shard_map/ppermute | solution.py:207
  48.7 36.8 %collective-permute-start.14 = (bf16[2,512,256]{2,1,0:T(8,128)(2,1)S(1)}, bf16[2,512,256]{2,1,0:T(8,128)(2,1)S(1)}, u32[]{:S(2)}, u32[]{:S(2)}) collective-permute-start(bf16[2,512,256]{2,1,0:T(8,128)(2,1)S(1)} %join_near.1.refs_3_), channel_id=1, source_target_pairs={{4,0},{8,12},{5,1},{9,13},{6,2},{10,14},{7,3},{11,15},{20,16},{24,... | collective-permute-start | bytes 1572872 | tf_op jit(solution)/shard_map/ppermute | solution.py:213
  53.6 24.7 %collective-permute-start.17 = (bf16[128,512]{1,0:T(8,128)(2,1)S(1)}, bf16[128,512]{1,0:T(8,128)(2,1)S(1)}, u32[]{:S(2)}, u32[]{:S(2)}) collective-permute-start(bf16[128,512]{1,0:T(8,128)(2,1)S(1)} %slice_weight.1.refs_1_), channel_id=1, source_target_pairs={{0,8},{4,12},{8,0},{12,4},{1,9},{5,13},{9,1},{13,5},{2,10},{6,14},... | collective-permute-start | bytes 393224 | tf_op jit(solution)/shard_map/ppermute | solution.py:207
  55.6 26.5 %collective-permute-start.18 = (bf16[128,512]{1,0:T(8,128)(2,1)S(1)}, bf16[128,512]{1,0:T(8,128)(2,1)S(1)}, u32[]{:S(2)}, u32[]{:S(2)}) collective-permute-start(bf16[128,512]{1,0:T(8,128)(2,1)S(1)} %slice_weight.1.refs_1_), channel_id=1, source_target_pairs={{0,12},{4,8},{8,4},{12,0},{1,13},{5,9},{9,5},{13,1},{2,14},{6,10},... | collective-permute-start | bytes 393224 | tf_op jit(solution)/shard_map/ppermute | solution.py:207
  65.3 29.8 %collective-permute-start.19 = (bf16[2,384,256]{2,1,0:T(8,128)(2,1)S(1)}, bf16[2,384,256]{2,1,0:T(8,128)(2,1)S(1)}, u32[]{:S(2)}, u32[]{:S(2)}) collective-permute-start(bf16[2,384,256]{2,1,0:T(8,128)(2,1)S(1)} %pack_queries.7.refs_10_.refs_9_), channel_id=1, source_target_pairs={{0,12},{4,8},{8,4},{12,0},{1,13},{5,9},{9,5},{13,1},{2,14},{6,10},... | collective-permute-start | bytes 1179656 | tf_op jit(solution)/shard_map/ppermute | solution.py:207
  82.7 23.8 %collective-permute-start.26 = (bf16[4,128,512]{2,1,0:T(8,128)(2,1)S(1)}, bf16[4,128,512]{2,1,0:T(8,128)(2,1)S(1)}, u32[]{:S(2)}, u32[]{:S(2)}) collective-permute-start(bf16[4,128,512]{2,1,0:T(8,128)(2,1)S(1)} %join_weight.1.refs_8_.refs_1_), channel_id=1, source_target_pairs={{0,2},{1,3},{2,0},{3,1},{16,18},{17,19},{18,16},{19,17},{4,6},{5,7... | collective-permute-start | bytes 1572872 | tf_op jit(solution)/shard_map/ppermute | solution.py:222
  84.0 22.5 %collective-permute-start.27 = (bf16[4,128,512]{2,1,0:T(8,128)(2,1)S(1)}, bf16[4,128,512]{2,1,0:T(8,128)(2,1)S(1)}, u32[]{:S(2)}, u32[]{:S(2)}) collective-permute-start(bf16[4,128,512]{2,1,0:T(8,128)(2,1)S(1)} %join_weight.1.refs_8_.refs_1_), channel_id=1, source_target_pairs={{0,16},{1,17},{2,18},{3,19},{16,0},{17,1},{18,2},{19,3},{4,20},{5,... | collective-permute-start | bytes 1572872 | tf_op jit(solution)/shard_map/ppermute | solution.py:222
  85.3 21.3 %collective-permute-start.28 = (bf16[4,128,512]{2,1,0:T(8,128)(2,1)S(1)}, bf16[4,128,512]{2,1,0:T(8,128)(2,1)S(1)}, u32[]{:S(2)}, u32[]{:S(2)}) collective-permute-start(bf16[4,128,512]{2,1,0:T(8,128)(2,1)S(1)} %join_weight.1.refs_8_.refs_1_), channel_id=1, source_target_pairs={{0,18},{1,19},{2,16},{3,17},{16,2},{17,3},{18,0},{19,1},{4,22},{5,... | collective-permute-start | bytes 1572872 | tf_op jit(solution)/shard_map/ppermute | solution.py:222
  119.2 20.0 %collective-permute-start.33 = (f32[256,512]{1,0:T(8,128)S(1)}, f32[256,512]{1,0:T(8,128)S(1)}, u32[]{:S(2)}, u32[]{:S(2)}) collective-permute-start(f32[256,512]{1,0:T(8,128)S(1)} %get-tuple-element.43), channel_id=1, source_target_pairs={{0,1},{1,0},{2,3},{3,2},{4,5},{5,4},{6,7},{7,6},{8,9},{9,8},{10,11... | collective-permute-start | bytes 1572872 | tf_op jit(solution)/shard_map/ppermute | solution.py:297
  119.3 20.9 %collective-permute-start.34 = (f32[256,512]{1,0:T(8,128)S(1)}, f32[256,512]{1,0:T(8,128)S(1)}, u32[]{:S(2)}, u32[]{:S(2)}) collective-permute-start(f32[256,512]{1,0:T(8,128)S(1)} %get-tuple-element.44), channel_id=1, source_target_pairs={{0,2},{1,3},{2,0},{3,1},{4,6},{5,7},{6,4},{7,5},{8,10},{9,11},{10,... | collective-permute-start | bytes 1572872 | tf_op jit(solution)/shard_map/ppermute | solution.py:297
  120.5 24.5 %collective-permute-start.35 = (f32[256,512]{1,0:T(8,128)S(1)}, f32[256,512]{1,0:T(8,128)S(1)}, u32[]{:S(2)}, u32[]{:S(2)}) collective-permute-start(f32[256,512]{1,0:T(8,128)S(1)} %get-tuple-element.45), channel_id=1, source_target_pairs={{0,3},{1,2},{2,1},{3,0},{4,7},{5,6},{6,5},{7,4},{8,11},{9,10},{10,... | collective-permute-start | bytes 1572872 | tf_op jit(solution)/shard_map/ppermute | solution.py:297
  121.3 13.6 %collective-permute-start.25 = (bf16[2,256,256]{2,1,0:T(8,128)(2,1)S(1)}, bf16[2,256,256]{2,1,0:T(8,128)(2,1)S(1)}, u32[]{:S(2)}, u32[]{:S(2)}) collective-permute-start(bf16[2,256,256]{2,1,0:T(8,128)(2,1)S(1)} %get-tuple-element.35.refs_2_.refs_1_), channel_id=1, source_target_pairs={{0,12},{4,8},{8,4},{12,0},{1,13},{5,9},{9,5},{13,1},{2,14},{6,10},... | collective-permute-start | bytes 786440 | tf_op jit(solution)/shard_map/ppermute | solution.py:207
  123.0 15.5 %collective-permute-start.20 = (bf16[384,256]{1,0:T(8,128)(2,1)S(1)}, bf16[384,256]{1,0:T(8,128)(2,1)S(1)}, u32[]{:S(2)}, u32[]{:S(2)}) collective-permute-start(bf16[384,256]{1,0:T(8,128)(2,1)S(1)} %get-tuple-element.32), channel_id=1, source_target_pairs={{0,4},{4,0},{8,12},{12,8},{1,5},{5,1},{9,13},{13,9},{2,6},{6,2},{1... | collective-permute-start | bytes 589832 | tf_op jit(solution)/shard_map/ppermute | solution.py:207
  135.0 12.1 %collective-permute-start.21 = (bf16[384,256]{1,0:T(8,128)(2,1)S(1)}, bf16[384,256]{1,0:T(8,128)(2,1)S(1)}, u32[]{:S(2)}, u32[]{:S(2)}) collective-permute-start(bf16[384,256]{1,0:T(8,128)(2,1)S(1)} %get-tuple-element.33), channel_id=1, source_target_pairs={{0,8},{4,12},{8,0},{12,4},{1,9},{5,13},{9,1},{13,5},{2,10},{6,14},... | collective-permute-start | bytes 589832 | tf_op jit(solution)/shard_map/ppermute | solution.py:207
  138.5 14.3 %collective-permute-start.22 = (bf16[384,256]{1,0:T(8,128)(2,1)S(1)}, bf16[384,256]{1,0:T(8,128)(2,1)S(1)}, u32[]{:S(2)}, u32[]{:S(2)}) collective-permute-start(bf16[384,256]{1,0:T(8,128)(2,1)S(1)} %get-tuple-element.34), channel_id=1, source_target_pairs={{0,12},{4,8},{8,4},{12,0},{1,13},{5,9},{9,5},{13,1},{2,14},{6,10},... | collective-permute-start | bytes 589832 | tf_op jit(solution)/shard_map/ppermute | solution.py:207
  139.2 15.2 %collective-permute-start.30 = (f32[96,512]{1,0:T(8,128)S(1)}, f32[96,512]{1,0:T(8,128)S(1)}, u32[]{:S(2)}, u32[]{:S(2)}) collective-permute-start(f32[96,512]{1,0:T(8,128)S(1)} %get-tuple-element.40), channel_id=1, source_target_pairs={{0,1},{1,0},{2,3},{3,2},{4,5},{5,4},{6,7},{7,6},{8,9},{9,8},{10,11... | collective-permute-start | bytes 589832 | tf_op jit(solution)/shard_map/ppermute | solution.py:326
  140.2 14.1 %collective-permute-start.31 = (f32[96,512]{1,0:T(8,128)S(1)}, f32[96,512]{1,0:T(8,128)S(1)}, u32[]{:S(2)}, u32[]{:S(2)}) collective-permute-start(f32[96,512]{1,0:T(8,128)S(1)} %get-tuple-element.41), channel_id=1, source_target_pairs={{0,2},{1,3},{2,0},{3,1},{4,6},{5,7},{6,4},{7,5},{8,10},{9,11},{10,... | collective-permute-start | bytes 589832 | tf_op jit(solution)/shard_map/ppermute | solution.py:326
  (18 other events, 142.1 us)

commit v6 on v5

--- a/solution.py
+++ b/solution.py
@@ -12,6 +12,7 @@
 KP = 256
 BF = jnp.bfloat16
 F32 = jnp.float32
+LOG2_E = 1.4426950408889634
 VMEM_LIMIT = 24 * 1024 * 1024
 
 
@@ -117,15 +118,15 @@
     for h in range(width // DH):
         mask = (lane >= h * DH) & (lane < (h + 1) * DH)
         k_h = jnp.where(mask, kk, jnp.zeros_like(kk))
-        v_h = jnp.where(mask, vv, jnp.zeros_like(vv))
+        v_h = jnp.where(mask, vv * scale, jnp.zeros_like(vv))
         for k in range(n):
             block = slice(k * rows, (k + 1) * rows)
             scores = dot(k_h, q_all[block, :], 1, 1)
-            e = jnp.exp((scores - jnp.max(scores, axis=0, keepdims=True)) * scale)
+            e = jnp.exp2((scores - jnp.max(scores, axis=0, keepdims=True)) * (scale * LOG2_E))
             p = e * (1.0 / jnp.sum(e, axis=0, keepdims=True))
             dp = dot(v_h, g_all[block, :], 1, 1)
             delta = jnp.sum(p * dp, axis=0, keepdims=True)
-            ds = (p * (dp - delta) * scale).astype(BF)
+            ds = (p * (dp - delta)).astype(BF)
             p_all[:, block] = p.astype(BF)
             ds_all[:, block] = ds
             term = dot(ds, k_h, 0, 0)

time: 157 us -> 157 us (level)
  no operation moved by 1% of the time
where the time goes in v6:
time: 157 us; the launch traced here: 155 us
  waiting for transfers between devices  83.7 us (53%)
  starting transfers between devices  39.1 us (25%)
  Pallas kernels  27 us (17%)
  local copies, waits for them, and re-layouts  4.63 us (3%)
    ppermute x19, waiting for transfers between devices, to_line(): return lax.ppermute(x, 'ctx', swap(n, k))  74.4 us
    pallas_call x20, Pallas kernels, call(): pl.pallas_call(run, out_shape=outs, in_specs=[pl.BlockSpec(memory_space=p...  27 us
    ppermute x19, starting transfers between devices, to_line(): return lax.ppermute(x, 'ctx', swap(n, k))  19.2 us
    ppermute x6, starting transfers between devices, over_plane(): across.append(lax.ppermute(x, ('groups', 'dp'), perm))  5.43 us
    ppermute x1, waiting for transfers between devices, over_line(): lax.ppermute(x, 'ctx', [(1, 2), (2, 1)])  4.62 us
    ppermute x2, starting transfers between devices, over_cores(): return lax.ppermute(x, 'dp', swap(nd, 1))  4.58 us
    unnamed x15, local copies, waits for them, and re-layouts  3.71 us
    ppermute x3, waiting for transfers between devices, by_heads(): lax.ppermute(weight[a], 'dp', swap(nd, a))  3.64 us
  transfers between devices with their start and end apart: 36, of which 16 were waited for; matrix products, arithmetic and copies ran while one was open for 0% of the time, Pallas kernels for 16%

profile of v6, /device:TPU:9, one launch (start us, length us, event | category | flops | bytes accessed | tf_op | source)
XLA Modules:
  0.0 155.4 jit_solution(521754546057408389)
XLA Ops:
  1.6 2.5 %collective-permute-start.1 = (bf16[48,512]{1,0:T(8,128)(2,1)S(1)}, bf16[48,512]{1,0:T(8,128)(2,1)S(1)}, u32[]{:S(2)}, u32[]{:S(2)}) collective-permute-start(bf16[48,512]{1,0:T(8,128)(2,1)S(1)} %bitcast.31), channel_id=1, source_target_pairs={{0,8},{4,12},{8,0},{12,4},{1,9},{5,13},{9,1},{13,5},{2,10},{6,14},... | collective-permute-start | bytes 147464 | tf_op jit(solution)/shard_map/ppermute | solution.py:208
  6.1 3.3 %collective-permute-start.6 = (bf16[384,256]{1,0:T(8,128)(2,1)S(1)}, bf16[384,256]{1,0:T(8,128)(2,1)S(1)}, u32[]{:S(2)}, u32[]{:S(2)}) collective-permute-start(bf16[384,256]{1,0:T(8,128)(2,1)S(1)} %get-tuple-element.25), channel_id=1, source_target_pairs={{0,8},{4,12},{8,0},{12,4},{1,9},{5,13},{9,1},{13,5},{2,10},{6,14},... | collective-permute-start | bytes 589832 | tf_op jit(solution)/shard_map/ppermute | solution.py:208
  17.4 4.0 %collective-permute-done.6.refs_5_ = bf16[384,256]{1,0:T(8,128)(2,1)S(1)} collective-permute-done((bf16[384,256]{1,0:T(8,128)(2,1)S(1)}, bf16[384,256]{1,0:T(8,128)(2,1)S(1)}, u32[]{:S(2)}, u32[]{:S(2)}) %collective-permute-start.6) | collective-permute-done | bytes 196640 | tf_op jit(solution)/shard_map/ppermute | solution.py:208
  21.4 4.9 %collective-permute-done.7.refs_6_ = bf16[384,256]{1,0:T(8,128)(2,1)S(1)} collective-permute-done((bf16[384,256]{1,0:T(8,128)(2,1)S(1)}, bf16[384,256]{1,0:T(8,128)(2,1)S(1)}, u32[]{:S(2)}, u32[]{:S(2)}) %collective-permute-start.7) | collective-permute-done | bytes 196640 | tf_op jit(solution)/shard_map/ppermute | solution.py:208
  29.7 5.0 %collective-permute-done.9.refs_4_ = bf16[384,256]{1,0:T(8,128)(2,1)S(1)} collective-permute-done((bf16[384,256]{1,0:T(8,128)(2,1)S(1)}, bf16[384,256]{1,0:T(8,128)(2,1)S(1)}, u32[]{:S(2)}, u32[]{:S(2)}) %collective-permute-start.9) | collective-permute-done | bytes 196640 | tf_op jit(solution)/shard_map/ppermute | solution.py:208
  36.1 2.7 %collective-permute-start.11 = (bf16[512,256]{1,0:T(8,128)(2,1)S(1)}, bf16[512,256]{1,0:T(8,128)(2,1)S(1)}, u32[]{:S(2)}, u32[]{:S(2)}) collective-permute-start(bf16[512,256]{1,0:T(8,128)(2,1)S(1)} %compress.1.refs_1_), channel_id=1, source_target_pairs={{4,8},{8,4},{5,9},{9,5},{6,10},{10,6},{7,11},{11,7},{20,24},{24,20... | collective-permute-start | bytes 786440 | tf_op jit(solution)/shard_map/ppermute | solution.py:212
  40.1 2.5 %collective-permute-start.10 = (bf16[512,256]{1,0:T(8,128)(2,1)S(1)}, bf16[512,256]{1,0:T(8,128)(2,1)S(1)}, u32[]{:S(2)}, u32[]{:S(2)}) collective-permute-start(bf16[512,256]{1,0:T(8,128)(2,1)S(1)} %compress.1.refs_1_), channel_id=1, source_target_pairs={{0,4},{4,0},{8,12},{12,8},{1,5},{5,1},{9,13},{13,9},{2,6},{6,2},{1... | collective-permute-start | bytes 786440 | tf_op jit(solution)/shard_map/ppermute | solution.py:208
  43.5 4.6 %collective-permute-done.11.refs_1_ = bf16[512,256]{1,0:T(8,128)(2,1)S(1)} collective-permute-done((bf16[512,256]{1,0:T(8,128)(2,1)S(1)}, bf16[512,256]{1,0:T(8,128)(2,1)S(1)}, u32[]{:S(2)}, u32[]{:S(2)}) %collective-permute-start.11) | collective-permute-done | bytes 262176 | tf_op jit(solution)/shard_map/ppermute | solution.py:212
  50.2 2.8 %collective-permute-done.10.refs_2_ = bf16[512,256]{1,0:T(8,128)(2,1)S(1)} collective-permute-done((bf16[512,256]{1,0:T(8,128)(2,1)S(1)}, bf16[512,256]{1,0:T(8,128)(2,1)S(1)}, u32[]{:S(2)}, u32[]{:S(2)}) %collective-permute-start.10) | collective-permute-done | bytes 262176 | tf_op jit(solution)/shard_map/ppermute | solution.py:208
  53.6 2.0 %collective-permute-start.17 = (bf16[128,512]{1,0:T(8,128)(2,1)S(1)}, bf16[128,512]{1,0:T(8,128)(2,1)S(1)}, u32[]{:S(2)}, u32[]{:S(2)}) collective-permute-start(bf16[128,512]{1,0:T(8,128)(2,1)S(1)} %slice_weight.1.refs_1_), channel_id=1, source_target_pairs={{0,8},{4,12},{8,0},{12,4},{1,9},{5,13},{9,1},{13,5},{2,10},{6,14},... | collective-permute-start | bytes 393224 | tf_op jit(solution)/shard_map/ppermute | solution.py:208
  56.2 9.1 %collective-permute-done.16.refs_2_ = bf16[128,512]{1,0:T(8,128)(2,1)S(1)} collective-permute-done((bf16[128,512]{1,0:T(8,128)(2,1)S(1)}, bf16[128,512]{1,0:T(8,128)(2,1)S(1)}, u32[]{:S(2)}, u32[]{:S(2)}) %collective-permute-start.16) | collective-permute-done | bytes 131104 | tf_op jit(solution)/shard_map/ppermute | solution.py:208
  66.0 12.3 %collective-permute-done.17.refs_3_ = bf16[128,512]{1,0:T(8,128)(2,1)S(1)} collective-permute-done((bf16[128,512]{1,0:T(8,128)(2,1)S(1)}, bf16[128,512]{1,0:T(8,128)(2,1)S(1)}, u32[]{:S(2)}, u32[]{:S(2)}) %collective-permute-start.17) | collective-permute-done | bytes 131104 | tf_op jit(solution)/shard_map/ppermute | solution.py:208
  78.3 3.9 %collective-permute-done.18.refs_4_ = bf16[128,512]{1,0:T(8,128)(2,1)S(1)} collective-permute-done((bf16[128,512]{1,0:T(8,128)(2,1)S(1)}, bf16[128,512]{1,0:T(8,128)(2,1)S(1)}, u32[]{:S(2)}, u32[]{:S(2)}) %collective-permute-start.18) | collective-permute-done | bytes 131104 | tf_op jit(solution)/shard_map/ppermute | solution.py:208
  86.5 8.6 %collective-permute-done.19.refs_6_ = bf16[2,384,256]{2,1,0:T(8,128)(2,1)S(1)} collective-permute-done((bf16[2,384,256]{2,1,0:T(8,128)(2,1)S(1)}, bf16[2,384,256]{2,1,0:T(8,128)(2,1)S(1)}, u32[]{:S(2)}, u32[]{:S(2)}) %collective-permute-start.19) | collective-permute-done | bytes 393248 | tf_op jit(solution)/shard_map/ppermute | solution.py:208
  95.1 8.1 %attention.1 = (bf16[384,256]{1,0:T(8,128)(2,1)S(1)}, bf16[384,256]{1,0:T(8,128)(2,1)S(1)}, bf16[384,256]{1,0:T(8,128)(2,1)S(1)}, bf16[384,256]{1,0:T(8,128)(2,1)S(1)}, bf16[2,256,256]{2,1,0:T(8,128)(2,1)S(1)}) custom-call(s32[6]{0:T(128)S(1)} %stack.27.refs_0_, bf16[256,256]{1,0:T(8,128)(2,1)S(1)} %get-tuple-element.29.refs_1_, ...), custom_call_target="tpu_custom_call" | custom-call | flops 1 | bytes 1 | tf_op jit(solution)/shard_map/attention/pallas_call | solution.py:29
  103.3 2.0 %collective-permute-start.24 = (bf16[2,256,256]{2,1,0:T(8,128)(2,1)S(1)}, bf16[2,256,256]{2,1,0:T(8,128)(2,1)S(1)}, u32[]{:S(2)}, u32[]{:S(2)}) collective-permute-start(bf16[2,256,256]{2,1,0:T(8,128)(2,1)S(1)} %get-tuple-element.35.refs_2_.refs_1_), channel_id=1, source_target_pairs={{0,8},{4,12},{8,0},{12,4},{1,9},{5,13},{9,1},{13,5},{2,10},{6,14},... | collective-permute-start | bytes 786440 | tf_op jit(solution)/shard_map/ppermute | solution.py:208
  106.3 3.0 %collective-permute-done.23.refs_6_.refs_4_.refs_2_ = bf16[2,256,256]{2,1,0:T(8,128)(2,1)S(1)} collective-permute-done((bf16[2,256,256]{2,1,0:T(8,128)(2,1)S(1)}, bf16[2,256,256]{2,1,0:T(8,128)(2,1)S(1)}, u32[]{:S(2)}, u32[]{:S(2)}) %collective-permute-start.23) | collective-permute-done | bytes 262176 | tf_op jit(solution)/shard_map/ppermute | solution.py:208
  109.3 5.6 %collective-permute-done.24.refs_7_.refs_3_ = bf16[2,256,256]{2,1,0:T(8,128)(2,1)S(1)} collective-permute-done((bf16[2,256,256]{2,1,0:T(8,128)(2,1)S(1)}, bf16[2,256,256]{2,1,0:T(8,128)(2,1)S(1)}, u32[]{:S(2)}, u32[]{:S(2)}) %collective-permute-start.24) | collective-permute-done | bytes 262176 | tf_op jit(solution)/shard_map/ppermute | solution.py:208
  115.7 3.3 %collective-permute-start.29 = (bf16[4,4,128,512]{3,2,1,0:T(8,128)(2,1)S(1)}, bf16[4,4,128,512]{3,2,1,0:T(8,128)(2,1)S(1)}, u32[]{:S(2)}, u32[]{:S(2)}) collective-permute-start(bf16[4,4,128,512]{3,2,1,0:T(8,128)(2,1)S(1)} %join_weights.1.refs_1_), channel_id=1, source_target_pairs={{0,1},{1,0},{2,3},{3,2},{4,5},{5,4},{6,7},{7,6},{8,9},{9,8},{10,11... | collective-permute-start | bytes 6291464 | tf_op jit(solution)/shard_map/ppermute | solution.py:227
  122.8 1.9 %collective-permute-start.20 = (bf16[384,256]{1,0:T(8,128)(2,1)S(1)}, bf16[384,256]{1,0:T(8,128)(2,1)S(1)}, u32[]{:S(2)}, u32[]{:S(2)}) collective-permute-start(bf16[384,256]{1,0:T(8,128)(2,1)S(1)} %get-tuple-element.32), channel_id=1, source_target_pairs={{0,4},{4,0},{8,12},{12,8},{1,5},{5,1},{9,13},{13,9},{2,6},{6,2},{1... | collective-permute-start | bytes 589832 | tf_op jit(solution)/shard_map/ppermute | solution.py:208
  125.8 9.0 %collective-permute-done.25.refs_4_ = bf16[2,256,256]{2,1,0:T(8,128)(2,1)S(1)} collective-permute-done((bf16[2,256,256]{2,1,0:T(8,128)(2,1)S(1)}, bf16[2,256,256]{2,1,0:T(8,128)(2,1)S(1)}, u32[]{:S(2)}, u32[]{:S(2)}) %collective-permute-start.25) | collective-permute-done | bytes 262176 | tf_op jit(solution)/shard_map/ppermute | solution.py:208
  134.7 3.5 %tail.1 = (f32[96,512]{1,0:T(8,128)S(1)}, f32[96,512]{1,0:T(8,128)S(1)}, f32[96,512]{1,0:T(8,128)S(1)}, f32[96,512]{1,0:T(8,128)S(1)}, bf16[384,1024]{1,0:T(8,128)(2,1)}) custom-call(s32[6]{0:T(128)S(1)} %stack.27.refs_0_, bf16[2,256,256]{2,1,0:T(8,128)(2,1)S(1)} %get-tuple-element.35.refs_2_.refs_1_, ...), custom_call_target="tpu_custom_call" | custom-call | flops 1 | bytes 1 | tf_op jit(solution)/shard_map/tail/pallas_call | solution.py:29
  141.2 3.6 %collective-permute-done.35.refs_4_ = f32[256,512]{1,0:T(8,128)S(1)} collective-permute-done((f32[256,512]{1,0:T(8,128)S(1)}, f32[256,512]{1,0:T(8,128)S(1)}, u32[]{:S(2)}, u32[]{:S(2)}) %collective-permute-start.35) | collective-permute-done | bytes 524320 | tf_op jit(solution)/shard_map/ppermute | solution.py:298
  146.9 5.7 %collective-permute-done.22.refs_4_ = bf16[384,256]{1,0:T(8,128)(2,1)S(1)} collective-permute-done((bf16[384,256]{1,0:T(8,128)(2,1)S(1)}, bf16[384,256]{1,0:T(8,128)(2,1)S(1)}, u32[]{:S(2)}, u32[]{:S(2)}) %collective-permute-start.22) | collective-permute-done | bytes 196640 | tf_op jit(solution)/shard_map/ppermute | solution.py:208
  (85 shorter events, 40.5 us)
Async XLA Ops:
  6.1 15.3 %collective-permute-start.6 = (bf16[384,256]{1,0:T(8,128)(2,1)S(1)}, bf16[384,256]{1,0:T(8,128)(2,1)S(1)}, u32[]{:S(2)}, u32[]{:S(2)}) collective-permute-start(bf16[384,256]{1,0:T(8,128)(2,1)S(1)} %get-tuple-element.25), channel_id=1, source_target_pairs={{0,8},{4,12},{8,0},{12,4},{1,9},{5,13},{9,1},{13,5},{2,10},{6,14},... | collective-permute-start | bytes 589832 | tf_op jit(solution)/shard_map/ppermute | solution.py:208
  9.4 16.9 %collective-permute-start.7 = (bf16[384,256]{1,0:T(8,128)(2,1)S(1)}, bf16[384,256]{1,0:T(8,128)(2,1)S(1)}, u32[]{:S(2)}, u32[]{:S(2)}) collective-permute-start(bf16[384,256]{1,0:T(8,128)(2,1)S(1)} %get-tuple-element.26), channel_id=1, source_target_pairs={{0,12},{4,8},{8,4},{12,0},{1,13},{5,9},{9,5},{13,1},{2,14},{6,10},... | collective-permute-start | bytes 589832 | tf_op jit(solution)/shard_map/ppermute | solution.py:208
  9.9 16.3 %collective-permute-start.3 = (bf16[4,48,512]{2,1,0:T(8,128)(2,1)S(1)}, bf16[4,48,512]{2,1,0:T(8,128)(2,1)S(1)}, u32[]{:S(2)}, u32[]{:S(2)}) collective-permute-start(bf16[4,48,512]{2,1,0:T(8,128)(2,1)S(1)} %join_pieces.1.refs_3_.refs_1_), channel_id=1, source_target_pairs={{0,2},{1,3},{2,0},{3,1},{16,18},{17,19},{18,16},{19,17},{4,6},{5,7... | collective-permute-start | bytes 589832 | tf_op jit(solution)/shard_map/ppermute | solution.py:223
  11.2 15.1 %collective-permute-start.4 = (bf16[4,48,512]{2,1,0:T(8,128)(2,1)S(1)}, bf16[4,48,512]{2,1,0:T(8,128)(2,1)S(1)}, u32[]{:S(2)}, u32[]{:S(2)}) collective-permute-start(bf16[4,48,512]{2,1,0:T(8,128)(2,1)S(1)} %join_pieces.1.refs_3_.refs_1_), channel_id=1, source_target_pairs={{0,16},{1,17},{2,18},{3,19},{16,0},{17,1},{18,2},{19,3},{4,20},{5,... | collective-permute-start | bytes 589832 | tf_op jit(solution)/shard_map/ppermute | solution.py:223
  12.5 13.8 %collective-permute-start.5 = (bf16[4,48,512]{2,1,0:T(8,128)(2,1)S(1)}, bf16[4,48,512]{2,1,0:T(8,128)(2,1)S(1)}, u32[]{:S(2)}, u32[]{:S(2)}) collective-permute-start(bf16[4,48,512]{2,1,0:T(8,128)(2,1)S(1)} %join_pieces.1.refs_3_.refs_1_), channel_id=1, source_target_pairs={{0,18},{1,19},{2,16},{3,17},{16,2},{17,3},{18,0},{19,1},{4,22},{5,... | collective-permute-start | bytes 589832 | tf_op jit(solution)/shard_map/ppermute | solution.py:223
  28.2 15.3 %collective-permute-start.13 = (bf16[2,384,256]{2,1,0:T(8,128)(2,1)S(1)}, bf16[2,384,256]{2,1,0:T(8,128)(2,1)S(1)}, u32[]{:S(2)}, u32[]{:S(2)}) collective-permute-start(bf16[2,384,256]{2,1,0:T(8,128)(2,1)S(1)} %pack_queries.5.refs_8_.refs_7_), channel_id=1, source_target_pairs={{0,4},{4,0},{8,12},{12,8},{1,5},{5,1},{9,13},{13,9},{2,6},{6,2},{1... | collective-permute-start | bytes 1179656 | tf_op jit(solution)/shard_map/ppermute | solution.py:208
  40.1 12.9 %collective-permute-start.10 = (bf16[512,256]{1,0:T(8,128)(2,1)S(1)}, bf16[512,256]{1,0:T(8,128)(2,1)S(1)}, u32[]{:S(2)}, u32[]{:S(2)}) collective-permute-start(bf16[512,256]{1,0:T(8,128)(2,1)S(1)} %compress.1.refs_1_), channel_id=1, source_target_pairs={{0,4},{4,0},{8,12},{12,8},{1,5},{5,1},{9,13},{13,9},{2,6},{6,2},{1... | collective-permute-start | bytes 786440 | tf_op jit(solution)/shard_map/ppermute | solution.py:208
  42.6 42.7 %collective-permute-start.15 = (bf16[2,384,256]{2,1,0:T(8,128)(2,1)S(1)}, bf16[2,384,256]{2,1,0:T(8,128)(2,1)S(1)}, u32[]{:S(2)}, u32[]{:S(2)}) collective-permute-start(bf16[2,384,256]{2,1,0:T(8,128)(2,1)S(1)} %pack_queries.6.refs_9_.refs_8_), channel_id=1, source_target_pairs={{0,8},{4,12},{8,0},{12,4},{1,9},{5,13},{9,1},{13,5},{2,10},{6,14},... | collective-permute-start | bytes 1179656 | tf_op jit(solution)/shard_map/ppermute | solution.py:208
  48.7 36.8 %collective-permute-start.14 = (bf16[2,512,256]{2,1,0:T(8,128)(2,1)S(1)}, bf16[2,512,256]{2,1,0:T(8,128)(2,1)S(1)}, u32[]{:S(2)}, u32[]{:S(2)}) collective-permute-start(bf16[2,512,256]{2,1,0:T(8,128)(2,1)S(1)} %join_near.1.refs_3_), channel_id=1, source_target_pairs={{4,0},{8,12},{5,1},{9,13},{6,2},{10,14},{7,3},{11,15},{20,16},{24,... | collective-permute-start | bytes 1572872 | tf_op jit(solution)/shard_map/ppermute | solution.py:214
  53.6 24.7 %collective-permute-start.17 = (bf16[128,512]{1,0:T(8,128)(2,1)S(1)}, bf16[128,512]{1,0:T(8,128)(2,1)S(1)}, u32[]{:S(2)}, u32[]{:S(2)}) collective-permute-start(bf16[128,512]{1,0:T(8,128)(2,1)S(1)} %slice_weight.1.refs_1_), channel_id=1, source_target_pairs={{0,8},{4,12},{8,0},{12,4},{1,9},{5,13},{9,1},{13,5},{2,10},{6,14},... | collective-permute-start | bytes 393224 | tf_op jit(solution)/shard_map/ppermute | solution.py:208
  55.6 26.5 %collective-permute-start.18 = (bf16[128,512]{1,0:T(8,128)(2,1)S(1)}, bf16[128,512]{1,0:T(8,128)(2,1)S(1)}, u32[]{:S(2)}, u32[]{:S(2)}) collective-permute-start(bf16[128,512]{1,0:T(8,128)(2,1)S(1)} %slice_weight.1.refs_1_), channel_id=1, source_target_pairs={{0,12},{4,8},{8,4},{12,0},{1,13},{5,9},{9,5},{13,1},{2,14},{6,10},... | collective-permute-start | bytes 393224 | tf_op jit(solution)/shard_map/ppermute | solution.py:208
  65.3 29.8 %collective-permute-start.19 = (bf16[2,384,256]{2,1,0:T(8,128)(2,1)S(1)}, bf16[2,384,256]{2,1,0:T(8,128)(2,1)S(1)}, u32[]{:S(2)}, u32[]{:S(2)}) collective-permute-start(bf16[2,384,256]{2,1,0:T(8,128)(2,1)S(1)} %pack_queries.7.refs_10_.refs_9_), channel_id=1, source_target_pairs={{0,12},{4,8},{8,4},{12,0},{1,13},{5,9},{9,5},{13,1},{2,14},{6,10},... | collective-permute-start | bytes 1179656 | tf_op jit(solution)/shard_map/ppermute | solution.py:208
  82.7 23.5 %collective-permute-start.26 = (bf16[4,128,512]{2,1,0:T(8,128)(2,1)S(1)}, bf16[4,128,512]{2,1,0:T(8,128)(2,1)S(1)}, u32[]{:S(2)}, u32[]{:S(2)}) collective-permute-start(bf16[4,128,512]{2,1,0:T(8,128)(2,1)S(1)} %join_weight.1.refs_8_.refs_1_), channel_id=1, source_target_pairs={{0,2},{1,3},{2,0},{3,1},{16,18},{17,19},{18,16},{19,17},{4,6},{5,7... | collective-permute-start | bytes 1572872 | tf_op jit(solution)/shard_map/ppermute | solution.py:223
  84.0 22.3 %collective-permute-start.27 = (bf16[4,128,512]{2,1,0:T(8,128)(2,1)S(1)}, bf16[4,128,512]{2,1,0:T(8,128)(2,1)S(1)}, u32[]{:S(2)}, u32[]{:S(2)}) collective-permute-start(bf16[4,128,512]{2,1,0:T(8,128)(2,1)S(1)} %join_weight.1.refs_8_.refs_1_), channel_id=1, source_target_pairs={{0,16},{1,17},{2,18},{3,19},{16,0},{17,1},{18,2},{19,3},{4,20},{5,... | collective-permute-start | bytes 1572872 | tf_op jit(solution)/shard_map/ppermute | solution.py:223
  85.3 21.0 %collective-permute-start.28 = (bf16[4,128,512]{2,1,0:T(8,128)(2,1)S(1)}, bf16[4,128,512]{2,1,0:T(8,128)(2,1)S(1)}, u32[]{:S(2)}, u32[]{:S(2)}) collective-permute-start(bf16[4,128,512]{2,1,0:T(8,128)(2,1)S(1)} %join_weight.1.refs_8_.refs_1_), channel_id=1, source_target_pairs={{0,18},{1,19},{2,16},{3,17},{16,2},{17,3},{18,0},{19,1},{4,22},{5,... | collective-permute-start | bytes 1572872 | tf_op jit(solution)/shard_map/ppermute | solution.py:223
  119.0 19.9 %collective-permute-start.33 = (f32[256,512]{1,0:T(8,128)S(1)}, f32[256,512]{1,0:T(8,128)S(1)}, u32[]{:S(2)}, u32[]{:S(2)}) collective-permute-start(f32[256,512]{1,0:T(8,128)S(1)} %get-tuple-element.43), channel_id=1, source_target_pairs={{0,1},{1,0},{2,3},{3,2},{4,5},{5,4},{6,7},{7,6},{8,9},{9,8},{10,11... | collective-permute-start | bytes 1572872 | tf_op jit(solution)/shard_map/ppermute | solution.py:298
  119.1 20.9 %collective-permute-start.34 = (f32[256,512]{1,0:T(8,128)S(1)}, f32[256,512]{1,0:T(8,128)S(1)}, u32[]{:S(2)}, u32[]{:S(2)}) collective-permute-start(f32[256,512]{1,0:T(8,128)S(1)} %get-tuple-element.44), channel_id=1, source_target_pairs={{0,2},{1,3},{2,0},{3,1},{4,6},{5,7},{6,4},{7,5},{8,10},{9,11},{10,... | collective-permute-start | bytes 1572872 | tf_op jit(solution)/shard_map/ppermute | solution.py:298
  120.3 24.5 %collective-permute-start.35 = (f32[256,512]{1,0:T(8,128)S(1)}, f32[256,512]{1,0:T(8,128)S(1)}, u32[]{:S(2)}, u32[]{:S(2)}) collective-permute-start(f32[256,512]{1,0:T(8,128)S(1)} %get-tuple-element.45), channel_id=1, source_target_pairs={{0,3},{1,2},{2,1},{3,0},{4,7},{5,6},{6,5},{7,4},{8,11},{9,10},{10,... | collective-permute-start | bytes 1572872 | tf_op jit(solution)/shard_map/ppermute | solution.py:298
  121.1 13.6 %collective-permute-start.25 = (bf16[2,256,256]{2,1,0:T(8,128)(2,1)S(1)}, bf16[2,256,256]{2,1,0:T(8,128)(2,1)S(1)}, u32[]{:S(2)}, u32[]{:S(2)}) collective-permute-start(bf16[2,256,256]{2,1,0:T(8,128)(2,1)S(1)} %get-tuple-element.35.refs_2_.refs_1_), channel_id=1, source_target_pairs={{0,12},{4,8},{8,4},{12,0},{1,13},{5,9},{9,5},{13,1},{2,14},{6,10},... | collective-permute-start | bytes 786440 | tf_op jit(solution)/shard_map/ppermute | solution.py:208
  122.8 15.5 %collective-permute-start.20 = (bf16[384,256]{1,0:T(8,128)(2,1)S(1)}, bf16[384,256]{1,0:T(8,128)(2,1)S(1)}, u32[]{:S(2)}, u32[]{:S(2)}) collective-permute-start(bf16[384,256]{1,0:T(8,128)(2,1)S(1)} %get-tuple-element.32), channel_id=1, source_target_pairs={{0,4},{4,0},{8,12},{12,8},{1,5},{5,1},{9,13},{13,9},{2,6},{6,2},{1... | collective-permute-start | bytes 589832 | tf_op jit(solution)/shard_map/ppermute | solution.py:208
  134.7 12.1 %collective-permute-start.21 = (bf16[384,256]{1,0:T(8,128)(2,1)S(1)}, bf16[384,256]{1,0:T(8,128)(2,1)S(1)}, u32[]{:S(2)}, u32[]{:S(2)}) collective-permute-start(bf16[384,256]{1,0:T(8,128)(2,1)S(1)} %get-tuple-element.33), channel_id=1, source_target_pairs={{0,8},{4,12},{8,0},{12,4},{1,9},{5,13},{9,1},{13,5},{2,10},{6,14},... | collective-permute-start | bytes 589832 | tf_op jit(solution)/shard_map/ppermute | solution.py:208
  138.3 14.3 %collective-permute-start.22 = (bf16[384,256]{1,0:T(8,128)(2,1)S(1)}, bf16[384,256]{1,0:T(8,128)(2,1)S(1)}, u32[]{:S(2)}, u32[]{:S(2)}) collective-permute-start(bf16[384,256]{1,0:T(8,128)(2,1)S(1)} %get-tuple-element.34), channel_id=1, source_target_pairs={{0,12},{4,8},{8,4},{12,0},{1,13},{5,9},{9,5},{13,1},{2,14},{6,10},... | collective-permute-start | bytes 589832 | tf_op jit(solution)/shard_map/ppermute | solution.py:208
  138.9 15.2 %collective-permute-start.30 = (f32[96,512]{1,0:T(8,128)S(1)}, f32[96,512]{1,0:T(8,128)S(1)}, u32[]{:S(2)}, u32[]{:S(2)}) collective-permute-start(f32[96,512]{1,0:T(8,128)S(1)} %get-tuple-element.40), channel_id=1, source_target_pairs={{0,1},{1,0},{2,3},{3,2},{4,5},{5,4},{6,7},{7,6},{8,9},{9,8},{10,11... | collective-permute-start | bytes 589832 | tf_op jit(solution)/shard_map/ppermute | solution.py:327
  139.9 14.1 %collective-permute-start.31 = (f32[96,512]{1,0:T(8,128)S(1)}, f32[96,512]{1,0:T(8,128)S(1)}, u32[]{:S(2)}, u32[]{:S(2)}) collective-permute-start(f32[96,512]{1,0:T(8,128)S(1)} %get-tuple-element.41), channel_id=1, source_target_pairs={{0,2},{1,3},{2,0},{3,1},{4,6},{5,7},{6,4},{7,5},{8,10},{9,11},{10,... | collective-permute-start | bytes 589832 | tf_op jit(solution)/shard_map/ppermute | solution.py:327
  (18 other events, 142.1 us)
